TPU v7x, 32 devices: a whole 2x2x4 slice. The times are simulated.
32 devices in a mesh: group: 2 (over y), gene: 4 (over z), lat: 2 (over x), sub: 2 (over core).
Axes of the slice: x: 2, y: 2, z: 4, core: 2. Of those that a mesh axis runs over, the one named last changes fastest.
Arguments:
- cell_index: int32 [2048], P(('group', 'lat', 'sub')), parts along dimension 0, may hold values from 0 to 511
- coords_table: float32 [4, 2048], P('group', ('lat', 'sub')), parts along dimension 0, may hold values from 0 to 1
- expr_table: bfloat16 [4096, 16384], P(('group', 'lat', 'sub'), 'gene'), parts along dimension 0, may hold values from -6 to 6
- inducing: float32 [4, 64, 8192], P('group', 'lat', 'sub'), parts along dimension 0, may hold values from 0 to 1
- ind_weights: float32 [128, 8192], P(('group', 'lat'), 'sub'), parts along dimension 0, may hold values from -0.6 to 0.6
- lengthscale: float32 [128], P(('group', 'lat')), parts along dimension 0, may hold values from 0.02 to 0.1
- variance: float32 [128], P(('group', 'lat')), parts along dimension 0, may hold values from 0.5 to 2
- mixing: bfloat16 [128, 16384], P('group', 'gene'), parts along dimension 0, may hold values from -0.75 to 0.75
- noise_prec: float32 [32768], P(('group', 'gene')), parts along dimension 0, may hold values from 0.5 to 4
Outputs:
- grad_mixing: float32 [128, 16384], P('group', 'gene'), parts along dimension 0
- grad_inducing: float32 [128, 8192], P(('group', 'lat'), 'sub'), parts along dimension 0
There are 2 independent parts, one for each index of `group`. A program takes and returns all parts, laid end to end along the dimension named above; each array names one. Nothing has to cross between parts.
Inputs may be any that keep to these rules, and one draw needn't show every extreme that they name: Entry n indexes a row inside block n // 256 of the tables: cell n is table row (n // 256) * 512 + cell_index[n]; cells may repeat.
All inputs are finite; a program needn't handle non-finite values.
Results may differ from a plain program's by a relative error of at most 0.00075.
Values may be sent and summed in bfloat16 or wider, within the bound.
No kernel may reach another device: no remote copies, remote signals or barrier semaphores. Data moves between devices by JAX's collectives and lax.ppermute only.
A program may use at most 64 MiB of HBM per device.

v0:
```python
import math

import jax
import jax.numpy as jnp
from jax import lax
from jax.sharding import PartitionSpec as P


def kernel_tile(cell_xy, points, length, height):
    delta_x = cell_xy[0][:, None] - points[0][None, :]
    delta_y = cell_xy[1][:, None] - points[1][None, :]
    return height * jnp.exp(-(delta_x * delta_x + delta_y * delta_y) * (0.5 / (length * length)))


def on_device(
    cell_index,
    coords_table,
    expr_table,
    inducing,
    ind_weights,
    lengthscale,
    variance,
    mixing,
    noise_prec,
):
    gene_count = lax.axis_size("gene")
    lat_count = lax.axis_size("lat")
    sub_count = lax.axis_size("sub")
    bat_rows = cell_index.shape[0]
    per_block = bat_rows // gene_count
    block_count = lat_count * sub_count
    gene_place = lax.axis_index("gene")
    local_xy = jnp.take(coords_table, cell_index, axis=1)
    every_xy = lax.all_gather(local_xy, ("lat", "sub"), axis=1, tiled=True)
    every_xy = every_xy.reshape(2, block_count, gene_count, per_block)
    kernel_xy = lax.dynamic_slice_in_dim(every_xy, gene_place, 1, 2).reshape(
        2, block_count * per_block
    )
    moved = jnp.moveaxis(inducing, 1, 0)

    def forward(packed):
        points, weights, length, height = packed
        return jnp.dot(
            kernel_tile(kernel_xy, points, length, height), weights, precision=lax.Precision.HIGHEST
        )

    local_latent = lax.map(forward, (moved, ind_weights, lengthscale, variance))
    swapped = lax.all_to_all(local_latent, "lat", split_axis=1, concat_axis=0, tiled=True)
    summed = lax.psum_scatter(swapped, "sub", scatter_dimension=1, tiled=True).astype(jnp.bfloat16)
    latent = lax.all_gather(summed, "gene", axis=1, tiled=True)
    observed = jnp.take(expr_table, cell_index, axis=0)
    predicted = lax.dot_general(
        latent, mixing, (((0,), (0,)), ((), ())), preferred_element_type=jnp.float32
    )
    weighted = (noise_prec[None, :] * (observed.astype(jnp.float32) - predicted)).astype(
        jnp.bfloat16
    )
    grad_scale = -1.0 / math.sqrt(bat_rows * block_count)
    mixing_term = grad_scale * jnp.dot(latent, weighted, preferred_element_type=jnp.float32)
    grad_mixing = lax.psum(mixing_term, ("lat", "sub"))
    cell_term = grad_scale * lax.dot_general(
        mixing, weighted, (((1,), (1,)), ((), ())), preferred_element_type=jnp.float32
    )
    shared = lax.psum_scatter(cell_term, "gene", scatter_dimension=1, tiled=True)
    paired = lax.all_gather(shared, "sub", axis=1, tiled=True)
    latent_grad = lax.all_to_all(paired, "lat", split_axis=0, concat_axis=1, tiled=True)

    def backward(packed):
        points, gradient, length, height = packed
        return jnp.dot(
            gradient,
            kernel_tile(kernel_xy, points, length, height),
            precision=lax.Precision.HIGHEST,
        )

    partial_inducing = lax.map(backward, (moved, latent_grad, lengthscale, variance))
    grad_inducing = lax.psum(partial_inducing, "gene")
    return (grad_mixing, grad_inducing)


def solution(mesh):
    in_specs = (
        P(("group", "lat", "sub")),
        P("group", ("lat", "sub")),
        P(("group", "lat", "sub"), "gene"),
        P("group", "lat", "sub"),
        P(("group", "lat"), "sub"),
        P(("group", "lat")),
        P(("group", "lat")),
        P("group", "gene"),
        P(("group", "gene")),
    )
    out_specs = (P("group", "gene"), P(("group", "lat"), "sub"))
    return jax.shard_map(
        on_device, mesh=mesh, in_specs=in_specs, out_specs=out_specs, check_vma=False
    )
```

profile of v0, /device:TPU:0, one launch (start us, length us, event | category | flops | bytes accessed | tf_op | source)
XLA Modules:
  0.0 742.9 jit_solution(11795437279426381336)
XLA Ops:
  10.3 8.6 %all_gather.9 = f32[2,1024]{0,1:T(8,128)S(1)} all-gather(f32[2,256]{0,1:T(8,128)S(1)} %select_bitcast_fusion), channel_id=1, replica_groups=mesh['group'=2,'gene'=4,'lat'=2,'sub'=2] {'lat','sub'}, dimensions={1}, use_global_device_ids=true | all-gather | bytes 10240 | tf_op jit(solution)/shard_map/all_gather | solution.py:34
  21.1 317.4 %while.20 = (s32[]{:T(128)}, f32[32,256]{1,0:T(8,128)S(1)}, f32[32]{0:T(128)}, f32[2,256]{1,0:T(2,128)S(1)}, f32[32,2,4096]{2,1,0:T(2,128)S(1)}, /*index=5*/f32[...) while((s32[]{:T(128)}, f32[32,256]{1,0:T(8,128)S(1)}, f32[32]{0:T(128)}, ...), condition=%wide.region_1.2_spmd, body=%wide.region_0.1_spmd.sunk | while | flops 20971524 | bytes 125121 | solution.py:47
  25.0 6.0 fusion.62
  34.9 6.0 fusion.62
  44.8 6.0 fusion.62
  54.7 6.0 fusion.62
  64.7 6.0 fusion.62
  74.6 6.0 fusion.62
  84.5 6.0 fusion.62
  94.4 6.0 fusion.62
  104.3 6.0 fusion.62
  114.2 6.0 fusion.62
  124.2 6.0 fusion.62
  134.1 6.0 fusion.62
  144.0 6.0 fusion.62
  153.9 6.0 fusion.62
  163.8 6.0 fusion.62
  183.7 6.0 fusion.62
  203.5 6.0 fusion.62
  213.4 6.0 fusion.62
  233.3 6.0 fusion.62
  243.2 6.0 fusion.62
  263.0 6.0 fusion.62
  292.8 6.0 fusion.62
  312.6 6.0 fusion.62
  322.5 6.0 fusion.62
  338.5 6.3 all_to_all.38
  345.6 7.9 %gather_fusion.1 = bf16[256,4096]{1,0:T(8,128)(2,1)} fusion(bf16[512,4096]{1,0:T(8,128)(2,1)} %param.15, s32[1024]{0:T(1024)S(1)} %pad_clamp_fusion), kind=kCustom, calls=%fused_computation.1 | custom fusion | bytes 4195328 | tf_op jit(solution)/shard_map/jit(_take)/gather | solution.py:51
  354.5 13.4 %all_gather.10 = bf16[64,256]{0,1:T(8,128)(2,1)S(1)} all-gather(bf16[64,64]{0,1:T(8,128)(2,1)S(1)} %copy.42), channel_id=1, replica_groups=mesh['group'=2,'gene'=4,'lat'=2,'sub'=2] {'gene'}, dimensions={1}, use_global_device_ids=true | all-gather | bytes 40960 | tf_op jit(solution)/shard_map/all_gather | solution.py:50
  371.9 20.1 %reduce-scatter.9.cloned.1.call-done = f32[64,64]{1,0:T(8,128)} async-done(((f32[256,64]{1,0:T(8,128)}), f32[64,64]{1,0:T(8,128)}) %reduce-scatter.9.cloned.1.call-update) | async-done | bytes 16400
  402.0 294.5 %while.21 = (s32[]{:T(128)}, f32[32,4096]{1,0:T(8,128)}, f32[32,256]{1,0:T(8,128)S(1)}, f32[32]{0:T(128)S(1)}, f32[2,256]{1,0:T(2,128)S(1)}, /*index=5*/f32[32,2...) while((s32[]{:T(128)}, f32[32,4096]{1,0:T(8,128)}, ...), condition=%wide.region_6.7_spmd, body=%wide.region_5.6_spmd.sunk | while | flops 20971524 | bytes 154825 | solution.py:76
  696.5 35.7 %all-reduce.5.cloned.1.call-done = f32[32,4096]{1,0:T(8,128)} async-done(((f32[32,4096]{1,0:T(8,128)}), f32[32,4096]{1,0:T(8,128)}) %all-reduce.5.cloned.1.call-update) | async-done | bytes 524304 | tf_op jit(solution)/shard_map/psum | solution.py:77
  (406 shorter events, 403.3 us)
Async XLA Ops:
  7.2 360.8 %copy-start = (bf16[64,4096]{1,0:T(8,128)(2,1)S(1)}, bf16[64,4096]{1,0:T(8,128)(2,1)}, u32[]{:S(2)}) copy-start(bf16[64,4096]{1,0:T(8,128)(2,1)} %param.20) | copy-start | bytes 1572868
  7.2 346.4 %reduce-scatter.7.cloned.1.call-start = ((), (), s32[]{:S(2)}) async-start(), calls=%async_computation.6 | async-start | bytes 98304
  338.5 15.1 %copy-start.1 = (f32[32,2,4096]{2,1,0:T(2,128)}, f32[32,2,4096]{2,1,0:T(2,128)S(1)}, u32[]{:S(2)}) copy-start(f32[32,2,4096]{2,1,0:T(2,128)S(1)} %get-tuple-element.290) | copy-start | bytes 3145732
  345.6 22.4 %copy-start.2 = (f32[4096]{0:T(1024)S(1)}, f32[4096]{0:T(1024)}, u32[]{:S(2)}) copy-start(f32[4096]{0:T(1024)} %param.21) | copy-start | bytes 49156
  345.6 46.5 %reduce-scatter.9.cloned.1.call-start = ((), (), s32[]{:S(2)}) async-start(), calls=%async_computation.7 | async-start | bytes 163840
  370.3 31.7 %copy-start.3 = (f32[32]{0:T(128)S(1)}, f32[32]{0:T(128)}, u32[]{:S(2)}) copy-start(f32[32]{0:T(128)} %get-tuple-element.303) | copy-start | bytes 388
  370.4 31.7 %copy-start.4 = (f32[32]{0:T(128)S(1)}, f32[32]{0:T(128)}, u32[]{:S(2)}) copy-start(f32[32]{0:T(128)} %get-tuple-element.304) | copy-start | bytes 388
  394.8 7.2 all-to-all-start.1
  398.1 298.4 %all-reduce.3.cloned.1.call-start = ((), (), s32[]{:S(2)}) async-start(), calls=%async_computation.4 | async-start | bytes 2097152 | tf_op jit(solution)/shard_map/psum | solution.py:60
  399.8 332.4 %all-reduce.5.cloned.1.call-start = ((), (), s32[]{:S(2)}) async-start(), calls=%async_computation.5 | async-start | bytes 1048576 | tf_op jit(solution)/shard_map/psum | solution.py:77
Sparse Core Ops, SparseCore 0:
  345.7 7.7 reduce-scatter.6
  372.0 19.9 reduce-scatter.8
  402.0 34.7 all-reduce.2
  696.6 35.5 all-reduce.4
where the time goes:
time: 749 us; the launch traced here: 743 us
  matrix products  325 us (43%)
  local copies, waits for them, and re-layouts  220 us (29%)
  loops' own time  90 us (12%)
  waiting for transfers between devices  58.1 us (8%)
  blocking collectives  30.4 us (4%)
  between operations  13.9 us (2%)
    dot_general x32, matrix products, forward(): jnp.dot(kernel_tile(kernel_xy, points, length, height), weights, precisio...  191 us
    dot_general x32, matrix products, backward(): jnp.dot(gradient, kernel_tile(kernel_xy, points, length, height), precisi...  129 us
    dynamic_slice x128, local copies, waits for them, and re-layouts, on_device(): local_latent = lax.map(forward, (moved, ind_weights, lengthscale, variance))  119 us
    dynamic_update_slice x32, local copies, waits for them, and re-layouts, on_device(): lax.map(backward, (moved, latent_grad, lengthscale, variance))  51.7 us
    another operation x1, loops' own time, on_device(): lax.map(backward, (moved, latent_grad, lengthscale, variance))  46 us
    another operation x1, loops' own time, on_device(): local_latent = lax.map(forward, (moved, ind_weights, lengthscale, variance))  44 us
    psum x1, waiting for transfers between devices, on_device(): grad_inducing = lax.psum(partial_inducing, 'gene')  35.7 us
    slice x128, local copies, waits for them, and re-layouts, kernel_tile(): delta_x = cell_xy[0][:, None] - points[0][None, :]  29.4 us
  transfers between devices with their start and end apart: 5, of which 3 were waited for; matrix products, arithmetic and copies ran while one was open for 35% of the time, Pallas kernels for 0%

commit v1 on v0

v1 whole, which is shorter than its diff:
```python
import functools
import math

import jax
import jax.numpy as jnp
from jax import lax
from jax.experimental import pallas as pl
from jax.experimental.pallas import tpu as pltpu
from jax.sharding import PartitionSpec as P

LOG2E = math.log2(math.e)

def row_of(shape):
    return lax.broadcasted_iota(jnp.int32, shape, 0)

def parts(u, w, a):
    L = u.shape[1]
    U = (u - 0.5) * a
    W = (w - 0.5) * a
    big = 1.5 * 2.0**20
    U1 = (U + big) - big
    W1 = (W + big) - big
    rU = U - U1
    rW = W - W1
    hi = U1 * U1 + W1 * W1
    lo = rU * (U1 + U) + rW * (W1 + W)
    r = row_of((8, L)) % 4
    T = jnp.where(r == 0, U, jnp.where(r == 1, W, jnp.where(r == 2, hi, lo)))
    rc = row_of((8, 1)) % 4
    magic = jnp.where(rc <= 1, 1.5 * 2.0**20, jnp.where(rc == 2, 1.5 * 2.0**26, 1.5 * 2.0**18)).astype(jnp.float32)
    T1 = ((T + magic) - magic).astype(jnp.bfloat16).astype(jnp.float32)
    R = T - T1
    T2 = R.astype(jnp.bfloat16).astype(jnp.float32)
    T3 = R - T2
    return T1, T2, T3

def point_rows(u, w, a):
    T1, T2, T3 = parts(u, w, a)
    one = jnp.ones_like(T1)
    return jnp.concatenate([T1, T1, T2, T2, T1, T2, T3, T3, one, jnp.zeros_like(one)], 0).astype(jnp.bfloat16)

def cell_rows(u, w, a):
    T1, T2, T3 = parts(u, w, a)
    r8 = row_of(T1.shape)
    r = r8 % 4
    xy = r <= 1
    A1 = jnp.where(xy, 2 * T1, -1.0)
    A2 = jnp.where(xy, 2 * T2, 0.0)
    A3 = jnp.where(xy, 2 * T3, 0.0)
    outs = []
    for k in range(2):
        mine = (r8 // 4) == k
        G = [jnp.where(mine, A, 0.0) for A in (A1, A2, A3)]
        def n(T, i):
            return -T[4 * k + i : 4 * k + i + 1]
        z = jnp.zeros_like(n(T1, 0))
        norm = jnp.concatenate([n(T1, 2), n(T2, 2), n(T1, 3), n(T2, 3), n(T3, 3), z, z, z], 0)
        G1, G2, G3 = G
        outs.append(jnp.concatenate([G1, G2, G1, G2, G3, G3, G1, G2, norm, jnp.zeros_like(norm)], 0))
    return outs

def fwd_kernel(scale_ref, var_ref, pts_ref, w_ref, xy_ref, out_ref, rhs, lhs, acc, *, NB, MB, SB):
    p = pl.program_id(0)
    q = 2 * p
    M = pts_ref.shape[2]
    N = xy_ref.shape[1]
    r81 = row_of((8, 1))
    a = jnp.where(r81 < 4, scale_ref[q], scale_ref[q + 1])
    CH = 512
    def build(i, _):
        s = pl.ds(pl.multiple_of(i * CH, CH), CH)
        a0 = pts_ref[0, pl.ds(q, 1), s]; b0 = pts_ref[0, pl.ds(q + 1, 1), s]
        a1 = pts_ref[1, pl.ds(q, 1), s]; b1 = pts_ref[1, pl.ds(q + 1, 1), s]
        m = row_of((8, CH)) < 4
        rhs[:, s] = point_rows(jnp.where(m, a0, b0), jnp.where(m, a1, b1), a)
        return 0
    lax.fori_loop(0, M // CH, build, 0)
    cu = jnp.broadcast_to(xy_ref[0:1, :], (8, N))
    cw = jnp.broadcast_to(xy_ref[1:2, :], (8, N))
    L0, L1 = cell_rows(cu, cw, a)
    lhs[0] = L0.T.astype(jnp.bfloat16)
    lhs[1] = L1.T.astype(jnp.bfloat16)
    for k in range(2):
        acc[...] = jnp.zeros_like(acc)
        def step(i, _):
            base = i * MB
            for nb in range(N // NB):
                X = lhs[k, nb * NB:(nb + 1) * NB, :]
                t = acc[nb * NB:(nb + 1) * NB, :]
                for j in range(MB // SB):
                    s = pl.ds(pl.multiple_of(base + j * SB, SB), SB)
                    E = jnp.dot(X, rhs[:, s], preferred_element_type=jnp.float32)
                    e = jnp.exp2(E) * w_ref[pl.ds(q + k, 1), s]
                    for c in range(SB // 128):
                        t = t + e[:, c * 128:(c + 1) * 128]
                acc[nb * NB:(nb + 1) * NB, :] = t
            return 0
        lax.fori_loop(0, M // MB, step, 0)
        res = lax.dot_general(jnp.ones((8, 128), jnp.float32), acc[...], (((1,), (1,)), ((), ())),
                              precision=lax.Precision.HIGHEST, preferred_element_type=jnp.float32)
        out_ref[pl.ds(q + k, 1), :] = res[0:1] * var_ref[q + k]

def fwd(scale, var, pts, w, xy, NB=256, MB=1024, SB=512):
    _, Q, M = pts.shape
    N = xy.shape[1]
    return pl.pallas_call(
        functools.partial(fwd_kernel, NB=NB, MB=MB, SB=SB),
        grid=(Q // 2,),
        out_shape=jax.ShapeDtypeStruct((Q, N), jnp.float32),
        in_specs=[pl.BlockSpec(memory_space=pltpu.SMEM)] * 2 + [pl.BlockSpec(memory_space=pltpu.VMEM)] * 3,
        out_specs=pl.BlockSpec(memory_space=pltpu.VMEM),
        scratch_shapes=[pltpu.VMEM((80, M), jnp.bfloat16), pltpu.VMEM((2, N, 80), jnp.bfloat16), pltpu.VMEM((N, 128), jnp.float32)],
        compiler_params=pltpu.CompilerParams(vmem_limit_bytes=48 << 20),
        name="forward",
    )(scale, var, pts, w, xy)

def bwd_kernel(scale_ref, var_ref, pts_ref, lg_ref, xy_ref, out_ref, rhs, lhs, lgb, *, NB, MB, MI):
    p = pl.program_id(0)
    q = 2 * p
    M = pts_ref.shape[2]
    N = xy_ref.shape[1]
    r81 = row_of((8, 1))
    a = jnp.where(r81 < 4, scale_ref[q], scale_ref[q + 1])
    CH = 512
    def build(i, _):
        s = pl.ds(pl.multiple_of(i * CH, CH), CH)
        a0 = pts_ref[0, pl.ds(q, 1), s]; b0 = pts_ref[0, pl.ds(q + 1, 1), s]
        a1 = pts_ref[1, pl.ds(q, 1), s]; b1 = pts_ref[1, pl.ds(q + 1, 1), s]
        m = row_of((8, CH)) < 4
        rhs[:, s] = point_rows(jnp.where(m, a0, b0), jnp.where(m, a1, b1), a)
        return 0
    lax.fori_loop(0, M // CH, build, 0)
    cu = jnp.broadcast_to(xy_ref[0:1, :], (8, N))
    cw = jnp.broadcast_to(xy_ref[1:2, :], (8, N))
    L0, L1 = cell_rows(cu, cw, a)
    lhs[0] = L0.T.astype(jnp.bfloat16)
    lhs[1] = L1.T.astype(jnp.bfloat16)
    for k in range(2):
        lgb[...] = jnp.broadcast_to(lg_ref[pl.ds(q + k, 1), :], (128, N)).T
        def step(i, _):
            for j in range(MI):
                s = pl.ds(pl.multiple_of((i * MI + j) * MB, MB), MB)
                R = rhs[:, s]
                accs = [jnp.zeros((8, 128), jnp.float32) for _ in range(MB // 128)]
                for nb in range(N // NB):
                    X = lhs[k, nb * NB:(nb + 1) * NB, :]
                    E = jnp.dot(X, R, preferred_element_type=jnp.float32)
                    e = jnp.exp2(E)
                    g = lgb[nb * NB:(nb + 1) * NB, :]
                    for c in range(MB // 128):
                        pr = (e[:, c * 128:(c + 1) * 128] * g).reshape(NB // 8, 8, 128)
                        accs[c] = accs[c] + jnp.sum(pr, 0)
                row = jnp.concatenate([jnp.sum(x, 0, keepdims=True) for x in accs], 1)
                out_ref[pl.ds(q + k, 1), s] = row * var_ref[q + k]
            return 0
        lax.fori_loop(0, M // (MB * MI), step, 0)

def bwd(scale, var, pts, lg, xy, NB=256, MB=1024, MI=1):
    _, Q, M = pts.shape
    N = xy.shape[1]
    return pl.pallas_call(
        functools.partial(bwd_kernel, NB=NB, MB=MB, MI=MI),
        grid=(Q // 2,),
        out_shape=jax.ShapeDtypeStruct((Q, M), jnp.float32),
        in_specs=[pl.BlockSpec(memory_space=pltpu.SMEM)] * 2 + [pl.BlockSpec(memory_space=pltpu.VMEM)] * 3,
        out_specs=pl.BlockSpec(memory_space=pltpu.VMEM),
        scratch_shapes=[pltpu.VMEM((80, M), jnp.bfloat16), pltpu.VMEM((2, N, 80), jnp.bfloat16), pltpu.VMEM((N, 128), jnp.float32)],
        compiler_params=pltpu.CompilerParams(vmem_limit_bytes=48 << 20),
        name="backward",
    )(scale, var, pts, lg, xy)


def middle_kernel(idx_ref, latent_ref, mixing_ref, noise_ref, expr_ref, grad_ref, cell_ref, hot, *, scale):
    @pl.when(pl.program_id(0) == 0)
    def _():
        rows = lax.broadcasted_iota(jnp.int32, hot.shape, 1)
        hot[...] = jnp.where(rows == idx_ref[...], 1.0, 0.0).astype(jnp.bfloat16)
        cell_ref[...] = jnp.zeros_like(cell_ref)

    observed = jnp.dot(hot[...], expr_ref[...], preferred_element_type=jnp.float32)
    predicted = lax.dot_general(
        latent_ref[...], mixing_ref[...], (((0,), (0,)), ((), ())), preferred_element_type=jnp.float32
    )
    weighted = (noise_ref[...] * (observed - predicted)).astype(jnp.bfloat16)
    grad_ref[...] = scale * jnp.dot(latent_ref[...], weighted, preferred_element_type=jnp.float32)
    cell_ref[...] += scale * lax.dot_general(
        mixing_ref[...], weighted, (((1,), (1,)), ((), ())), preferred_element_type=jnp.float32
    )


def middle(idx, latent, mixing, noise, expr, scale):
    q, cells = latent.shape
    rows, genes = expr.shape
    width = math.gcd(genes, 512)
    return pl.pallas_call(
        functools.partial(middle_kernel, scale=scale),
        grid=(genes // width,),
        out_shape=(
            jax.ShapeDtypeStruct((q, genes), jnp.float32),
            jax.ShapeDtypeStruct((q, cells), jnp.float32),
        ),
        in_specs=[
            pl.BlockSpec((cells, 1), lambda i: (0, 0)),
            pl.BlockSpec((q, cells), lambda i: (0, 0)),
            pl.BlockSpec((q, width), lambda i: (0, i)),
            pl.BlockSpec((1, width), lambda i: (0, i)),
            pl.BlockSpec((rows, width), lambda i: (0, i)),
        ],
        out_specs=(
            pl.BlockSpec((q, width), lambda i: (0, i)),
            pl.BlockSpec((q, cells), lambda i: (0, 0)),
        ),
        scratch_shapes=[pltpu.VMEM((cells, rows), jnp.bfloat16)],
        compiler_params=pltpu.CompilerParams(vmem_limit_bytes=32 << 20),
        name="middle",
    )(idx, latent, mixing, noise, expr)


def on_device(cell_index, coords_table, expr_table, inducing, ind_weights, lengthscale, variance, mixing, noise_prec):
    genes, lats, subs = (lax.axis_size(name) for name in ("gene", "lat", "sub"))
    blocks = lats * subs
    cells = cell_index.shape[0]
    local_q = ind_weights.shape[0]
    points = ind_weights.shape[1]
    latent_cuts = math.gcd(genes, local_q // 2)
    cell_cuts = genes // latent_cuts
    own_q = local_q // latent_cuts
    part = cells // cell_cuts
    place = lax.axis_index("gene")
    first_q = place // cell_cuts * own_q
    every = ("gene", "lat", "sub")

    local_xy = jnp.take(coords_table, cell_index, axis=1)
    every_xy = lax.all_gather(local_xy, ("lat", "sub"), axis=1, tiled=True)
    every_xy = every_xy.reshape(2, blocks, cell_cuts, part)
    kernel_xy = lax.dynamic_slice_in_dim(every_xy, place % cell_cuts, 1, 2).reshape(2, blocks * part)
    own = functools.partial(lax.dynamic_slice_in_dim, start_index=first_q, slice_size=own_q)
    own_points = own(inducing, axis=1)
    own_weights = own(ind_weights, axis=0)
    own_scale = math.sqrt(0.5 * LOG2E) / own(lengthscale, axis=0)
    own_variance = own(variance, axis=0)

    partial = fwd(own_scale, own_variance, own_points, own_weights, kernel_xy)
    partial = partial.reshape(own_q, blocks, part).transpose(1, 0, 2)
    partial = jnp.broadcast_to(partial[None], (genes, blocks, own_q, part))
    partial = partial.reshape(genes * blocks, own_q, part)
    pieces = lax.all_to_all(partial, every, 0, 0, tiled=True)
    pieces = pieces.reshape(latent_cuts, cell_cuts, lats, subs, own_q, part).sum(3).astype(jnp.bfloat16)
    latent = pieces.transpose(2, 0, 3, 1, 4).reshape(lats * local_q, cells)

    grad_scale = -1.0 / math.sqrt(cells * blocks)
    mixing_term, cell_term = middle(
        cell_index[:, None], latent, mixing, noise_prec[None, :], expr_table, grad_scale
    )
    grad_mixing = lax.psum(mixing_term, ("lat", "sub"))

    send = cell_term.reshape(lats, latent_cuts, own_q, cell_cuts, part).transpose(1, 3, 0, 2, 4)
    send = jnp.broadcast_to(send[:, :, :, None], (latent_cuts, cell_cuts, lats, subs, own_q, part))
    send = send.reshape(genes * blocks, own_q, part)
    pieces = lax.all_to_all(send, every, 0, 0, tiled=True)
    latent_grad = pieces.reshape(genes, blocks, own_q, part).sum(0).transpose(1, 0, 2)
    latent_grad = latent_grad.reshape(own_q, blocks * part)

    inducing_term = bwd(own_scale, own_variance, own_points, latent_grad, kernel_xy)
    gathered = lax.all_gather(inducing_term, "gene", axis=0, tiled=True)
    grad_inducing = gathered.reshape(latent_cuts, cell_cuts, own_q, points).sum(1)
    return (grad_mixing, grad_inducing.reshape(local_q, points))


def solution(mesh):
    in_specs = (
        P(("group", "lat", "sub")),
        P("group", ("lat", "sub")),
        P(("group", "lat", "sub"), "gene"),
        P("group", "lat", "sub"),
        P(("group", "lat"), "sub"),
        P(("group", "lat")),
        P(("group", "lat")),
        P("group", "gene"),
        P(("group", "gene")),
    )
    out_specs = (P("group", "gene"), P(("group", "lat"), "sub"))
    return jax.shard_map(
        on_device, mesh=mesh, in_specs=in_specs, out_specs=out_specs, check_vma=False
    )
```

time: 749 us -> 136 us (0.18)
  matrix products: 325 us -> 0 us
  local copies, waits for them, and re-layouts: 220 us -> 11.8 us
  loops' own time: 90 us -> 0 us
  Pallas kernels: 0 us -> 61.6 us
  waiting for transfers between devices: 58.1 us -> 7.09 us
    dot_general x67 -> x0, matrix products: 325 us -> none  [the longest x32 191 us: forward(): jnp.dot(kernel_tile(kernel_xy, points, length, height), weights, precisio...]
    dynamic_slice x129 -> x3, local copies, waits for them, and re-layouts: 119 us -> 1.67 us  [the longest x1 0.91 us: on_device(): own_weights = own(ind_weights, axis=0)]
    another operation x2 -> x0, loops' own time: 90 us -> none  [the longest x1 46 us: on_device(): lax.map(backward, (moved, latent_grad, lengthscale, variance))]
    pallas_call x0 -> x3, Pallas kernels: none -> 61.6 us  [the longest x1 29 us: fwd(): pl.pallas_call(functools.partial(fwd_kernel, NB=NB, MB=MB, SB=SB), grid=(...]
    dynamic_update_slice x64 -> x0, local copies, waits for them, and re-layouts: 52.9 us -> none  [the longest x32 51.7 us: on_device(): lax.map(backward, (moved, latent_grad, lengthscale, variance))]
    psum x1 -> x0, waiting for transfers between devices: 35.7 us -> none  [on_device(): grad_inducing = lax.psum(partial_inducing, 'gene')]
    slice x128 -> x0, local copies, waits for them, and re-layouts: 29.4 us -> none  [kernel_tile(): delta_x = cell_xy[0][:, None] - points[0][None, :]]
    unnamed x6 -> x1, waiting for transfers between devices: 20.2 us -> 0.02 us
  transfers between devices with their start and end apart: 5 -> 2, of which waited for: 3 -> 1; matrix products, arithmetic and copies ran while one was open for 35% -> 1% of each run, Pallas kernels for 0% -> 20%
where the time goes in v1:
time: 136 us
  Pallas kernels  61.6 us (45%)
  blocking collectives  32.5 us (24%)
  between operations  14.1 us (10%)
  local copies, waits for them, and re-layouts  11.8 us (9%)
  waiting for transfers between devices  7.09 us (5%)
  starting transfers between devices  6.46 us (5%)
  other arithmetic  2.22 us (2%)
    pallas_call x1, Pallas kernels, fwd(): pl.pallas_call(functools.partial(fwd_kernel, NB=NB, MB=MB, SB=SB), grid=(...  29 us
    pallas_call x1, Pallas kernels, bwd(): pl.pallas_call(functools.partial(bwd_kernel, NB=NB, MB=MB, MI=MI), grid=(...  26.6 us
    all_gather x1, blocking collectives, on_device(): gathered = lax.all_gather(inducing_term, 'gene', axis=0, tiled=True)  15.9 us
    all_to_all x1, blocking collectives, on_device(): pieces = lax.all_to_all(send, every, 0, 0, tiled=True)  10.5 us
    unnamed x11, local copies, waits for them, and re-layouts  7.84 us
    all_to_all x1, waiting for transfers between devices, on_device(): pieces = lax.all_to_all(partial, every, 0, 0, tiled=True)  7.07 us
    all_to_all x1, starting transfers between devices, on_device(): pieces = lax.all_to_all(partial, every, 0, 0, tiled=True)  6.41 us
    all_gather x1, blocking collectives, on_device(): every_xy = lax.all_gather(local_xy, ('lat', 'sub'), axis=1, tiled=True)  6.11 us
  transfers between devices with their start and end apart: 2, of which 1 were waited for; matrix products, arithmetic and copies ran while one was open for 1% of the time, Pallas kernels for 20%

profile of v1, /device:TPU:0, one launch (start us, length us, event | category | flops | bytes accessed | tf_op | source)
XLA Modules:
  0.0 135.8 jit_solution(13552956447962361366)
XLA Ops:
  7.2 0.0 copy-start
  7.2 0.8 compare_and_fusion
  8.0 0.7 compare_select_fusion
  8.6 0.7 dynamic-slice_divide_fusion.scale_ref
  9.4 0.7 dynamic_slice.14.var_ref
  10.1 0.9 constant_dynamic-slice_fusion.w_ref
  11.0 0.0 copy-done
  11.1 0.8 copy.18
  11.9 0.7 gather_fusion
  12.6 0.1 copy.19
  12.7 6.1 %all_gather.6.xy_ref = f32[2,1024]{1,0:T(2,128)S(1)} all-gather(f32[2,256]{1,0:T(2,128)S(1)} %select_bitcast_fusion), channel_id=1, replica_groups=mesh['group'=2,'gene'=4,'lat'=2,'sub'=2] {'lat','sub'}, dimensions={1}, use_global_device_ids=true | all-gather | bytes 10240 | tf_op jit(solution)/shard_map/all_gather | solution.py:234
  18.8 29.0 %forward.1 = f32[8,1024]{1,0:T(8,128)S(1)} custom-call(f32[8]{0:T(128)S(1)} %dynamic-slice_divide_fusion.scale_ref, f32[8]{0:T(128)S(1)} %dynamic_slice.14.var_ref, f32[2,8,4096]{2,1,0:T(8,128)S(1)} %constant_dynamic-slice_fusion.1.pts_ref, f32[8,4096]{1,0:T(8,128)S(1)} %constant_dynamic-slice_fusion.w_ref, f32[2,1024]{1,0:T(2,128)S(1)} %all_gather.6.xy_ref), custom_call_target="tpu_custom_call" | custom-call | tf_op jit(solution)/shard_map/forward/pallas_call | solution.py:106
  47.8 0.7 broadcast_in_dim.36
  48.5 6.4 %all-to-all-start = ((f32[16,8,256]{2,1,0:T(8,128)}), f32[16,8,256]{2,1,0:T(8,128)S(1)}, u32[]{:S(2)}, u32[]{:S(2)}) async-start(f32[16,8,256]{2,1,0:T(8,128)} %bitcast.4), calls=%async_computation | async-start | bytes 262144 | tf_op jit(solution)/shard_map/all_to_all | solution.py:247
  54.9 0.0 all-reduce.2.cloned.1.call-start
  55.0 0.8 copy.21.idx_ref
  55.8 7.1 %all-to-all-done = f32[16,8,256]{2,1,0:T(8,128)S(1)} async-done(((f32[16,8,256]{2,1,0:T(8,128)}), f32[16,8,256]{2,1,0:T(8,128)S(1)}, u32[]{:S(2)}, u32[]{:S(2)}) %all-to-all-start) | async-done | bytes 131104 | tf_op jit(solution)/shard_map/all_to_all | solution.py:247
  62.9 0.0 copy-start.1
  62.9 2.2 %copy-done.1 = bf16[512,4096]{1,0:T(8,128)(2,1)S(1)} copy-done((bf16[512,4096]{1,0:T(8,128)(2,1)S(1)}, bf16[512,4096]{1,0:T(8,128)(2,1)}, u32[]{:S(2)}) %copy-start.1) | copy-done | bytes 4194328
  65.1 0.0 copy-start.2
  65.1 1.0 copy-done.2
  66.1 0.0 copy-start.3
  66.1 0.7 copy-done.3
  66.9 5.9 %middle.1 = (f32[64,4096]{1,0:T(8,128)}, f32[64,256]{1,0:T(8,128)S(1)}) custom-call(s32[256,1]{1,0:T(8,128)S(1)} %copy.21.idx_ref, bf16[64,256]{1,0:T(8,128)(2,1)S(1)} %bitcast.26, bf16[64,4096]{1,0:T(8,128)(2,1)S(1)} %copy-done.2, f32[1,4096]{1,0:T(1,128)S(1)} %bitcast.30, bf16[512,4096]{1,0:T(8,128)(2,1)S(1)} %copy-done.1), custom_call_target="tpu_custom_call" | custom-call | tf_op jit(solution)/shard_map/middle/pallas_call | solution.py:195
  72.8 0.0 all-reduce.2.cloned.1.call-update
  72.8 10.5 %all_to_all.10 = f32[16,8,256]{2,1,0:T(8,128)S(1)} all-to-all(f32[16,8,256]{2,1,0:T(8,128)S(1)} %bitcast.32), channel_id=1, replica_groups=mesh['group'=2,'gene'=4,'lat'=2,'sub'=2] {'gene','lat','sub'}, dimensions={0} | all-to-all | bytes 262144 | tf_op jit(solution)/shard_map/all_to_all | solution.py:260
  83.4 26.6 %backward.1 = f32[8,4096]{1,0:T(8,128)S(1)} custom-call(f32[8]{0:T(128)S(1)} %dynamic-slice_divide_fusion.scale_ref, f32[8]{0:T(128)S(1)} %dynamic_slice.14.var_ref, f32[2,8,4096]{2,1,0:T(8,128)S(1)} %constant_dynamic-slice_fusion.1.pts_ref, f32[8,1024]{1,0:T(8,128)S(1)} %bitcast.27, f32[2,1024]{1,0:T(2,128)S(1)} %all_gather.6.xy_ref), custom_call_target="tpu_custom_call" | custom-call | tf_op jit(solution)/shard_map/backward/pallas_call | solution.py:161
  110.0 15.9 %all_gather.7 = f32[32,4096]{1,0:T(8,128)S(1)} all-gather(f32[8,4096]{1,0:T(8,128)S(1)} %backward.1), channel_id=1, replica_groups=mesh['group'=2,'gene'=4,'lat'=2,'sub'=2] {'gene'}, dimensions={0}, use_global_device_ids=true | all-gather | bytes 655360 | tf_op jit(solution)/shard_map/all_gather | solution.py:265
  125.9 0.0 all-reduce.2.cloned.1.call-done
  125.9 2.3 %copy.25 = f32[64,4096]{1,0:T(8,128)} copy(f32[64,4096]{1,0:T(8,128)} %all-reduce.2.cloned.1.call-done) | data formatting | bytes 2097152
  128.2 0.8 copy.26
  (8 shorter events, 0.1 us)
Async XLA Ops:
  7.2 3.9 %copy-start = (f32[2,32,4096]{2,1,0:T(8,128)S(1)}, f32[2,32,4096]{2,1,0:T(8,128)}, u32[]{:S(2)}) copy-start(f32[2,32,4096]{2,1,0:T(8,128)} %param.12) | copy-start | bytes 3145732
  48.5 14.4 %all-to-all-start = ((f32[16,8,256]{2,1,0:T(8,128)}), f32[16,8,256]{2,1,0:T(8,128)S(1)}, u32[]{:S(2)}, u32[]{:S(2)}) async-start(f32[16,8,256]{2,1,0:T(8,128)} %bitcast.4), calls=%async_computation | async-start | bytes 262144 | tf_op jit(solution)/shard_map/all_to_all | solution.py:247
  54.9 71.0 %all-reduce.2.cloned.1.call-start = ((), (), s32[]{:S(2)}) async-start(), calls=%async_computation.2 | async-start | bytes 2097152 | tf_op jit(solution)/shard_map/psum | solution.py:255
  62.9 2.2 %copy-start.1 = (bf16[512,4096]{1,0:T(8,128)(2,1)S(1)}, bf16[512,4096]{1,0:T(8,128)(2,1)}, u32[]{:S(2)}) copy-start(bf16[512,4096]{1,0:T(8,128)(2,1)} %expr_ref.1) | copy-start | bytes 12582916
  65.1 1.0 copy-start.2
  66.1 0.7 copy-start.3
Sparse Core Ops, SparseCore 0:
  72.9 35.1 all-reduce.1

commit v2 on v0

v2 whole, which is shorter than its diff:
```python
import functools
import math

import jax
import jax.numpy as jnp
from jax import lax
from jax.experimental import pallas as pl
from jax.experimental.pallas import tpu as pltpu
from jax.sharding import PartitionSpec as P

LOG2E = math.log2(math.e)

def row_of(shape):
    return lax.broadcasted_iota(jnp.int32, shape, 0)

def parts(u, w, a):
    L = u.shape[1]
    U = (u - 0.5) * a
    W = (w - 0.5) * a
    big = 1.5 * 2.0**20
    U1 = (U + big) - big
    W1 = (W + big) - big
    rU = U - U1
    rW = W - W1
    hi = U1 * U1 + W1 * W1
    lo = rU * (U1 + U) + rW * (W1 + W)
    r = row_of((8, L)) % 4
    T = jnp.where(r == 0, U, jnp.where(r == 1, W, jnp.where(r == 2, hi, lo)))
    rc = row_of((8, 1)) % 4
    magic = jnp.where(rc <= 1, 1.5 * 2.0**20, jnp.where(rc == 2, 1.5 * 2.0**26, 1.5 * 2.0**18)).astype(jnp.float32)
    T1 = ((T + magic) - magic).astype(jnp.bfloat16).astype(jnp.float32)
    R = T - T1
    T2 = R.astype(jnp.bfloat16).astype(jnp.float32)
    T3 = R - T2
    return T1, T2, T3

def point_rows(u, w, a):
    T1, T2, T3 = parts(u, w, a)
    one = jnp.ones_like(T1)
    return jnp.concatenate([T1, T1, T2, T2, T1, T2, T3, T3, one, jnp.zeros_like(one)], 0).astype(jnp.bfloat16)

def cell_rows(u, w, a):
    T1, T2, T3 = parts(u, w, a)
    r8 = row_of(T1.shape)
    r = r8 % 4
    xy = r <= 1
    A1 = jnp.where(xy, 2 * T1, -1.0)
    A2 = jnp.where(xy, 2 * T2, 0.0)
    A3 = jnp.where(xy, 2 * T3, 0.0)
    outs = []
    for k in range(2):
        mine = (r8 // 4) == k
        G = [jnp.where(mine, A, 0.0) for A in (A1, A2, A3)]
        def n(T, i):
            return -T[4 * k + i : 4 * k + i + 1]
        z = jnp.zeros_like(n(T1, 0))
        norm = jnp.concatenate([n(T1, 2), n(T2, 2), n(T1, 3), n(T2, 3), n(T3, 3), z, z, z], 0)
        G1, G2, G3 = G
        outs.append(jnp.concatenate([G1, G2, G1, G2, G3, G3, G1, G2, norm, jnp.zeros_like(norm)], 0))
    return outs

VMEM = pltpu.VMEM
SMEM = pltpu.SMEM


def whole(space):
    return pl.BlockSpec(memory_space=space)


def partner(place, step, blocks):
    if blocks & (blocks - 1) == 0:
        return place ^ step
    return (place + step) % blocks


def locate_kernel(index_ref, table_ref, out_ref):
    table = table_ref[...]
    rows = table.shape[1]
    column = jnp.concatenate([table, jnp.zeros((8 - table.shape[0], rows), jnp.float32)], 0).T
    hot = lax.broadcasted_iota(jnp.int32, (rows, index_ref.shape[1]), 0) == index_ref[...]
    picked = [
        jnp.sum(jnp.where(hot, column[:, axis : axis + 1], 0.0), 0, keepdims=True)
        for axis in range(table.shape[0])
    ]
    out_ref[...] = jnp.concatenate(picked, 0)


def locate(index, table):
    return pl.pallas_call(
        locate_kernel,
        out_shape=jax.ShapeDtypeStruct((table.shape[0], index.shape[0]), jnp.float32),
        name="locate",
    )(index[None, :], table)


def scale_of(length_ref, q):
    lengths = jnp.where(row_of((8, 1)) < 4, length_ref[q], length_ref[q + 1])
    return math.sqrt(0.5 * LOG2E) / lengths


def build_kernel(first_ref, length_ref, points_ref, rhs_ref):
    q = first_ref[0] + 2 * pl.program_id(0)
    scale = scale_of(length_ref, q)
    width = math.gcd(points_ref.shape[2], 512)

    def step(i, _):
        s = pl.ds(pl.multiple_of(i * width, width), width)
        low = row_of((8, width)) < 4
        u, w = (
            jnp.where(low, points_ref[d, pl.ds(q, 1), s], points_ref[d, pl.ds(q + 1, 1), s]) for d in (0, 1)
        )
        rhs_ref[0, :, s] = point_rows(u, w, scale)
        return 0

    lax.fori_loop(0, points_ref.shape[2] // width, step, 0)


def build(first, lengths, points, own_q):
    count = points.shape[2]
    return pl.pallas_call(
        build_kernel,
        grid=(own_q // 2,),
        out_shape=jax.ShapeDtypeStruct((own_q // 2, 80, count), jnp.bfloat16),
        in_specs=[whole(SMEM), whole(SMEM), whole(VMEM)],
        out_specs=pl.BlockSpec((1, 80, count), lambda i: (i, 0, 0)),
        compiler_params=pltpu.CompilerParams(vmem_limit_bytes=16 << 20),
        cost_estimate=pl.CostEstimate(flops=4_000_000_000, bytes_accessed=4_000_000, transcendentals=0),
        name="build",
    )(first, lengths, points)


def forward_kernel(first_ref, order_ref, length_ref, var_ref, weight_ref, rhs_ref, *rest, blocks, NB, SB):
    xy_refs, (out_ref, lhs_ref, acc) = rest[:blocks], rest[blocks:]
    local = 2 * pl.program_id(0)
    q = first_ref[0] + local
    points = rhs_ref.shape[2]
    part = xy_refs[0].shape[1]
    cells = blocks * part
    scale = scale_of(length_ref, q)
    u, w = (
        jnp.broadcast_to(jnp.concatenate([ref[d : d + 1, :] for ref in xy_refs], 1), (8, cells)) for d in (0, 1)
    )
    for k, rows in enumerate(cell_rows(u, w, scale)):
        lhs_ref[0, k] = rows.T.astype(jnp.bfloat16)

    def latent(k, _):
        for nb in range(cells // NB):
            rows = slice(nb * NB, (nb + 1) * NB)
            cell = lhs_ref[0, k, rows, :]
            total = jnp.zeros((NB, 128), jnp.float32)
            for j in range(points // SB):
                s = slice(j * SB, (j + 1) * SB)
                e = jnp.exp2(jnp.dot(cell, rhs_ref[0, :, s], preferred_element_type=jnp.float32))
                weight = weight_ref[pl.ds(q + k, 1), s]
                for c in range(SB // 128):
                    total = total + e[:, c * 128 : (c + 1) * 128] * weight[:, c * 128 : (c + 1) * 128]
            acc[rows, :] = total
        result = lax.dot_general(
            jnp.ones((8, 128), jnp.float32),
            acc[...],
            (((1,), (1,)), ((), ())),
            precision=lax.Precision.HIGHEST,
            preferred_element_type=jnp.float32,
        )
        result = result[0:1] * var_ref[q + k]
        for b in range(blocks):
            for copy in range(out_ref.shape[0]):
                out_ref[copy, order_ref[b], pl.ds(local + k, 1), :] = result[:, b * part : (b + 1) * part]
        return 0

    lax.fori_loop(0, 2, latent, 0)


def forward(first, order, lengths, var, weights, rhs, xys, own_q, copies):
    points = rhs.shape[2]
    blocks = len(xys)
    part = xys[0].shape[1]
    cells = blocks * part
    return pl.pallas_call(
        functools.partial(forward_kernel, blocks=blocks, NB=math.gcd(cells, 256), SB=math.gcd(points, 512)),
        grid=(own_q // 2,),
        out_shape=(
            jax.ShapeDtypeStruct((copies, blocks, own_q, part), jnp.float32),
            jax.ShapeDtypeStruct((own_q // 2, 2, cells, 80), jnp.bfloat16),
        ),
        in_specs=[whole(SMEM)] * 4
        + [whole(VMEM), pl.BlockSpec((1, 80, points), lambda i: (i, 0, 0))]
        + [whole(VMEM)] * blocks,
        out_specs=(whole(VMEM), pl.BlockSpec((1, 2, cells, 80), lambda i: (i, 0, 0, 0))),
        scratch_shapes=[VMEM((cells, 128), jnp.float32)],
        compiler_params=pltpu.CompilerParams(vmem_limit_bytes=24 << 20),
        cost_estimate=pl.CostEstimate(flops=25_000_000_000, bytes_accessed=4_000_000, transcendentals=0),
        name="forward",
    )(first, order, lengths, var, weights, rhs, *xys)


def backward_kernel(first_ref, order_ref, var_ref, grad_ref, rhs_ref, lhs_ref, out_ref, held, spread, *, NB):
    local = 2 * pl.program_id(0)
    q = first_ref[0] + local
    points = rhs_ref.shape[2]
    copies, blocks, _, part = grad_ref.shape
    cells = blocks * part

    @pl.when(pl.program_id(0) == 0)
    def _():
        for b in range(blocks):
            held[b] = functools.reduce(jnp.add, [grad_ref[copy, order_ref[b]] for copy in range(copies)])

    def latent(k, _):
        for b in range(blocks):
            row = held[b, pl.ds(local + k, 1), :]
            spread[b * part : (b + 1) * part, :] = jnp.broadcast_to(row, (128, part)).T
        totals = [jnp.zeros((8, 128), jnp.float32) for _ in range(points // 128)]
        for nb in range(cells // NB):
            rows = slice(nb * NB, (nb + 1) * NB)
            cell = lhs_ref[0, k, rows, :]
            e = jnp.exp2(jnp.dot(cell, rhs_ref[0], preferred_element_type=jnp.float32))
            grad = spread[rows, :]
            for c in range(points // 128):
                term = (e[:, c * 128 : (c + 1) * 128] * grad).reshape(NB // 8, 8, 128)
                totals[c] = totals[c] + jnp.sum(term, 0)
        row = jnp.concatenate([jnp.sum(total, 0, keepdims=True) for total in totals], 1)
        out_ref[pl.ds(local + k, 1), :] = row * var_ref[q + k]
        return 0

    lax.fori_loop(0, 2, latent, 0)


def backward(first, order, var, grads, rhs, lhs):
    pairs, _, points = rhs.shape
    _, blocks, own_q, part = grads.shape
    cells = blocks * part
    return pl.pallas_call(
        functools.partial(backward_kernel, NB=math.gcd(cells, 256)),
        grid=(pairs,),
        out_shape=jax.ShapeDtypeStruct((own_q, points), jnp.float32),
        in_specs=[whole(SMEM)] * 3
        + [
            whole(VMEM),
            pl.BlockSpec((1, 80, points), lambda i: (i, 0, 0)),
            pl.BlockSpec((1, 2, cells, 80), lambda i: (i, 0, 0, 0)),
        ],
        out_specs=whole(VMEM),
        scratch_shapes=[VMEM((blocks, own_q, part), jnp.float32), VMEM((cells, 128), jnp.float32)],
        compiler_params=pltpu.CompilerParams(vmem_limit_bytes=24 << 20),
        cost_estimate=pl.CostEstimate(flops=25_000_000_000, bytes_accessed=4_000_000, transcendentals=0),
        name="backward",
    )(first, order, var, grads, rhs, lhs)


def observe_kernel(index_ref, expr_ref, out_ref, hot):
    @pl.when(pl.program_id(0) == 0)
    def _():
        rows = lax.broadcasted_iota(jnp.int32, hot.shape, 1)
        hot[...] = jnp.where(rows == index_ref[...], 1.0, 0.0).astype(jnp.bfloat16)

    picked = jnp.dot(hot[...], expr_ref[...], preferred_element_type=jnp.float32)
    out_ref[...] = picked.astype(jnp.bfloat16)


def observe(index, expr):
    rows, genes = expr.shape
    cells = index.shape[0]
    width = math.gcd(genes, 1024)
    return pl.pallas_call(
        observe_kernel,
        grid=(genes // width,),
        out_shape=jax.ShapeDtypeStruct((cells, genes), jnp.bfloat16),
        in_specs=[pl.BlockSpec((cells, 1), lambda i: (0, 0)), pl.BlockSpec((rows, width), lambda i: (0, i))],
        out_specs=pl.BlockSpec((cells, width), lambda i: (0, i)),
        scratch_shapes=[VMEM((cells, rows), jnp.bfloat16)],
        compiler_params=pltpu.CompilerParams(vmem_limit_bytes=16 << 20),
        cost_estimate=pl.CostEstimate(flops=3_000_000_000, bytes_accessed=6_000_000, transcendentals=0),
        name="observe",
    )(index[:, None], expr)


def middle_kernel(piece_ref, mixing_ref, noise_ref, observed_ref, grad_ref, send_ref, wide, *, scale, cuts, width):
    latent_cuts, cell_cuts, lats, subs = cuts
    own_q, part = piece_ref.shape[2:]
    for lat in range(lats):
        for a in range(latent_cuts):
            for b in range(cell_cuts):
                pieces = [piece_ref[a * cell_cuts + b, lat * subs + sub] for sub in range(subs)]
                first = (lat * latent_cuts + a) * own_q
                wide[first : first + own_q, b * part : (b + 1) * part] = functools.reduce(jnp.add, pieces)
    latent = wide[...].astype(jnp.bfloat16)
    turned = wide[...].T.astype(jnp.bfloat16)
    total = jnp.zeros(latent.shape, jnp.float32)
    for j in range(mixing_ref.shape[1] // width):
        s = slice(j * width, (j + 1) * width)
        predicted = jnp.dot(turned, mixing_ref[:, s], preferred_element_type=jnp.float32)
        observed = observed_ref[:, s].astype(jnp.float32)
        weighted = (noise_ref[:, s] * (observed - predicted)).astype(jnp.bfloat16)
        grad_ref[:, s] = scale * jnp.dot(latent, weighted, preferred_element_type=jnp.float32)
        total = total + lax.dot_general(
            mixing_ref[:, s], weighted, (((1,), (1,)), ((), ())), preferred_element_type=jnp.float32
        )
    wide[...] = scale * total
    for lat in range(lats):
        for a in range(latent_cuts):
            for b in range(cell_cuts):
                first = (lat * latent_cuts + a) * own_q
                piece = wide[first : first + own_q, b * part : (b + 1) * part]
                for sub in range(subs):
                    send_ref[a * cell_cuts + b, lat * subs + sub] = piece


def middle(pieces, mixing, noise, observed, scale, cuts):
    cells, genes = observed.shape
    q = mixing.shape[0]
    return pl.pallas_call(
        functools.partial(middle_kernel, scale=scale, cuts=cuts, width=math.gcd(genes, 512)),
        out_shape=(
            jax.ShapeDtypeStruct((q, genes), jnp.float32),
            jax.ShapeDtypeStruct(pieces.shape, jnp.float32),
        ),
        scratch_shapes=[VMEM((q, cells), jnp.float32)],
        compiler_params=pltpu.CompilerParams(vmem_limit_bytes=24 << 20),
        cost_estimate=pl.CostEstimate(flops=3_000_000_000, bytes_accessed=4_000_000, transcendentals=0),
        name="middle",
    )(pieces, mixing, noise[None, :], observed)


def shifted(x, axes, step, size):
    return lax.ppermute(x, axes, [(partner(i, step, size), i) for i in range(size)])


def sum_over(x, first_axis, then_axis):
    n = lax.axis_size(first_axis)
    m = lax.axis_size(then_axis)
    me = lax.axis_index(first_axis)
    rows = x.shape[0] // n

    def rows_of(place):
        return lax.dynamic_slice_in_dim(x, place * rows, rows, 0)

    total = rows_of(me)
    for step in range(1, n):
        to = me ^ step if n & (n - 1) == 0 else (me - step) % n
        total = total + shifted(rows_of(to), first_axis, step, n)
    total = functools.reduce(jnp.add, [total] + [shifted(total, then_axis, step, m) for step in range(1, m)])
    out = lax.dynamic_update_slice_in_dim(jnp.zeros_like(x), total, me * rows, 0)
    for step in range(1, n):
        out = lax.dynamic_update_slice_in_dim(
            out, shifted(total, first_axis, step, n), partner(me, step, n) * rows, 0
        )
    return out


def on_device(cell_index, coords_table, expr_table, inducing, ind_weights, lengthscale, variance, mixing, noise_prec):
    genes, lats, subs = (lax.axis_size(name) for name in ("gene", "lat", "sub"))
    blocks = lats * subs
    cells = cell_index.shape[0]
    local_q, points = ind_weights.shape
    latent_cuts = math.gcd(genes, local_q // 2)
    cell_cuts = genes // latent_cuts
    cuts = (latent_cuts, cell_cuts, lats, subs)
    own_q = local_q // latent_cuts
    part = cells // cell_cuts
    place = lax.axis_index("gene")
    block = lax.axis_index("lat") * subs + lax.axis_index("sub")
    first = (place // cell_cuts * own_q).reshape(1)
    order = jnp.stack([partner(block, step, blocks) for step in range(blocks)])
    every = ("gene", "lat", "sub")

    local_xy = locate(cell_index, coords_table)
    xys = [local_xy] + [shifted(local_xy, ("lat", "sub"), step, blocks) for step in range(1, blocks)]
    xys = [lax.dynamic_slice_in_dim(xy, place % cell_cuts * part, part, 1) for xy in xys]
    rhs = build(first, lengthscale, inducing, own_q)

    partial, lhs = forward(first, order, lengthscale, variance, ind_weights, rhs, xys, own_q, genes)
    expr_table, partial = lax.optimization_barrier((expr_table, partial))
    pieces = lax.all_to_all(partial.reshape(genes * blocks, own_q, part), every, 0, 0, tiled=True)
    observed = observe(cell_index, expr_table)

    grad_scale = -1.0 / math.sqrt(cells * blocks)
    mixing_term, send = middle(
        pieces.reshape(genes, blocks, own_q, part), mixing, noise_prec, observed, grad_scale, cuts
    )
    pieces = lax.all_to_all(send.reshape(genes * blocks, own_q, part), every, 0, 0, tiled=True)
    grad_mixing = sum_over(mixing_term, "sub", "lat")

    inducing_term = backward(first, order, variance, pieces.reshape(genes, blocks, own_q, part), rhs, lhs)
    gathered = lax.all_gather(inducing_term, "gene", axis=0, tiled=True)
    grad_inducing = gathered.reshape(latent_cuts, cell_cuts, own_q, points).sum(1)
    return (grad_mixing, grad_inducing.reshape(local_q, points))


def solution(mesh):
    in_specs = (
        P(("group", "lat", "sub")),
        P("group", ("lat", "sub")),
        P(("group", "lat", "sub"), "gene"),
        P("group", "lat", "sub"),
        P(("group", "lat"), "sub"),
        P(("group", "lat")),
        P(("group", "lat")),
        P("group", "gene"),
        P(("group", "gene")),
    )
    out_specs = (P("group", "gene"), P(("group", "lat"), "sub"))
    return jax.shard_map(
        on_device, mesh=mesh, in_specs=in_specs, out_specs=out_specs, check_vma=False
    )
```

time: 749 us -> 115 us (0.15)
  matrix products: 325 us -> 0 us
  local copies, waits for them, and re-layouts: 220 us -> 16.4 us
  loops' own time: 90 us -> 0 us
  Pallas kernels: 0 us -> 52.6 us
  waiting for transfers between devices: 58.1 us -> 14.6 us
  blocking collectives: 30.4 us -> 16 us
  between operations: 13.9 us -> 0.86 us
  starting transfers between devices: 3.6 us -> 14 us
    dot_general x67 -> x0, matrix products: 325 us -> none  [the longest x32 191 us: forward(): jnp.dot(kernel_tile(kernel_xy, points, length, height), weights, precisio...]
    dynamic_slice x129 -> x1, local copies, waits for them, and re-layouts: 119 us -> 0.03 us  [rows_of(): return lax.dynamic_slice_in_dim(x, place * rows, rows, 0)]
    another operation x2 -> x0, loops' own time: 90 us -> none  [the longest x1 46 us: on_device(): lax.map(backward, (moved, latent_grad, lengthscale, variance))]
    dynamic_update_slice x64 -> x1, local copies, waits for them, and re-layouts: 52.9 us -> 0.04 us  [sum_over(): lax.dynamic_update_slice_in_dim(out, shifted(total, first_axis, step, n),...]
    pallas_call x0 -> x6, Pallas kernels: none -> 52.6 us  [the longest x1 24.1 us: forward(): pl.pallas_call(functools.partial(forward_kernel, blocks=blocks, NB=math.g...]
    psum x2 -> x0, waiting for transfers between devices: 35.7 us -> none  [the longest x1 35.7 us: on_device(): grad_inducing = lax.psum(partial_inducing, 'gene')]
    slice x128 -> x0, local copies, waits for them, and re-layouts: 29.4 us -> none  [kernel_tile(): delta_x = cell_xy[0][:, None] - points[0][None, :]]
    unnamed x6 -> x0, waiting for transfers between devices: 20.2 us -> none
  transfers between devices with their start and end apart: 5 -> 8, of which waited for: 3 -> 3; matrix products, arithmetic and copies ran while one was open for 35% -> 0% of each run, Pallas kernels for 0% -> 21%
where the time goes in v2:
time: 115 us
  Pallas kernels  52.6 us (46%)
  local copies, waits for them, and re-layouts  16.4 us (14%)
  blocking collectives  16 us (14%)
  waiting for transfers between devices  14.6 us (13%)
  starting transfers between devices  14 us (12%)
    pallas_call x1, Pallas kernels, forward(): pl.pallas_call(functools.partial(forward_kernel, blocks=blocks, NB=math.g...  24.1 us
    pallas_call x1, Pallas kernels, backward(): pl.pallas_call(functools.partial(backward_kernel, NB=math.gcd(cells, 256)...  19.8 us
    unnamed x37, local copies, waits for them, and re-layouts  16.1 us
    all_gather x1, blocking collectives, on_device(): gathered = lax.all_gather(inducing_term, 'gene', axis=0, tiled=True)  16 us
    ppermute x6, waiting for transfers between devices, shifted(): lax.ppermute(x, axes, [(partner(i, step, size), i) for i in range(size)])  12.6 us
    all_to_all x1, starting transfers between devices, on_device(): lax.all_to_all(partial.reshape(genes * blocks, own_q, part), every, 0, 0,...  6.15 us
    all_to_all x1, starting transfers between devices, on_device(): lax.all_to_all(send.reshape(genes * blocks, own_q, part), every, 0, 0, ti...  4.5 us
    ppermute x6, starting transfers between devices, shifted(): lax.ppermute(x, axes, [(partner(i, step, size), i) for i in range(size)])  3.3 us
  transfers between devices with their start and end apart: 8, of which 3 were waited for; matrix products, arithmetic and copies ran while one was open for 0% of the time, Pallas kernels for 21%

profile of v2, /device:TPU:0, one launch (start us, length us, event | category | flops | bytes accessed | tf_op | source)
XLA Modules:
  0.0 114.7 jit_solution(1741924228350312720)
XLA Ops:
  0.6 1.6 %locate.1.rest_0_ = f32[2,256]{1,0:T(2,128)} custom-call(s32[1,256]{1,0:T(1,128)} %bitcast.15, f32[2,512]{1,0:T(2,128)} %table_ref.1), custom_call_target="tpu_custom_call" | custom-call | tf_op jit(solution)/shard_map/locate/pallas_call | solution.py:89
  2.3 0.5 collective-permute-start
  2.7 2.5 %collective-permute-start.1 = (f32[2,256]{1,0:T(2,128)}, f32[2,256]{1,0:T(2,128)S(1)}, u32[]{:S(2)}, u32[]{:S(2)}) collective-permute-start(f32[2,256]{1,0:T(2,128)} %locate.1.rest_0_), channel_id=1, source_target_pairs={{2,0},{3,1},{0,2},{1,3},{6,4},{7,5},{4,6},{5,7},{10,8},{11,9},{8,1... | collective-permute-start | bytes 6152 | tf_op jit(solution)/shard_map/ppermute | solution.py:326
  5.2 0.1 collective-permute-start.2
  5.4 1.2 %copy-done.2 = f32[2,32,4096]{2,1,0:T(8,128)S(1)} copy-done((f32[2,32,4096]{2,1,0:T(8,128)S(1)}, f32[2,32,4096]{2,1,0:T(8,128)}, u32[]{:S(2)}) %copy-start.2) | copy-done | bytes 1048600
  6.6 0.7 copy-done.6
  7.3 1.7 %build.1.rhs_ref = bf16[4,80,4096]{2,1,0:T(8,128)(2,1)S(1)} custom-call(s32[1]{0:T(128)} %bitcast.first_ref, f32[32]{0:T(128)S(1)} %copy-done.6, f32[2,32,4096]{2,1,0:T(8,128)S(1)} %copy-done.2), custom_call_target="tpu_custom_call" | custom-call | flops 4000000000 | bytes 4000000 | tf_op jit(solution)/shard_map/build/pallas_call | solution.py:120
  8.9 1.5 %copy-done.11 = bf16[4,80,4096]{2,1,0:T(8,128)(2,1)} copy-done((bf16[4,80,4096]{2,1,0:T(8,128)(2,1)}, bf16[4,80,4096]{2,1,0:T(8,128)(2,1)S(1)}, u32[]{:S(2)}) %copy-start.11) | copy-done | bytes 2621464
  10.4 0.1 pad_add_fusion.order_ref
  10.5 0.1 copy.11.index_ref
  10.7 1.7 %copy-done.12 = bf16[4,80,4096]{2,1,0:T(8,128)(2,1)S(1)} copy-done((bf16[4,80,4096]{2,1,0:T(8,128)(2,1)S(1)}, bf16[4,80,4096]{2,1,0:T(8,128)(2,1)}, u32[]{:S(2)}) %copy-start.12) | copy-done | bytes 2621464
  12.5 24.1 %forward.1 = (f32[4,4,8,256]{3,2,1,0:T(8,128)}, bf16[4,2,1024,80]{3,2,1,0:T(8,128)(2,1)S(1)}) custom-call(s32[1]{0:T(128)} %bitcast.first_ref, s32[4]{0:T(128)S(1)} %pad_add_fusion.order_ref, f32[32]{0:T(128)S(1)} %copy-done.7, f32[32]{0:T(128)S(1)} %copy-done.8, f32[32,4096]{1,0:T(8,128)S(1)} %copy-done.3, bf16[4,80,4096]{2,1,0:T(8,128)(2,1)S(1)} %copy-done.12, ...), custom_call_target="tpu_custom_call" | custom-call | flops 24999999488 | bytes 4000000 | tf_op jit(solution)/shard_map/forward/pallas_call | solution.py:179
  36.6 1.4 %copy-done.14 = bf16[4,2,1024,80]{3,2,1,0:T(8,128)(2,1)} copy-done((bf16[4,2,1024,80]{3,2,1,0:T(8,128)(2,1)}, bf16[4,2,1024,80]{3,2,1,0:T(8,128)(2,1)S(1)}, u32[]{:S(2)}) %copy-start.14) | copy-done | bytes 1310744
  38.0 6.2 %all-to-all-start = ((f32[16,8,256]{2,1,0:T(8,128)}), f32[16,8,256]{2,1,0:T(8,128)S(1)}, u32[]{:S(2)}, u32[]{:S(2)}) async-start(f32[16,8,256]{2,1,0:T(8,128)} %bitcast.6), calls=%async_computation | async-start | bytes 262144 | tf_op jit(solution)/shard_map/all_to_all | solution.py:374
  44.2 2.2 %copy-done.1 = bf16[512,4096]{1,0:T(8,128)(2,1)S(1)} copy-done((bf16[512,4096]{1,0:T(8,128)(2,1)S(1)}, bf16[512,4096]{1,0:T(8,128)(2,1)}, u32[]{:S(2)}) %copy-start.1) | copy-done | bytes 4194328
  46.3 2.3 %observe.1.observed_ref = bf16[256,4096]{1,0:T(8,128)(2,1)S(1)} custom-call(s32[256,1]{1,0:T(8,128)S(1)} %copy.11.index_ref, bf16[512,4096]{1,0:T(8,128)(2,1)S(1)} %copy-done.1), custom_call_target="tpu_custom_call" | custom-call | flops 3000000000 | bytes 6000000 | tf_op jit(solution)/shard_map/observe/pallas_call | solution.py:265
  48.7 1.4 %copy-done.9 = bf16[256,4096]{1,0:T(8,128)(2,1)} copy-done((bf16[256,4096]{1,0:T(8,128)(2,1)}, bf16[256,4096]{1,0:T(8,128)(2,1)S(1)}, u32[]{:S(2)}) %copy-start.9) | copy-done | bytes 2097176
  50.0 2.1 %all-to-all-done = f32[16,8,256]{2,1,0:T(8,128)S(1)} async-done(((f32[16,8,256]{2,1,0:T(8,128)}), f32[16,8,256]{2,1,0:T(8,128)S(1)}, u32[]{:S(2)}, u32[]{:S(2)}) %all-to-all-start) | async-done | bytes 131104 | tf_op jit(solution)/shard_map/all_to_all | solution.py:374
  52.1 1.6 %copy-done.10 = bf16[256,4096]{1,0:T(8,128)(2,1)S(1)} copy-done((bf16[256,4096]{1,0:T(8,128)(2,1)S(1)}, bf16[256,4096]{1,0:T(8,128)(2,1)}, u32[]{:S(2)}) %copy-start.10) | copy-done | bytes 2097176
  53.7 3.1 %middle.1 = (f32[64,4096]{1,0:T(8,128)S(1)}, f32[4,4,8,256]{3,2,1,0:T(8,128)}) custom-call(f32[4,4,8,256]{3,2,1,0:T(8,128)S(1)} %bitcast.13, bf16[64,4096]{1,0:T(8,128)(2,1)S(1)} %copy-done.4, f32[1,4096]{1,0:T(1,128)S(1)} %bitcast.14, bf16[256,4096]{1,0:T(8,128)(2,1)S(1)} %copy-done.10), custom_call_target="tpu_custom_call" | custom-call | flops 3000000000 | bytes 4000000 | tf_op jit(solution)/shard_map/middle/pallas_call | solution.py:312
  56.8 0.1 collective-permute-start.3
  56.9 1.9 %collective-permute-done.3 = f32[32,4096]{1,0:T(8,128)S(1)} collective-permute-done((f32[32,4096]{1,0:T(8,128)S(1)}, f32[32,4096]{1,0:T(8,128)S(1)}, u32[]{:S(2)}, u32[]{:S(2)}) %collective-permute-start.3) | collective-permute-done | bytes 524320 | tf_op jit(solution)/shard_map/ppermute | solution.py:326
  58.8 0.1 dynamic-slice_add_fusion
  58.9 4.5 %all-to-all-start.1 = ((f32[16,8,256]{2,1,0:T(8,128)}), f32[16,8,256]{2,1,0:T(8,128)S(1)}, u32[]{:S(2)}, u32[]{:S(2)}) async-start(f32[16,8,256]{2,1,0:T(8,128)} %bitcast.10), calls=%async_computation.1 | async-start | bytes 262144 | tf_op jit(solution)/shard_map/all_to_all | solution.py:381
  63.4 10.7 %collective-permute-done.4 = f32[32,4096]{1,0:T(8,128)S(1)} collective-permute-done((f32[32,4096]{1,0:T(8,128)S(1)}, f32[32,4096]{1,0:T(8,128)S(1)}, u32[]{:S(2)}, u32[]{:S(2)}) %collective-permute-start.4) | collective-permute-done | bytes 524320 | tf_op jit(solution)/shard_map/ppermute | solution.py:326
  74.2 0.1 constant_dynamic-update-slice_fusion.1
  74.4 1.7 %copy-done.13 = bf16[4,80,4096]{2,1,0:T(8,128)(2,1)S(1)} copy-done((bf16[4,80,4096]{2,1,0:T(8,128)(2,1)S(1)}, bf16[4,80,4096]{2,1,0:T(8,128)(2,1)}, u32[]{:S(2)}) %copy-start.13) | copy-done | bytes 2621464
  76.1 1.6 %copy-done.15 = bf16[4,2,1024,80]{3,2,1,0:T(8,128)(2,1)S(1)} copy-done((bf16[4,2,1024,80]{3,2,1,0:T(8,128)(2,1)S(1)}, bf16[4,2,1024,80]{3,2,1,0:T(8,128)(2,1)}, u32[]{:S(2)}) %copy-start.15) | copy-done | bytes 1310744
  77.7 19.8 %backward.1 = f32[8,4096]{1,0:T(8,128)S(1)} custom-call(s32[1]{0:T(128)} %bitcast.first_ref, s32[4]{0:T(128)S(1)} %pad_add_fusion.order_ref, f32[32]{0:T(128)S(1)} %copy-done.8, f32[4,4,8,256]{3,2,1,0:T(8,128)S(1)} %bitcast.12, bf16[4,80,4096]{2,1,0:T(8,128)(2,1)S(1)} %copy-done.13, bf16[4,2,1024,80]{3,2,1,0:T(8,128)(2,1)S(1)} %copy-done.15), custom_call_target="tpu_custom_call" | custom-call | flops 24999999488 | bytes 4000000 | tf_op jit(solution)/shard_map/backward/pallas_call | solution.py:233
  97.6 16.0 %all_gather.3 = f32[32,4096]{1,0:T(8,128)S(1)} all-gather(f32[8,4096]{1,0:T(8,128)S(1)} %backward.1), channel_id=1, replica_groups=mesh['group'=2,'gene'=4,'lat'=2,'sub'=2] {'gene'}, dimensions={0}, use_global_device_ids=true | all-gather | bytes 655360 | tf_op jit(solution)/shard_map/all_gather | solution.py:385
  113.6 0.8 copy.15
  114.4 0.3 copy-done.16
  (35 shorter events, 0.3 us)
Async XLA Ops:
  2.3 8.4 %collective-permute-start = (f32[2,256]{1,0:T(2,128)}, f32[2,256]{1,0:T(2,128)S(1)}, u32[]{:S(2)}, u32[]{:S(2)}) collective-permute-start(f32[2,256]{1,0:T(2,128)} %locate.1.rest_0_), channel_id=1, source_target_pairs={{1,0},{0,1},{3,2},{2,3},{5,4},{4,5},{7,6},{6,7},{9,8},{8,9},{11,10... | collective-permute-start | bytes 6152 | tf_op jit(solution)/shard_map/ppermute | solution.py:326
  2.7 8.0 %collective-permute-start.1 = (f32[2,256]{1,0:T(2,128)}, f32[2,256]{1,0:T(2,128)S(1)}, u32[]{:S(2)}, u32[]{:S(2)}) collective-permute-start(f32[2,256]{1,0:T(2,128)} %locate.1.rest_0_), channel_id=1, source_target_pairs={{2,0},{3,1},{0,2},{1,3},{6,4},{7,5},{4,6},{5,7},{10,8},{11,9},{8,1... | collective-permute-start | bytes 6152 | tf_op jit(solution)/shard_map/ppermute | solution.py:326
  5.2 5.5 %collective-permute-start.2 = (f32[2,256]{1,0:T(2,128)}, f32[2,256]{1,0:T(2,128)S(1)}, u32[]{:S(2)}, u32[]{:S(2)}) collective-permute-start(f32[2,256]{1,0:T(2,128)} %locate.1.rest_0_), channel_id=1, source_target_pairs={{3,0},{2,1},{1,2},{0,3},{7,4},{6,5},{5,6},{4,7},{11,8},{10,9},{9,1... | collective-permute-start | bytes 6152 | tf_op jit(solution)/shard_map/ppermute | solution.py:326
  5.3 1.2 %copy-start.2 = (f32[2,32,4096]{2,1,0:T(8,128)S(1)}, f32[2,32,4096]{2,1,0:T(8,128)}, u32[]{:S(2)}) copy-start(f32[2,32,4096]{2,1,0:T(8,128)} %points_ref.1) | copy-start | bytes 3145732
  6.6 0.7 copy-start.6
  7.2 3.3 %copy-start.17 = (s32[256]{0:T(256)S(1)}, s32[256]{0:T(256)}, u32[]{:S(2)}) copy-start(s32[256]{0:T(256)} %param.9) | copy-start | bytes 3076
  7.2 3.5 %copy-start = (f32[2,256]{1,0:T(2,128)S(1)}, f32[2,256]{1,0:T(2,128)}, u32[]{:S(2)}) copy-start(f32[2,256]{1,0:T(2,128)} %locate.1.rest_0_) | copy-start | bytes 6148
  7.2 3.5 %copy-start.3 = (f32[32,4096]{1,0:T(8,128)S(1)}, f32[32,4096]{1,0:T(8,128)}, u32[]{:S(2)}) copy-start(f32[32,4096]{1,0:T(8,128)} %weight_ref.1) | copy-start | bytes 1572868
  7.2 3.5 %copy-start.7 = (f32[32]{0:T(128)S(1)}, f32[32]{0:T(128)}, u32[]{:S(2)}) copy-start(f32[32]{0:T(128)} %length_ref.3) | copy-start | bytes 388
  7.2 3.5 %copy-start.8 = (f32[32]{0:T(128)S(1)}, f32[32]{0:T(128)}, u32[]{:S(2)}) copy-start(f32[32]{0:T(128)} %var_ref.3) | copy-start | bytes 388
  8.9 1.5 %copy-start.11 = (bf16[4,80,4096]{2,1,0:T(8,128)(2,1)}, bf16[4,80,4096]{2,1,0:T(8,128)(2,1)S(1)}, u32[]{:S(2)}) copy-start(bf16[4,80,4096]{2,1,0:T(8,128)(2,1)S(1)} %build.1.rhs_ref) | copy-start | bytes 7864324
  10.7 1.7 %copy-start.12 = (bf16[4,80,4096]{2,1,0:T(8,128)(2,1)S(1)}, bf16[4,80,4096]{2,1,0:T(8,128)(2,1)}, u32[]{:S(2)}) copy-start(bf16[4,80,4096]{2,1,0:T(8,128)(2,1)} %copy-done.11) | copy-start | bytes 7864324
  36.6 1.4 %copy-start.14 = (bf16[4,2,1024,80]{3,2,1,0:T(8,128)(2,1)}, bf16[4,2,1024,80]{3,2,1,0:T(8,128)(2,1)S(1)}, u32[]{:S(2)}) copy-start(bf16[4,2,1024,80]{3,2,1,0:T(8,128)(2,1)S(1)} %get-tuple-element.13.lhs_ref) | copy-start | bytes 3932164
  38.0 14.1 %all-to-all-start = ((f32[16,8,256]{2,1,0:T(8,128)}), f32[16,8,256]{2,1,0:T(8,128)S(1)}, u32[]{:S(2)}, u32[]{:S(2)}) async-start(f32[16,8,256]{2,1,0:T(8,128)} %bitcast.6), calls=%async_computation | async-start | bytes 262144 | tf_op jit(solution)/shard_map/all_to_all | solution.py:374
  44.2 2.2 %copy-start.1 = (bf16[512,4096]{1,0:T(8,128)(2,1)S(1)}, bf16[512,4096]{1,0:T(8,128)(2,1)}, u32[]{:S(2)}) copy-start(bf16[512,4096]{1,0:T(8,128)(2,1)} %expr_ref) | copy-start | bytes 12582916
  46.3 5.7 %copy-start.4 = (bf16[64,4096]{1,0:T(8,128)(2,1)S(1)}, bf16[64,4096]{1,0:T(8,128)(2,1)}, u32[]{:S(2)}) copy-start(bf16[64,4096]{1,0:T(8,128)(2,1)} %mixing_ref.1) | copy-start | bytes 1572868
  46.3 5.7 %copy-start.5 = (f32[4096]{0:T(1024)S(1)}, f32[4096]{0:T(1024)}, u32[]{:S(2)}) copy-start(f32[4096]{0:T(1024)} %param.17) | copy-start | bytes 49156
  48.7 1.4 %copy-start.9 = (bf16[256,4096]{1,0:T(8,128)(2,1)}, bf16[256,4096]{1,0:T(8,128)(2,1)S(1)}, u32[]{:S(2)}) copy-start(bf16[256,4096]{1,0:T(8,128)(2,1)S(1)} %observe.1.observed_ref) | copy-start | bytes 6291460
  52.1 1.6 %copy-start.10 = (bf16[256,4096]{1,0:T(8,128)(2,1)S(1)}, bf16[256,4096]{1,0:T(8,128)(2,1)}, u32[]{:S(2)}) copy-start(bf16[256,4096]{1,0:T(8,128)(2,1)} %copy-done.9) | copy-start | bytes 6291460
  56.8 2.0 %collective-permute-start.3 = (f32[32,4096]{1,0:T(8,128)S(1)}, f32[32,4096]{1,0:T(8,128)S(1)}, u32[]{:S(2)}, u32[]{:S(2)}) collective-permute-start(f32[32,4096]{1,0:T(8,128)S(1)} %constant_dynamic-slice_fusion), channel_id=1, source_target_pairs={{1,0},{0,1},{3,2},{2,3},{5,4},{4,5},{7,6},{6,7},{9,8},{8,9},{11,10... | collective-permute-start | bytes 1572872 | tf_op jit(solution)/shard_map/ppermute | solution.py:326
  58.8 15.3 %collective-permute-start.4 = (f32[32,4096]{1,0:T(8,128)S(1)}, f32[32,4096]{1,0:T(8,128)S(1)}, u32[]{:S(2)}, u32[]{:S(2)}) collective-permute-start(f32[32,4096]{1,0:T(8,128)S(1)} %dynamic-slice_add_fusion), channel_id=1, source_target_pairs={{2,0},{0,2},{3,1},{1,3},{6,4},{4,6},{7,5},{5,7},{10,8},{8,10},{11,... | collective-permute-start | bytes 1572872 | tf_op jit(solution)/shard_map/ppermute | solution.py:326
  58.9 15.4 %all-to-all-start.1 = ((f32[16,8,256]{2,1,0:T(8,128)}), f32[16,8,256]{2,1,0:T(8,128)S(1)}, u32[]{:S(2)}, u32[]{:S(2)}) async-start(f32[16,8,256]{2,1,0:T(8,128)} %bitcast.10), calls=%async_computation.1 | async-start | bytes 262144 | tf_op jit(solution)/shard_map/all_to_all | solution.py:381
  74.3 39.2 %collective-permute-start.5 = (f32[32,4096]{1,0:T(8,128)S(1)}, f32[32,4096]{1,0:T(8,128)S(1)}, u32[]{:S(2)}, u32[]{:S(2)}) collective-permute-start(f32[32,4096]{1,0:T(8,128)S(1)} %get-tuple-element.15), channel_id=1, source_target_pairs={{1,0},{0,1},{3,2},{2,3},{5,4},{4,5},{7,6},{6,7},{9,8},{8,9},{11,10... | collective-permute-start | bytes 1572872 | tf_op jit(solution)/shard_map/ppermute | solution.py:326
  74.4 1.7 %copy-start.13 = (bf16[4,80,4096]{2,1,0:T(8,128)(2,1)S(1)}, bf16[4,80,4096]{2,1,0:T(8,128)(2,1)}, u32[]{:S(2)}) copy-start(bf16[4,80,4096]{2,1,0:T(8,128)(2,1)} %copy-done.11) | copy-start | bytes 7864324
  76.1 1.6 %copy-start.15 = (bf16[4,2,1024,80]{3,2,1,0:T(8,128)(2,1)S(1)}, bf16[4,2,1024,80]{3,2,1,0:T(8,128)(2,1)}, u32[]{:S(2)}) copy-start(bf16[4,2,1024,80]{3,2,1,0:T(8,128)(2,1)} %copy-done.14) | copy-start | bytes 3932164
  113.6 1.1 copy-start.16

commit v3 on v2

--- a/solution.py
+++ b/solution.py
@@ -9,6 +9,7 @@
 from jax.sharding import PartitionSpec as P
 
 LOG2E = math.log2(math.e)
+ROOM = 24 << 20
 
 def row_of(shape):
     return lax.broadcasted_iota(jnp.int32, shape, 0)
@@ -120,10 +121,10 @@
     return pl.pallas_call(
         build_kernel,
         grid=(own_q // 2,),
-        out_shape=jax.ShapeDtypeStruct((own_q // 2, 80, count), jnp.bfloat16),
+        out_shape=pltpu.HBM((own_q // 2, 80, count), jnp.bfloat16),
         in_specs=[whole(SMEM), whole(SMEM), whole(VMEM)],
         out_specs=pl.BlockSpec((1, 80, count), lambda i: (i, 0, 0)),
-        compiler_params=pltpu.CompilerParams(vmem_limit_bytes=16 << 20),
+        compiler_params=pltpu.CompilerParams(vmem_limit_bytes=ROOM),
         cost_estimate=pl.CostEstimate(flops=4_000_000_000, bytes_accessed=4_000_000, transcendentals=0),
         name="build",
     )(first, lengths, points)
@@ -155,12 +156,21 @@
                 for c in range(SB // 128):
                     total = total + e[:, c * 128 : (c + 1) * 128] * weight[:, c * 128 : (c + 1) * 128]
             acc[rows, :] = total
-        result = lax.dot_general(
-            jnp.ones((8, 128), jnp.float32),
-            acc[...],
-            (((1,), (1,)), ((), ())),
-            precision=lax.Precision.HIGHEST,
-            preferred_element_type=jnp.float32,
+        high = acc[...].astype(jnp.bfloat16)
+        rest = acc[...] - high.astype(jnp.float32)
+        middle = rest.astype(jnp.bfloat16)
+        low = (rest - middle.astype(jnp.float32)).astype(jnp.bfloat16)
+        result = functools.reduce(
+            jnp.add,
+            [
+                lax.dot_general(
+                    jnp.ones((8, 128), jnp.bfloat16),
+                    term,
+                    (((1,), (1,)), ((), ())),
+                    preferred_element_type=jnp.float32,
+                )
+                for term in (high, middle, low)
+            ],
         )
         result = result[0:1] * var_ref[q + k]
         for b in range(blocks):
@@ -177,21 +187,21 @@
     part = xys[0].shape[1]
     cells = blocks * part
     return pl.pallas_call(
-        functools.partial(forward_kernel, blocks=blocks, NB=math.gcd(cells, 256), SB=math.gcd(points, 512)),
+        functools.partial(forward_kernel, blocks=blocks, NB=math.gcd(cells, 256), SB=points),
         grid=(own_q // 2,),
         out_shape=(
             jax.ShapeDtypeStruct((copies, blocks, own_q, part), jnp.float32),
-            jax.ShapeDtypeStruct((own_q // 2, 2, cells, 80), jnp.bfloat16),
+            pltpu.HBM((own_q // 2, 2, cells, 80), jnp.bfloat16),
         ),
         in_specs=[whole(SMEM)] * 4
         + [whole(VMEM), pl.BlockSpec((1, 80, points), lambda i: (i, 0, 0))]
         + [whole(VMEM)] * blocks,
         out_specs=(whole(VMEM), pl.BlockSpec((1, 2, cells, 80), lambda i: (i, 0, 0, 0))),
         scratch_shapes=[VMEM((cells, 128), jnp.float32)],
-        compiler_params=pltpu.CompilerParams(vmem_limit_bytes=24 << 20),
+        compiler_params=pltpu.CompilerParams(vmem_limit_bytes=ROOM),
         cost_estimate=pl.CostEstimate(flops=25_000_000_000, bytes_accessed=4_000_000, transcendentals=0),
         name="forward",
-    )(first, order, lengths, var, weights, rhs, *xys)
+    )(first, order, lengths, var, weights, pltpu.with_memory_space_constraint(rhs, pltpu.HBM), *xys)
 
 
 def backward_kernel(first_ref, order_ref, var_ref, grad_ref, rhs_ref, lhs_ref, out_ref, held, spread, *, NB):
@@ -242,57 +252,81 @@
         ],
         out_specs=whole(VMEM),
         scratch_shapes=[VMEM((blocks, own_q, part), jnp.float32), VMEM((cells, 128), jnp.float32)],
-        compiler_params=pltpu.CompilerParams(vmem_limit_bytes=24 << 20),
+        compiler_params=pltpu.CompilerParams(vmem_limit_bytes=ROOM),
         cost_estimate=pl.CostEstimate(flops=25_000_000_000, bytes_accessed=4_000_000, transcendentals=0),
         name="backward",
-    )(first, order, var, grads, rhs, lhs)
-
-
-def observe_kernel(index_ref, expr_ref, out_ref, hot):
-    @pl.when(pl.program_id(0) == 0)
-    def _():
-        rows = lax.broadcasted_iota(jnp.int32, hot.shape, 1)
-        hot[...] = jnp.where(rows == index_ref[...], 1.0, 0.0).astype(jnp.bfloat16)
-
-    picked = jnp.dot(hot[...], expr_ref[...], preferred_element_type=jnp.float32)
-    out_ref[...] = picked.astype(jnp.bfloat16)
+    )(first, order, var, grads, *(pltpu.with_memory_space_constraint(x, pltpu.HBM) for x in (rhs, lhs)))
+
+
+def observe_kernel(index_ref, expr_hbm, out_hbm, expr_ref, out_ref, load_sem, store_sem):
+    rows, genes = expr_ref.shape
+    count, cells, width = out_ref.shape
+    columns = [slice(j * width, (j + 1) * width) for j in range(genes // width)]
+    loads = [
+        pltpu.make_async_copy(expr_hbm.at[:, s], expr_ref.at[:, s], load_sem.at[j]) for j, s in enumerate(columns)
+    ]
+    for copy in loads:
+        copy.start()
+    places = lax.broadcasted_iota(jnp.int32, (cells, rows), 1)
+    hot = jnp.where(places == index_ref[...], 1.0, 0.0).astype(jnp.bfloat16)
+    stores = []
+    for j, s in enumerate(columns):
+        loads[j].wait()
+        out_ref[j] = jnp.dot(hot, expr_ref[:, s], preferred_element_type=jnp.float32).astype(jnp.bfloat16)
+        copy = pltpu.make_async_copy(out_ref.at[j], out_hbm.at[j], store_sem.at[j])
+        copy.start()
+        stores.append(copy)
+    for copy in stores:
+        copy.wait()
 
 
 def observe(index, expr):
     rows, genes = expr.shape
     cells = index.shape[0]
-    width = math.gcd(genes, 1024)
+    width = math.gcd(genes, 512)
+    count = genes // width
     return pl.pallas_call(
         observe_kernel,
-        grid=(genes // width,),
-        out_shape=jax.ShapeDtypeStruct((cells, genes), jnp.bfloat16),
-        in_specs=[pl.BlockSpec((cells, 1), lambda i: (0, 0)), pl.BlockSpec((rows, width), lambda i: (0, i))],
-        out_specs=pl.BlockSpec((cells, width), lambda i: (0, i)),
-        scratch_shapes=[VMEM((cells, rows), jnp.bfloat16)],
-        compiler_params=pltpu.CompilerParams(vmem_limit_bytes=16 << 20),
+        out_shape=pltpu.HBM((count, cells, width), jnp.bfloat16),
+        in_specs=[whole(VMEM), whole(pltpu.HBM)],
+        out_specs=whole(pltpu.HBM),
+        scratch_shapes=[
+            VMEM((rows, genes), jnp.bfloat16),
+            VMEM((count, cells, width), jnp.bfloat16),
+            pltpu.SemaphoreType.DMA((count,)),
+            pltpu.SemaphoreType.DMA((count,)),
+        ],
+        compiler_params=pltpu.CompilerParams(vmem_limit_bytes=ROOM),
         cost_estimate=pl.CostEstimate(flops=3_000_000_000, bytes_accessed=6_000_000, transcendentals=0),
         name="observe",
-    )(index[:, None], expr)
-
-
-def middle_kernel(piece_ref, mixing_ref, noise_ref, observed_ref, grad_ref, send_ref, wide, *, scale, cuts, width):
+    )(index[:, None], pltpu.with_memory_space_constraint(expr, pltpu.HBM))
+
+
+def middle_kernel(rows_ref, piece_ref, mixing_ref, noise_ref, observed_ref, *rest, scale, cuts, shares):
+    grad_refs, (send_ref, wide, latent) = rest[:shares], rest[shares:]
     latent_cuts, cell_cuts, lats, subs = cuts
     own_q, part = piece_ref.shape[2:]
+    count, _, width = observed_ref.shape
+    share = mixing_ref.shape[0] // shares
     for lat in range(lats):
         for a in range(latent_cuts):
             for b in range(cell_cuts):
                 pieces = [piece_ref[a * cell_cuts + b, lat * subs + sub] for sub in range(subs)]
                 first = (lat * latent_cuts + a) * own_q
                 wide[first : first + own_q, b * part : (b + 1) * part] = functools.reduce(jnp.add, pieces)
-    latent = wide[...].astype(jnp.bfloat16)
+    latent[...] = wide[...].astype(jnp.bfloat16)
     turned = wide[...].T.astype(jnp.bfloat16)
+    halves = [latent[pl.ds(pl.multiple_of(rows_ref[i] * share, share), share), :] for i in range(shares)]
+    ordered = jnp.concatenate(halves, 0)
     total = jnp.zeros(latent.shape, jnp.float32)
-    for j in range(mixing_ref.shape[1] // width):
+    for j in range(count):
         s = slice(j * width, (j + 1) * width)
         predicted = jnp.dot(turned, mixing_ref[:, s], preferred_element_type=jnp.float32)
-        observed = observed_ref[:, s].astype(jnp.float32)
+        observed = observed_ref[j].astype(jnp.float32)
         weighted = (noise_ref[:, s] * (observed - predicted)).astype(jnp.bfloat16)
-        grad_ref[:, s] = scale * jnp.dot(latent, weighted, preferred_element_type=jnp.float32)
+        grads = scale * jnp.dot(ordered, weighted, preferred_element_type=jnp.float32)
+        for i in range(shares):
+            grad_refs[i][:, s] = grads[i * share : (i + 1) * share]
         total = total + lax.dot_general(
             mixing_ref[:, s], weighted, (((1,), (1,)), ((), ())), preferred_element_type=jnp.float32
         )
@@ -306,45 +340,43 @@
                     send_ref[a * cell_cuts + b, lat * subs + sub] = piece
 
 
-def middle(pieces, mixing, noise, observed, scale, cuts):
-    cells, genes = observed.shape
-    q = mixing.shape[0]
-    return pl.pallas_call(
-        functools.partial(middle_kernel, scale=scale, cuts=cuts, width=math.gcd(genes, 512)),
-        out_shape=(
-            jax.ShapeDtypeStruct((q, genes), jnp.float32),
-            jax.ShapeDtypeStruct(pieces.shape, jnp.float32),
-        ),
-        scratch_shapes=[VMEM((q, cells), jnp.float32)],
-        compiler_params=pltpu.CompilerParams(vmem_limit_bytes=24 << 20),
+def middle(rows, pieces, mixing, noise, observed, scale, cuts):
+    count, cells, width = observed.shape
+    q, genes = mixing.shape
+    shares = rows.shape[0]
+    return pl.pallas_call(
+        functools.partial(middle_kernel, scale=scale, cuts=cuts, shares=shares),
+        out_shape=(jax.ShapeDtypeStruct((q // shares, genes), jnp.float32),) * shares
+        + (jax.ShapeDtypeStruct(pieces.shape, jnp.float32),),
+        in_specs=[whole(SMEM)] + [whole(VMEM)] * 4,
+        out_specs=(whole(VMEM),) * (shares + 1),
+        scratch_shapes=[
+            VMEM((q, cells), jnp.float32),
+            VMEM((q, cells), jnp.bfloat16),
+        ],
+        compiler_params=pltpu.CompilerParams(vmem_limit_bytes=ROOM),
         cost_estimate=pl.CostEstimate(flops=3_000_000_000, bytes_accessed=4_000_000, transcendentals=0),
         name="middle",
-    )(pieces, mixing, noise[None, :], observed)
+    )(
+        rows,
+        pieces,
+        mixing,
+        noise[None, :],
+        observed,
+    )
 
 
 def shifted(x, axes, step, size):
     return lax.ppermute(x, axes, [(partner(i, step, size), i) for i in range(size)])
 
 
-def sum_over(x, first_axis, then_axis):
-    n = lax.axis_size(first_axis)
-    m = lax.axis_size(then_axis)
-    me = lax.axis_index(first_axis)
-    rows = x.shape[0] // n
-
-    def rows_of(place):
-        return lax.dynamic_slice_in_dim(x, place * rows, rows, 0)
-
-    total = rows_of(me)
+def gather_rows(x, axis):
+    n = lax.axis_size(axis)
+    me = lax.axis_index(axis)
+    rows = x.shape[0]
+    out = lax.dynamic_update_slice_in_dim(jnp.zeros((n * rows, x.shape[1]), x.dtype), x, me * rows, 0)
     for step in range(1, n):
-        to = me ^ step if n & (n - 1) == 0 else (me - step) % n
-        total = total + shifted(rows_of(to), first_axis, step, n)
-    total = functools.reduce(jnp.add, [total] + [shifted(total, then_axis, step, m) for step in range(1, m)])
-    out = lax.dynamic_update_slice_in_dim(jnp.zeros_like(x), total, me * rows, 0)
-    for step in range(1, n):
-        out = lax.dynamic_update_slice_in_dim(
-            out, shifted(total, first_axis, step, n), partner(me, step, n) * rows, 0
-        )
+        out = lax.dynamic_update_slice_in_dim(out, shifted(x, axis, step, n), partner(me, step, n) * rows, 0)
     return out
 
 
@@ -370,18 +402,25 @@
     rhs = build(first, lengthscale, inducing, own_q)
 
     partial, lhs = forward(first, order, lengthscale, variance, ind_weights, rhs, xys, own_q, genes)
-    expr_table, partial = lax.optimization_barrier((expr_table, partial))
+    late_index, partial = lax.optimization_barrier((cell_index, partial))
     pieces = lax.all_to_all(partial.reshape(genes * blocks, own_q, part), every, 0, 0, tiled=True)
-    observed = observe(cell_index, expr_table)
+    observed = observe(late_index, expr_table)
 
     grad_scale = -1.0 / math.sqrt(cells * blocks)
-    mixing_term, send = middle(
-        pieces.reshape(genes, blocks, own_q, part), mixing, noise_prec, observed, grad_scale, cuts
+    sub = lax.axis_index("sub")
+    rows = [sub ^ step if subs & (subs - 1) == 0 else (sub - step) % subs for step in range(subs)]
+    *terms, send = middle(
+        jnp.stack(rows), pieces.reshape(genes, blocks, own_q, part), mixing, noise_prec, observed, grad_scale, cuts
     )
     pieces = lax.all_to_all(send.reshape(genes * blocks, own_q, part), every, 0, 0, tiled=True)
-    grad_mixing = sum_over(mixing_term, "sub", "lat")
+    half = functools.reduce(
+        jnp.add, [terms[0]] + [shifted(terms[step], "sub", step, subs) for step in range(1, subs)]
+    )
+    others = [shifted(half, "lat", step, lats) for step in range(1, lats)]
 
     inducing_term = backward(first, order, variance, pieces.reshape(genes, blocks, own_q, part), rhs, lhs)
+    inducing_term, *others = lax.optimization_barrier((inducing_term, *others))
+    grad_mixing = gather_rows(functools.reduce(jnp.add, others, half), "sub")
     gathered = lax.all_gather(inducing_term, "gene", axis=0, tiled=True)
     grad_inducing = gathered.reshape(latent_cuts, cell_cuts, own_q, points).sum(1)
     return (grad_mixing, grad_inducing.reshape(local_q, points))

time: 115 us -> 104 us (0.904)
  local copies, waits for them, and re-layouts: 16.4 us -> 4.87 us
  waiting for transfers between devices: 14.6 us -> 9.48 us
  Pallas kernels: 52.6 us -> 57.2 us
    ppermute x6, waiting for transfers between devices: 12.6 us -> 0.02 us  [shifted(): lax.ppermute(x, axes, [(partner(i, step, size), i) for i in range(size)])]
    unnamed x37 -> x21, local copies, waits for them, and re-layouts: 16.1 us -> 4.64 us
    all_to_all x1, waiting for transfers between devices: 0.01 us -> 5.95 us  [on_device(): lax.all_to_all(send.reshape(genes * blocks, own_q, part), every, 0, 0, ti...]
    pallas_call x3, Pallas kernels: 7.03 us -> 11.1 us  [the longest x1 4.39 us: observe(): pl.pallas_call(observe_kernel, out_shape=pltpu.HBM((count, cells, width),...]
    ppermute x6, starting transfers between devices: 3.3 us -> 5.03 us  [shifted(): lax.ppermute(x, axes, [(partner(i, step, size), i) for i in range(size)])]
    all_to_all x1, waiting for transfers between devices: 2.06 us -> 3.51 us  [on_device(): lax.all_to_all(partial.reshape(genes * blocks, own_q, part), every, 0, 0,...]
  transfers between devices with their start and end apart: 8 -> 8, of which waited for: 3 -> 2; matrix products, arithmetic and copies ran while one was open for 0% -> 0% of each run, Pallas kernels for 21% -> 27%
where the time goes in v3:
time: 104 us; the launch traced here: 103 us
  Pallas kernels  57.2 us (55%)
  blocking collectives  16.2 us (16%)
  starting transfers between devices  14.7 us (14%)
  waiting for transfers between devices  9.48 us (9%)
  local copies, waits for them, and re-layouts  4.87 us (5%)
    pallas_call x1, Pallas kernels, forward(): pl.pallas_call(functools.partial(forward_kernel, blocks=blocks, NB=math.g...  23.9 us
    pallas_call x1, Pallas kernels, backward(): pl.pallas_call(functools.partial(backward_kernel, NB=math.gcd(cells, 256)...  20.6 us
    all_gather x1, blocking collectives, on_device(): gathered = lax.all_gather(inducing_term, 'gene', axis=0, tiled=True)  16.2 us
    all_to_all x1, starting transfers between devices, on_device(): lax.all_to_all(partial.reshape(genes * blocks, own_q, part), every, 0, 0,...  6.14 us
    all_to_all x1, waiting for transfers between devices, on_device(): lax.all_to_all(send.reshape(genes * blocks, own_q, part), every, 0, 0, ti...  5.95 us
    ppermute x6, starting transfers between devices, shifted(): lax.ppermute(x, axes, [(partner(i, step, size), i) for i in range(size)])  5.03 us
    unnamed x21, local copies, waits for them, and re-layouts  4.64 us
    pallas_call x1, Pallas kernels, observe(): pl.pallas_call(observe_kernel, out_shape=pltpu.HBM((count, cells, width),...  4.39 us
  transfers between devices with their start and end apart: 8, of which 2 were waited for; matrix products, arithmetic and copies ran while one was open for 0% of the time, Pallas kernels for 27%

profile of v3, /device:TPU:0, one launch (start us, length us, event | category | flops | bytes accessed | tf_op | source)
XLA Modules:
  0.0 103.5 jit_solution(7805511736207615011)
XLA Ops:
  0.6 1.6 %locate.1.rest_0_ = f32[2,256]{1,0:T(2,128)} custom-call(s32[1,256]{1,0:T(1,128)} %bitcast.17, f32[2,512]{1,0:T(2,128)} %table_ref.1), custom_call_target="tpu_custom_call" | custom-call | tf_op jit(solution)/shard_map/locate/pallas_call | solution.py:90
  2.3 0.5 collective-permute-start
  2.7 2.5 %collective-permute-start.1 = (f32[2,256]{1,0:T(2,128)}, f32[2,256]{1,0:T(2,128)S(1)}, u32[]{:S(2)}, u32[]{:S(2)}) collective-permute-start(f32[2,256]{1,0:T(2,128)} %locate.1.rest_0_), channel_id=1, source_target_pairs={{2,0},{3,1},{0,2},{1,3},{6,4},{7,5},{4,6},{5,7},{10,8},{11,9},{8,1... | collective-permute-start | bytes 6152 | tf_op jit(solution)/shard_map/ppermute | solution.py:370
  5.2 0.1 collective-permute-start.2
  5.3 0.1 pad_add_fusion.rows_ref
  5.4 1.2 %copy-done.1 = f32[2,32,4096]{2,1,0:T(8,128)S(1)} copy-done((f32[2,32,4096]{2,1,0:T(8,128)S(1)}, f32[2,32,4096]{2,1,0:T(8,128)}, u32[]{:S(2)}) %copy-start.1) | copy-done | bytes 1048600
  6.7 0.7 copy-done.5
  7.3 3.1 %build.1.rhs_ref = bf16[4,80,4096]{2,1,0:T(8,128)(2,1)} custom-call(s32[1]{0:T(128)} %bitcast.2.first_ref, f32[32]{0:T(128)S(1)} %copy-done.5, f32[2,32,4096]{2,1,0:T(8,128)S(1)} %copy-done.1), custom_call_target="tpu_custom_call" | custom-call | flops 4000000000 | bytes 4000000 | tf_op jit(solution)/shard_map/build/pallas_call | solution.py:121
  10.4 0.1 pad_add_fusion.1.order_ref
  10.5 0.0 collective-permute-done.2.rest_3_
  10.5 23.9 %forward.1 = (f32[4,4,8,256]{3,2,1,0:T(8,128)}, bf16[4,2,1024,80]{3,2,1,0:T(8,128)(2,1)}) custom-call(s32[1]{0:T(128)} %bitcast.2.first_ref, s32[4]{0:T(128)S(1)} %pad_add_fusion.1.order_ref, f32[32]{0:T(128)S(1)} %copy-done.5, f32[32]{0:T(128)S(1)} %copy-done.6, f32[32,4096]{1,0:T(8,128)S(1)} %copy-done.2, bf16[4,80,4096]{2,1,0:T(8,128)(2,1)} %build.1.rhs_ref, ...), custom_call_target="tpu_custom_call" | custom-call | flops 24999999488 | bytes 4000000 | tf_op jit(solution)/shard_map/forward/pallas_call | solution.py:189
  34.4 0.1 copy.11.index_ref
  34.5 6.1 %all-to-all-start = ((f32[16,8,256]{2,1,0:T(8,128)}), f32[16,8,256]{2,1,0:T(8,128)S(1)}, u32[]{:S(2)}, u32[]{:S(2)}) async-start(f32[16,8,256]{2,1,0:T(8,128)} %bitcast.8), calls=%async_computation | async-start | bytes 262144 | tf_op jit(solution)/shard_map/all_to_all | solution.py:406
  40.7 0.0 copy-start.3
  40.7 0.0 copy-start.4
  40.7 4.4 %observe.1.observed_ref = bf16[8,256,512]{2,1,0:T(8,128)(2,1)} custom-call(s32[256,1]{1,0:T(8,128)S(1)} %copy.11.index_ref, bf16[512,4096]{1,0:T(8,128)(2,1)} %expr_hbm.1), custom_call_target="tpu_custom_call" | custom-call | flops 3000000000 | bytes 6000000 | tf_op jit(solution)/shard_map/observe/pallas_call | solution.py:288
  45.1 3.5 %all-to-all-done = f32[16,8,256]{2,1,0:T(8,128)S(1)} async-done(((f32[16,8,256]{2,1,0:T(8,128)}), f32[16,8,256]{2,1,0:T(8,128)S(1)}, u32[]{:S(2)}, u32[]{:S(2)}) %all-to-all-start) | async-done | bytes 131104 | tf_op jit(solution)/shard_map/all_to_all | solution.py:406
  48.6 1.6 %copy-done.7 = bf16[8,256,512]{2,1,0:T(8,128)(2,1)S(1)} copy-done((bf16[8,256,512]{2,1,0:T(8,128)(2,1)S(1)}, bf16[8,256,512]{2,1,0:T(8,128)(2,1)}, u32[]{:S(2)}) %copy-start.7) | copy-done | bytes 2097176
  50.2 3.6 %middle.1 = (f32[32,4096]{1,0:T(8,128)S(1)}, f32[32,4096]{1,0:T(8,128)S(1)}, f32[4,4,8,256]{3,2,1,0:T(8,128)}) custom-call(s32[2]{0:T(128)S(1)} %pad_add_fusion.rows_ref, f32[4,4,8,256]{3,2,1,0:T(8,128)S(1)} %bitcast.15, bf16[64,4096]{1,0:T(8,128)(2,1)S(1)} %copy-done.3, f32[1,4096]{1,0:T(1,128)S(1)} %bitcast.16, bf16[8,256,512]{2,1,0:T(8,128)(2,1)S(1)} %copy-done.7), custom_call_target="tpu_custom_call" | custom-call | flops 3000000000 | bytes 4000000 | tf_op jit(solution)/shard_map/middle/pallas_call | solution.py:347
  53.8 3.5 %all-to-all-start.1 = ((f32[16,8,256]{2,1,0:T(8,128)}), f32[16,8,256]{2,1,0:T(8,128)S(1)}, u32[]{:S(2)}, u32[]{:S(2)}) async-start(f32[16,8,256]{2,1,0:T(8,128)} %bitcast.12), calls=%async_computation.1 | async-start | bytes 262144 | tf_op jit(solution)/shard_map/all_to_all | solution.py:415
  57.4 0.0 collective-permute-done.3
  57.4 0.1 add.26
  57.4 1.9 %collective-permute-start.4 = (f32[32,4096]{1,0:T(8,128)S(1)}, f32[32,4096]{1,0:T(8,128)S(1)}, u32[]{:S(2)}, u32[]{:S(2)}) collective-permute-start(f32[32,4096]{1,0:T(8,128)S(1)} %add.26), channel_id=1, source_target_pairs={{2,0},{0,2},{3,1},{1,3},{6,4},{4,6},{7,5},{5,7},{10,8},{8,10},{11,... | collective-permute-start | bytes 1572872 | tf_op jit(solution)/shard_map/ppermute | solution.py:370
  59.3 6.0 %all-to-all-done.1 = f32[16,8,256]{2,1,0:T(8,128)S(1)} async-done(((f32[16,8,256]{2,1,0:T(8,128)}), f32[16,8,256]{2,1,0:T(8,128)S(1)}, u32[]{:S(2)}, u32[]{:S(2)}) %all-to-all-start.1) | async-done | bytes 131104 | tf_op jit(solution)/shard_map/all_to_all | solution.py:415
  65.3 20.6 %backward.1 = f32[8,4096]{1,0:T(8,128)S(1)} custom-call(s32[1]{0:T(128)} %bitcast.2.first_ref, s32[4]{0:T(128)S(1)} %pad_add_fusion.1.order_ref, f32[32]{0:T(128)S(1)} %copy-done.6, f32[4,4,8,256]{3,2,1,0:T(8,128)S(1)} %bitcast.14, bf16[4,80,4096]{2,1,0:T(8,128)(2,1)} %build.1.rhs_ref, bf16[4,2,1024,80]{3,2,1,0:T(8,128)(2,1)} %get-tuple-element.17.lhs_ref), custom_call_target="tpu_custom_call" | custom-call | flops 24999999488 | bytes 4000000 | tf_op jit(solution)/shard_map/backward/pallas_call | solution.py:243
  85.9 0.1 broadcast_in_dim.12
  86.0 0.1 constant_dynamic-update-slice_fusion.1
  86.0 0.1 collective-permute-start.5
  86.1 16.2 %all_gather.3 = f32[32,4096]{1,0:T(8,128)S(1)} all-gather(f32[8,4096]{1,0:T(8,128)S(1)} %backward.1), channel_id=1, replica_groups=mesh['group'=2,'gene'=4,'lat'=2,'sub'=2] {'gene'}, dimensions={0}, use_global_device_ids=true | all-gather | bytes 655360 | tf_op jit(solution)/shard_map/all_gather | solution.py:424
  102.3 0.0 copy-start.8
  102.4 0.8 copy.15
  103.2 0.3 copy-done.8
  (19 shorter events, 0.1 us)
Async XLA Ops:
  2.3 8.2 %collective-permute-start = (f32[2,256]{1,0:T(2,128)}, f32[2,256]{1,0:T(2,128)S(1)}, u32[]{:S(2)}, u32[]{:S(2)}) collective-permute-start(f32[2,256]{1,0:T(2,128)} %locate.1.rest_0_), channel_id=1, source_target_pairs={{1,0},{0,1},{3,2},{2,3},{5,4},{4,5},{7,6},{6,7},{9,8},{8,9},{11,10... | collective-permute-start | bytes 6152 | tf_op jit(solution)/shard_map/ppermute | solution.py:370
  2.7 7.7 %collective-permute-start.1 = (f32[2,256]{1,0:T(2,128)}, f32[2,256]{1,0:T(2,128)S(1)}, u32[]{:S(2)}, u32[]{:S(2)}) collective-permute-start(f32[2,256]{1,0:T(2,128)} %locate.1.rest_0_), channel_id=1, source_target_pairs={{2,0},{3,1},{0,2},{1,3},{6,4},{7,5},{4,6},{5,7},{10,8},{11,9},{8,1... | collective-permute-start | bytes 6152 | tf_op jit(solution)/shard_map/ppermute | solution.py:370
  5.2 5.3 %collective-permute-start.2 = (f32[2,256]{1,0:T(2,128)}, f32[2,256]{1,0:T(2,128)S(1)}, u32[]{:S(2)}, u32[]{:S(2)}) collective-permute-start(f32[2,256]{1,0:T(2,128)} %locate.1.rest_0_), channel_id=1, source_target_pairs={{3,0},{2,1},{1,2},{0,3},{7,4},{6,5},{5,6},{4,7},{11,8},{10,9},{9,1... | collective-permute-start | bytes 6152 | tf_op jit(solution)/shard_map/ppermute | solution.py:370
  5.4 1.2 %copy-start.1 = (f32[2,32,4096]{2,1,0:T(8,128)S(1)}, f32[2,32,4096]{2,1,0:T(8,128)}, u32[]{:S(2)}) copy-start(f32[2,32,4096]{2,1,0:T(8,128)} %points_ref.1) | copy-start | bytes 3145732
  6.6 0.7 copy-start.5
  7.3 3.2 %copy-start = (f32[2,256]{1,0:T(2,128)S(1)}, f32[2,256]{1,0:T(2,128)}, u32[]{:S(2)}) copy-start(f32[2,256]{1,0:T(2,128)} %locate.1.rest_0_) | copy-start | bytes 6148
  7.3 3.2 %copy-start.2 = (f32[32,4096]{1,0:T(8,128)S(1)}, f32[32,4096]{1,0:T(8,128)}, u32[]{:S(2)}) copy-start(f32[32,4096]{1,0:T(8,128)} %weight_ref.1) | copy-start | bytes 1572868
  7.3 3.2 %copy-start.6 = (f32[32]{0:T(128)S(1)}, f32[32]{0:T(128)}, u32[]{:S(2)}) copy-start(f32[32]{0:T(128)} %var_ref.3) | copy-start | bytes 388
  10.5 23.9 %copy-start.9 = (s32[256]{0:T(256)S(1)}, s32[256]{0:T(256)}, u32[]{:S(2)}) copy-start(s32[256]{0:T(256)} %param.9) | copy-start | bytes 3076
  34.5 14.1 %all-to-all-start = ((f32[16,8,256]{2,1,0:T(8,128)}), f32[16,8,256]{2,1,0:T(8,128)S(1)}, u32[]{:S(2)}, u32[]{:S(2)}) async-start(f32[16,8,256]{2,1,0:T(8,128)} %bitcast.8), calls=%async_computation | async-start | bytes 262144 | tf_op jit(solution)/shard_map/all_to_all | solution.py:406
  40.7 7.9 %copy-start.3 = (bf16[64,4096]{1,0:T(8,128)(2,1)S(1)}, bf16[64,4096]{1,0:T(8,128)(2,1)}, u32[]{:S(2)}) copy-start(bf16[64,4096]{1,0:T(8,128)(2,1)} %mixing_ref.1) | copy-start | bytes 1572868
  40.7 7.9 %copy-start.4 = (f32[4096]{0:T(1024)S(1)}, f32[4096]{0:T(1024)}, u32[]{:S(2)}) copy-start(f32[4096]{0:T(1024)} %param.17) | copy-start | bytes 49156
  48.6 1.6 %copy-start.7 = (bf16[8,256,512]{2,1,0:T(8,128)(2,1)S(1)}, bf16[8,256,512]{2,1,0:T(8,128)(2,1)}, u32[]{:S(2)}) copy-start(bf16[8,256,512]{2,1,0:T(8,128)(2,1)} %observe.1.observed_ref) | copy-start | bytes 6291460
  53.8 3.5 %collective-permute-start.3 = (f32[32,4096]{1,0:T(8,128)S(1)}, f32[32,4096]{1,0:T(8,128)S(1)}, u32[]{:S(2)}, u32[]{:S(2)}) collective-permute-start(f32[32,4096]{1,0:T(8,128)S(1)} %get-tuple-element.15), channel_id=1, source_target_pairs={{1,0},{0,1},{3,2},{2,3},{5,4},{4,5},{7,6},{6,7},{9,8},{8,9},{11,10... | collective-permute-start | bytes 1572872 | tf_op jit(solution)/shard_map/ppermute | solution.py:370
  53.8 11.4 %all-to-all-start.1 = ((f32[16,8,256]{2,1,0:T(8,128)}), f32[16,8,256]{2,1,0:T(8,128)S(1)}, u32[]{:S(2)}, u32[]{:S(2)}) async-start(f32[16,8,256]{2,1,0:T(8,128)} %bitcast.12), calls=%async_computation.1 | async-start | bytes 262144 | tf_op jit(solution)/shard_map/all_to_all | solution.py:415
  57.4 28.4 %collective-permute-start.4 = (f32[32,4096]{1,0:T(8,128)S(1)}, f32[32,4096]{1,0:T(8,128)S(1)}, u32[]{:S(2)}, u32[]{:S(2)}) collective-permute-start(f32[32,4096]{1,0:T(8,128)S(1)} %add.26), channel_id=1, source_target_pairs={{2,0},{0,2},{3,1},{1,3},{6,4},{4,6},{7,5},{5,7},{10,8},{8,10},{11,... | collective-permute-start | bytes 1572872 | tf_op jit(solution)/shard_map/ppermute | solution.py:370
  86.0 16.3 %collective-permute-start.5 = (f32[32,4096]{1,0:T(8,128)S(1)}, f32[32,4096]{1,0:T(8,128)S(1)}, u32[]{:S(2)}, u32[]{:S(2)}) collective-permute-start(f32[32,4096]{1,0:T(8,128)S(1)} %get-tuple-element.21), channel_id=1, source_target_pairs={{1,0},{0,1},{3,2},{2,3},{5,4},{4,5},{7,6},{6,7},{9,8},{8,9},{11,10... | collective-permute-start | bytes 1572872 | tf_op jit(solution)/shard_map/ppermute | solution.py:370
  102.3 1.1 %copy-start.8 = (f32[64,4096]{1,0:T(8,128)}, f32[64,4096]{1,0:T(8,128)S(1)}, u32[]{:S(2)}) copy-start(f32[64,4096]{1,0:T(8,128)S(1)} %constant_dynamic-update-slice_fusion) | copy-start | bytes 3145732

commit v4 on v3

--- a/solution.py
+++ b/solution.py
@@ -99,16 +99,17 @@
     return math.sqrt(0.5 * LOG2E) / lengths
 
 
-def build_kernel(first_ref, length_ref, points_ref, rhs_ref):
-    q = first_ref[0] + 2 * pl.program_id(0)
-    scale = scale_of(length_ref, q)
-    width = math.gcd(points_ref.shape[2], 512)
+def build_kernel(first_ref, length_ref, points_ref, rhs_ref, *, aligned):
+    local = 2 * pl.program_id(0)
+    scale = scale_of(length_ref, first_ref[0] + local)
+    row = local if aligned else first_ref[0] + local
+    width = math.gcd(points_ref.shape[2], 2048)
 
     def step(i, _):
         s = pl.ds(pl.multiple_of(i * width, width), width)
         low = row_of((8, width)) < 4
         u, w = (
-            jnp.where(low, points_ref[d, pl.ds(q, 1), s], points_ref[d, pl.ds(q + 1, 1), s]) for d in (0, 1)
+            jnp.where(low, points_ref[d, pl.ds(row, 1), s], points_ref[d, pl.ds(row + 1, 1), s]) for d in (0, 1)
         )
         rhs_ref[0, :, s] = point_rows(u, w, scale)
         return 0
@@ -117,17 +118,22 @@
 
 
 def build(first, lengths, points, own_q):
-    count = points.shape[2]
-    return pl.pallas_call(
-        build_kernel,
-        grid=(own_q // 2,),
+    axes, local_q, count = points.shape
+    aligned = own_q % 8 == 0
+    block = (axes, own_q if aligned else local_q, count)
+    return pl.pallas_call(
+        functools.partial(build_kernel, aligned=aligned),
         out_shape=pltpu.HBM((own_q // 2, 80, count), jnp.bfloat16),
-        in_specs=[whole(SMEM), whole(SMEM), whole(VMEM)],
-        out_specs=pl.BlockSpec((1, 80, count), lambda i: (i, 0, 0)),
-        compiler_params=pltpu.CompilerParams(vmem_limit_bytes=ROOM),
+        grid_spec=pltpu.PrefetchScalarGridSpec(
+            num_scalar_prefetch=2,
+            grid=(own_q // 2,),
+            in_specs=[pl.BlockSpec(block, lambda i, first, _: (0, first[0] // own_q if aligned else 0, 0))],
+            out_specs=pl.BlockSpec((1, 80, count), lambda i, *_: (i, 0, 0)),
+        ),
+        compiler_params=pltpu.CompilerParams(vmem_limit_bytes=16 << 20),
         cost_estimate=pl.CostEstimate(flops=4_000_000_000, bytes_accessed=4_000_000, transcendentals=0),
         name="build",
-    )(first, lengths, points)
+    )(first, lengths, pltpu.with_memory_space_constraint(points, pltpu.HBM))
 
 
 def forward_kernel(first_ref, order_ref, length_ref, var_ref, weight_ref, rhs_ref, *rest, blocks, NB, SB):
@@ -156,29 +162,14 @@
                 for c in range(SB // 128):
                     total = total + e[:, c * 128 : (c + 1) * 128] * weight[:, c * 128 : (c + 1) * 128]
             acc[rows, :] = total
-        high = acc[...].astype(jnp.bfloat16)
-        rest = acc[...] - high.astype(jnp.float32)
-        middle = rest.astype(jnp.bfloat16)
-        low = (rest - middle.astype(jnp.float32)).astype(jnp.bfloat16)
-        result = functools.reduce(
-            jnp.add,
-            [
-                lax.dot_general(
-                    jnp.ones((8, 128), jnp.bfloat16),
-                    term,
-                    (((1,), (1,)), ((), ())),
-                    preferred_element_type=jnp.float32,
-                )
-                for term in (high, middle, low)
-            ],
-        )
-        result = result[0:1] * var_ref[q + k]
+        result = jnp.sum(acc[...].T, 0, keepdims=True) * var_ref[q + k]
         for b in range(blocks):
             for copy in range(out_ref.shape[0]):
                 out_ref[copy, order_ref[b], pl.ds(local + k, 1), :] = result[:, b * part : (b + 1) * part]
         return 0
 
-    lax.fori_loop(0, 2, latent, 0)
+    for k in range(2):
+        latent(k, 0)
 
 
 def forward(first, order, lengths, var, weights, rhs, xys, own_q, copies):
@@ -204,8 +195,9 @@
     )(first, order, lengths, var, weights, pltpu.with_memory_space_constraint(rhs, pltpu.HBM), *xys)
 
 
-def backward_kernel(first_ref, order_ref, var_ref, grad_ref, rhs_ref, lhs_ref, out_ref, held, spread, *, NB):
-    local = 2 * pl.program_id(0)
+def backward_kernel(first_ref, order_ref, var_ref, grad_ref, rhs_ref, lhs_ref, out_ref, held, spread, *, NB, start):
+    here = 2 * pl.program_id(0)
+    local = 2 * start + here
     q = first_ref[0] + local
     points = rhs_ref.shape[2]
     copies, blocks, _, part = grad_ref.shape
@@ -230,25 +222,26 @@
                 term = (e[:, c * 128 : (c + 1) * 128] * grad).reshape(NB // 8, 8, 128)
                 totals[c] = totals[c] + jnp.sum(term, 0)
         row = jnp.concatenate([jnp.sum(total, 0, keepdims=True) for total in totals], 1)
-        out_ref[pl.ds(local + k, 1), :] = row * var_ref[q + k]
+        out_ref[pl.ds(here + k, 1), :] = row * var_ref[q + k]
         return 0
 
-    lax.fori_loop(0, 2, latent, 0)
-
-
-def backward(first, order, var, grads, rhs, lhs):
-    pairs, _, points = rhs.shape
+    for k in range(2):
+        latent(k, 0)
+
+
+def backward(first, order, var, grads, rhs, lhs, start, pairs):
+    points = rhs.shape[2]
     _, blocks, own_q, part = grads.shape
     cells = blocks * part
     return pl.pallas_call(
-        functools.partial(backward_kernel, NB=math.gcd(cells, 256)),
+        functools.partial(backward_kernel, NB=math.gcd(cells, 256), start=start),
         grid=(pairs,),
-        out_shape=jax.ShapeDtypeStruct((own_q, points), jnp.float32),
+        out_shape=jax.ShapeDtypeStruct((2 * pairs, points), jnp.float32),
         in_specs=[whole(SMEM)] * 3
         + [
             whole(VMEM),
-            pl.BlockSpec((1, 80, points), lambda i: (i, 0, 0)),
-            pl.BlockSpec((1, 2, cells, 80), lambda i: (i, 0, 0, 0)),
+            pl.BlockSpec((1, 80, points), lambda i: (i + start, 0, 0)),
+            pl.BlockSpec((1, 2, cells, 80), lambda i: (i + start, 0, 0, 0)),
         ],
         out_specs=whole(VMEM),
         scratch_shapes=[VMEM((blocks, own_q, part), jnp.float32), VMEM((cells, 128), jnp.float32)],
@@ -256,6 +249,29 @@
         cost_estimate=pl.CostEstimate(flops=25_000_000_000, bytes_accessed=4_000_000, transcendentals=0),
         name="backward",
     )(first, order, var, grads, *(pltpu.with_memory_space_constraint(x, pltpu.HBM) for x in (rhs, lhs)))
+
+
+def gather_kernel(order_ref, *refs):
+    *piece_refs, out_ref = refs
+    each = len(piece_refs) // order_ref.shape[0]
+    for step in range(order_ref.shape[0]):
+        rows = jnp.concatenate([ref[...] for ref in piece_refs[step * each : (step + 1) * each]], 0)
+        out_ref[order_ref[step]] = rows
+
+
+def gather(order, pieces):
+    count = order.shape[0]
+    rows = sum(piece.shape[0] for piece in pieces) // count
+    width = pieces[0].shape[1]
+    out = pl.pallas_call(
+        gather_kernel,
+        out_shape=jax.ShapeDtypeStruct((count, rows, width), jnp.float32),
+        in_specs=[whole(SMEM)] + [whole(VMEM)] * len(pieces),
+        out_specs=whole(VMEM),
+        compiler_params=pltpu.CompilerParams(vmem_limit_bytes=16 << 20),
+        name="gather",
+    )(order, *pieces)
+    return out.reshape(count * rows, width)
 
 
 def observe_kernel(index_ref, expr_hbm, out_hbm, expr_ref, out_ref, load_sem, store_sem):
@@ -418,10 +434,29 @@
     )
     others = [shifted(half, "lat", step, lats) for step in range(1, lats)]
 
-    inducing_term = backward(first, order, variance, pieces.reshape(genes, blocks, own_q, part), rhs, lhs)
-    inducing_term, *others = lax.optimization_barrier((inducing_term, *others))
-    grad_mixing = gather_rows(functools.reduce(jnp.add, others, half), "sub")
-    gathered = lax.all_gather(inducing_term, "gene", axis=0, tiled=True)
+    grads = pieces.reshape(genes, blocks, own_q, part)
+    pairs = own_q // 2
+    early = pairs // 2 if cell_cuts == 1 else 0
+    cut = [(0, early), (early, pairs)] if early else [(0, pairs)]
+    inducing_terms, arrived = [], []
+    for start, stop in cut:
+        term = backward(first, order, variance, grads, rhs, lhs, start, stop - start)
+        if start == 0:
+            term, *others = lax.optimization_barrier((term, *others))
+            half = functools.reduce(jnp.add, others, half)
+        else:
+            term, arrived = lax.optimization_barrier((term, arrived))
+        inducing_terms.append(term)
+        if cell_cuts == 1:
+            arrived = arrived + [[shifted(term, "gene", step, genes) for step in range(1, genes)]]
+    grad_mixing = gather_rows(half, "sub")
+    if cell_cuts == 1:
+        gene_order = jnp.stack([partner(place, step, genes) for step in range(genes)])
+        pieces = list(inducing_terms)
+        for step in range(genes - 1):
+            pieces += [parts[step] for parts in arrived]
+        return (grad_mixing, gather(gene_order, pieces))
+    gathered = lax.all_gather(inducing_terms[0], "gene", axis=0, tiled=True)
     grad_inducing = gathered.reshape(latent_cuts, cell_cuts, own_q, points).sum(1)
     return (grad_mixing, grad_inducing.reshape(local_q, points))
 

time: 104 us -> 99.3 us (0.955)
  blocking collectives: 16.2 us -> 0 us
  starting transfers between devices: 14.7 us -> 22.7 us
  waiting for transfers between devices: 9.48 us -> 14.1 us
  local copies, waits for them, and re-layouts: 4.87 us -> 3.48 us
    all_gather x1 -> x0, blocking collectives: 16.2 us -> none  [on_device(): gathered = lax.all_gather(inducing_term, 'gene', axis=0, tiled=True)]
    ppermute x6 -> x12, starting transfers between devices: 5.03 us -> 12.8 us  [shifted(): lax.ppermute(x, axes, [(partner(i, step, size), i) for i in range(size)])]
    ppermute x6 -> x12, waiting for transfers between devices: 0.02 us -> 4.66 us  [shifted(): lax.ppermute(x, axes, [(partner(i, step, size), i) for i in range(size)])]
    pallas_call x1, Pallas kernels: 23.9 us -> 21.2 us  [forward(): pl.pallas_call(functools.partial(forward_kernel, blocks=blocks, NB=math.g...]
    pallas_call x1 -> x2, Pallas kernels: 3.07 us -> 5.21 us  [the longest x1 3.83 us: build(): pl.pallas_call(functools.partial(build_kernel, aligned=aligned), out_shap...]
    unnamed x21 -> x20, local copies, waits for them, and re-layouts: 4.64 us -> 3.24 us
    pallas_call x1 -> x2, Pallas kernels: 20.6 us -> 21.3 us  [backward(): pl.pallas_call(functools.partial(backward_kernel, NB=math.gcd(cells, 256)...]
  transfers between devices with their start and end apart: 8 -> 14, of which waited for: 2 -> 4; matrix products, arithmetic and copies ran while one was open for 0% -> 0% of each run, Pallas kernels for 27% -> 31%
where the time goes in v4:
time: 99.3 us; the launch traced here: 98.8 us
  Pallas kernels  57.3 us (58%)
  starting transfers between devices  22.7 us (23%)
  waiting for transfers between devices  14.1 us (14%)
  local copies, waits for them, and re-layouts  3.48 us (4%)
    pallas_call x2, Pallas kernels, backward(): pl.pallas_call(functools.partial(backward_kernel, NB=math.gcd(cells, 256)...  21.3 us
    pallas_call x1, Pallas kernels, forward(): pl.pallas_call(functools.partial(forward_kernel, blocks=blocks, NB=math.g...  21.2 us
    ppermute x12, starting transfers between devices, shifted(): lax.ppermute(x, axes, [(partner(i, step, size), i) for i in range(size)])  12.8 us
    all_to_all x1, starting transfers between devices, on_device(): lax.all_to_all(partial.reshape(genes * blocks, own_q, part), every, 0, 0,...  6.14 us
    all_to_all x1, waiting for transfers between devices, on_device(): lax.all_to_all(send.reshape(genes * blocks, own_q, part), every, 0, 0, ti...  5.95 us
    ppermute x12, waiting for transfers between devices, shifted(): lax.ppermute(x, axes, [(partner(i, step, size), i) for i in range(size)])  4.66 us
    pallas_call x1, Pallas kernels, observe(): pl.pallas_call(observe_kernel, out_shape=pltpu.HBM((count, cells, width),...  4.41 us
    pallas_call x1, Pallas kernels, build(): pl.pallas_call(functools.partial(build_kernel, aligned=aligned), out_shap...  3.83 us
  transfers between devices with their start and end apart: 14, of which 4 were waited for; matrix products, arithmetic and copies ran while one was open for 0% of the time, Pallas kernels for 31%

profile of v4, /device:TPU:0, one launch (start us, length us, event | category | flops | bytes accessed | tf_op | source)
XLA Modules:
  0.0 98.8 jit_solution(15679355494518050384)
XLA Ops:
  0.6 1.6 %locate.1.rest_0_ = f32[2,256]{1,0:T(2,128)} custom-call(s32[1,256]{1,0:T(1,128)} %bitcast.24, f32[2,512]{1,0:T(2,128)} %table_ref.1), custom_call_target="tpu_custom_call" | custom-call | tf_op jit(solution)/shard_map/locate/pallas_call | solution.py:90
  2.3 0.5 collective-permute-start
  2.7 2.5 %collective-permute-start.1 = (f32[2,256]{1,0:T(2,128)}, f32[2,256]{1,0:T(2,128)S(1)}, u32[]{:S(2)}, u32[]{:S(2)}) collective-permute-start(f32[2,256]{1,0:T(2,128)} %locate.1.rest_0_), channel_id=1, source_target_pairs={{2,0},{3,1},{0,2},{1,3},{6,4},{7,5},{4,6},{5,7},{10,8},{11,9},{8,1... | collective-permute-start | bytes 6152 | tf_op jit(solution)/shard_map/ppermute | solution.py:386
  5.2 0.1 collective-permute-start.2
  5.3 0.1 pad_add_fusion.rows_ref
  5.4 0.7 copy-done.4
  6.1 3.8 %build.1.rhs_ref = bf16[4,80,4096]{2,1,0:T(8,128)(2,1)} custom-call(s32[1]{0:T(128)} %bitcast.2.first_ref, f32[32]{0:T(128)S(1)} %copy-done.4, f32[2,32,4096]{2,1,0:T(8,128)} %points_ref.1), custom_call_target="tpu_custom_call" | custom-call | flops 4000000000 | bytes 4000000 | tf_op jit(solution)/shard_map/build/pallas_call | solution.py:124
  9.9 0.1 pad_add_fusion.1.order_ref
  10.1 21.2 %forward.1 = (f32[4,4,8,256]{3,2,1,0:T(8,128)}, bf16[4,2,1024,80]{3,2,1,0:T(8,128)(2,1)}) custom-call(s32[1]{0:T(128)} %bitcast.2.first_ref, s32[4]{0:T(128)S(1)} %pad_add_fusion.1.order_ref, f32[32]{0:T(128)S(1)} %copy-done.5, f32[32]{0:T(128)S(1)} %copy-done.6, f32[32,4096]{1,0:T(8,128)S(1)} %copy-done.1, bf16[4,80,4096]{2,1,0:T(8,128)(2,1)} %build.1.rhs_ref, ...), custom_call_target="tpu_custom_call" | custom-call | flops 24999999488 | bytes 4000000 | tf_op jit(solution)/shard_map/forward/pallas_call | solution.py:180
  31.3 0.1 copy.11.index_ref
  31.4 6.1 %all-to-all-start = ((f32[16,8,256]{2,1,0:T(8,128)}), f32[16,8,256]{2,1,0:T(8,128)S(1)}, u32[]{:S(2)}, u32[]{:S(2)}) async-start(f32[16,8,256]{2,1,0:T(8,128)} %bitcast.8), calls=%async_computation | async-start | bytes 262144 | tf_op jit(solution)/shard_map/all_to_all | solution.py:422
  37.6 4.4 %observe.1.observed_ref = bf16[8,256,512]{2,1,0:T(8,128)(2,1)} custom-call(s32[256,1]{1,0:T(8,128)S(1)} %copy.11.index_ref, bf16[512,4096]{1,0:T(8,128)(2,1)} %expr_hbm.1), custom_call_target="tpu_custom_call" | custom-call | flops 3000000000 | bytes 6000000 | tf_op jit(solution)/shard_map/observe/pallas_call | solution.py:304
  42.0 3.5 %all-to-all-done = f32[16,8,256]{2,1,0:T(8,128)S(1)} async-done(((f32[16,8,256]{2,1,0:T(8,128)}), f32[16,8,256]{2,1,0:T(8,128)S(1)}, u32[]{:S(2)}, u32[]{:S(2)}) %all-to-all-start) | async-done | bytes 131104 | tf_op jit(solution)/shard_map/all_to_all | solution.py:422
  45.5 1.6 %copy-done.7 = bf16[8,256,512]{2,1,0:T(8,128)(2,1)S(1)} copy-done((bf16[8,256,512]{2,1,0:T(8,128)(2,1)S(1)}, bf16[8,256,512]{2,1,0:T(8,128)(2,1)}, u32[]{:S(2)}) %copy-start.7) | copy-done | bytes 2097176
  47.1 3.6 %middle.1 = (f32[32,4096]{1,0:T(8,128)S(1)}, f32[32,4096]{1,0:T(8,128)S(1)}, f32[4,4,8,256]{3,2,1,0:T(8,128)}) custom-call(s32[2]{0:T(128)S(1)} %pad_add_fusion.rows_ref, f32[4,4,8,256]{3,2,1,0:T(8,128)S(1)} %bitcast.21, bf16[64,4096]{1,0:T(8,128)(2,1)S(1)} %copy-done.2, f32[1,4096]{1,0:T(1,128)S(1)} %bitcast.22, bf16[8,256,512]{2,1,0:T(8,128)(2,1)S(1)} %copy-done.7), custom_call_target="tpu_custom_call" | custom-call | flops 3000000000 | bytes 4000000 | tf_op jit(solution)/shard_map/middle/pallas_call | solution.py:363
  50.7 3.7 %all-to-all-start.1 = ((f32[16,8,256]{2,1,0:T(8,128)}), f32[16,8,256]{2,1,0:T(8,128)S(1)}, u32[]{:S(2)}, u32[]{:S(2)}) async-start(f32[16,8,256]{2,1,0:T(8,128)} %bitcast.12), calls=%async_computation.1 | async-start | bytes 262144 | tf_op jit(solution)/shard_map/all_to_all | solution.py:431
  54.5 1.7 %collective-permute-start.4 = (f32[32,4096]{1,0:T(8,128)S(1)}, f32[32,4096]{1,0:T(8,128)S(1)}, u32[]{:S(2)}, u32[]{:S(2)}) collective-permute-start(f32[32,4096]{1,0:T(8,128)S(1)} %add.26), channel_id=1, source_target_pairs={{2,0},{0,2},{3,1},{1,3},{6,4},{4,6},{7,5},{5,7},{10,8},{8,10},{11,... | collective-permute-start | bytes 1572872 | tf_op jit(solution)/shard_map/ppermute | solution.py:386
  56.2 6.0 %all-to-all-done.1 = f32[16,8,256]{2,1,0:T(8,128)S(1)} async-done(((f32[16,8,256]{2,1,0:T(8,128)}), f32[16,8,256]{2,1,0:T(8,128)S(1)}, u32[]{:S(2)}, u32[]{:S(2)}) %all-to-all-start.1) | async-done | bytes 131104 | tf_op jit(solution)/shard_map/all_to_all | solution.py:431
  62.2 10.6 %backward.2.refs_0_ = f32[4,4096]{1,0:T(4,128)S(1)} custom-call(s32[1]{0:T(128)} %bitcast.2.first_ref, s32[4]{0:T(128)S(1)} %pad_add_fusion.1.order_ref, f32[32]{0:T(128)S(1)} %copy-done.6, f32[4,4,8,256]{3,2,1,0:T(8,128)S(1)} %bitcast.19, bf16[4,80,4096]{2,1,0:T(8,128)(2,1)} %build.1.rhs_ref, bf16[4,2,1024,80]{3,2,1,0:T(8,128)(2,1)} %get-tuple-element.21.lhs_ref), custom_call_target="tpu_custom_call" | custom-call | flops 24999999488 | bytes 4000000 | tf_op jit(solution)/shard_map/backward/pallas_call | solution.py:236
  72.8 0.1 collective-permute-start.6
  72.9 1.2 %collective-permute-start.7 = (f32[4,4096]{1,0:T(4,128)S(1)}, f32[4,4096]{1,0:T(4,128)S(1)}, u32[]{:S(2)}, u32[]{:S(2)}) collective-permute-start(f32[4,4096]{1,0:T(4,128)S(1)} %backward.2.refs_0_), channel_id=1, source_target_pairs={{8,0},{12,4},{0,8},{4,12},{9,1},{13,5},{1,9},{5,13},{10,2},{14,6},... | collective-permute-start | bytes 196616 | tf_op jit(solution)/shard_map/ppermute | solution.py:386
  74.1 3.2 %collective-permute-start.8 = (f32[4,4096]{1,0:T(4,128)S(1)}, f32[4,4096]{1,0:T(4,128)S(1)}, u32[]{:S(2)}, u32[]{:S(2)}) collective-permute-start(f32[4,4096]{1,0:T(4,128)S(1)} %backward.2.refs_0_), channel_id=1, source_target_pairs={{12,0},{8,4},{4,8},{0,12},{13,1},{9,5},{5,9},{1,13},{14,2},{10,6},... | collective-permute-start | bytes 196616 | tf_op jit(solution)/shard_map/ppermute | solution.py:386
  77.3 0.1 constant_dynamic-update-slice_fusion.1
  77.4 0.1 collective-permute-start.5
  77.5 10.6 %backward.3.refs_1_ = f32[4,4096]{1,0:T(4,128)S(1)} custom-call(s32[1]{0:T(128)} %bitcast.2.first_ref, s32[4]{0:T(128)S(1)} %pad_add_fusion.1.order_ref, f32[32]{0:T(128)S(1)} %copy-done.6, f32[4,4,8,256]{3,2,1,0:T(8,128)S(1)} %bitcast.20, bf16[4,80,4096]{2,1,0:T(8,128)(2,1)} %build.1.rhs_ref, bf16[4,2,1024,80]{3,2,1,0:T(8,128)(2,1)} %get-tuple-element.21.lhs_ref), custom_call_target="tpu_custom_call" | custom-call | flops 24999999488 | bytes 4000000 | tf_op jit(solution)/shard_map/backward/pallas_call | solution.py:236
  88.2 1.5 %collective-permute-start.11 = (f32[4,4096]{1,0:T(4,128)S(1)}, f32[4,4096]{1,0:T(4,128)S(1)}, u32[]{:S(2)}, u32[]{:S(2)}) collective-permute-start(f32[4,4096]{1,0:T(4,128)S(1)} %backward.3.refs_1_), channel_id=1, source_target_pairs={{12,0},{8,4},{4,8},{0,12},{13,1},{9,5},{5,9},{1,13},{14,2},{10,6},... | collective-permute-start | bytes 196616 | tf_op jit(solution)/shard_map/ppermute | solution.py:386
  89.8 1.9 %collective-permute-start.9 = (f32[4,4096]{1,0:T(4,128)S(1)}, f32[4,4096]{1,0:T(4,128)S(1)}, u32[]{:S(2)}, u32[]{:S(2)}) collective-permute-start(f32[4,4096]{1,0:T(4,128)S(1)} %backward.3.refs_1_), channel_id=1, source_target_pairs={{4,0},{0,4},{12,8},{8,12},{5,1},{1,5},{13,9},{9,13},{6,2},{2,6},{1... | collective-permute-start | bytes 196616 | tf_op jit(solution)/shard_map/ppermute | solution.py:386
  91.7 0.1 pad_add_fusion.2.order_ref
  91.8 3.6 %collective-permute-done.10.refs_5_ = f32[4,4096]{1,0:T(4,128)S(1)} collective-permute-done((f32[4,4096]{1,0:T(4,128)S(1)}, f32[4,4096]{1,0:T(4,128)S(1)}, u32[]{:S(2)}, u32[]{:S(2)}) %collective-permute-start.10) | collective-permute-done | bytes 65568 | tf_op jit(solution)/shard_map/ppermute | solution.py:386
  95.4 1.0 %collective-permute-done.9.refs_3_ = f32[4,4096]{1,0:T(4,128)S(1)} collective-permute-done((f32[4,4096]{1,0:T(4,128)S(1)}, f32[4,4096]{1,0:T(4,128)S(1)}, u32[]{:S(2)}, u32[]{:S(2)}) %collective-permute-start.9) | collective-permute-done | bytes 65568 | tf_op jit(solution)/shard_map/ppermute | solution.py:386
  96.4 1.4 %gather.1 = f32[4,8,4096]{2,1,0:T(8,128)} custom-call(s32[4]{0:T(128)S(1)} %pad_add_fusion.2.order_ref, f32[4,4096]{1,0:T(4,128)S(1)} %backward.2.refs_0_, f32[4,4096]{1,0:T(4,128)S(1)} %backward.3.refs_1_, f32[4,4096]{1,0:T(4,128)S(1)} %collective-permute-done.6.refs_2_, f32[4,4096]{1,0:T(4,128)S(1)} %collective-permute-done.9.refs_3_, ...), custom_call_target="tpu_custom_call" | custom-call | tf_op jit(solution)/shard_map/gather/pallas_call | solution.py:266
  97.9 1.0 copy-done.8
  (32 shorter events, 0.3 us)
Async XLA Ops:
  2.3 7.7 %collective-permute-start = (f32[2,256]{1,0:T(2,128)}, f32[2,256]{1,0:T(2,128)S(1)}, u32[]{:S(2)}, u32[]{:S(2)}) collective-permute-start(f32[2,256]{1,0:T(2,128)} %locate.1.rest_0_), channel_id=1, source_target_pairs={{1,0},{0,1},{3,2},{2,3},{5,4},{4,5},{7,6},{6,7},{9,8},{8,9},{11,10... | collective-permute-start | bytes 6152 | tf_op jit(solution)/shard_map/ppermute | solution.py:386
  2.7 7.3 %collective-permute-start.1 = (f32[2,256]{1,0:T(2,128)}, f32[2,256]{1,0:T(2,128)S(1)}, u32[]{:S(2)}, u32[]{:S(2)}) collective-permute-start(f32[2,256]{1,0:T(2,128)} %locate.1.rest_0_), channel_id=1, source_target_pairs={{2,0},{3,1},{0,2},{1,3},{6,4},{7,5},{4,6},{5,7},{10,8},{11,9},{8,1... | collective-permute-start | bytes 6152 | tf_op jit(solution)/shard_map/ppermute | solution.py:386
  5.2 4.8 %collective-permute-start.2 = (f32[2,256]{1,0:T(2,128)}, f32[2,256]{1,0:T(2,128)S(1)}, u32[]{:S(2)}, u32[]{:S(2)}) collective-permute-start(f32[2,256]{1,0:T(2,128)} %locate.1.rest_0_), channel_id=1, source_target_pairs={{3,0},{2,1},{1,2},{0,3},{7,4},{6,5},{5,6},{4,7},{11,8},{10,9},{9,1... | collective-permute-start | bytes 6152 | tf_op jit(solution)/shard_map/ppermute | solution.py:386
  5.4 0.7 copy-start.4
  6.1 3.9 %copy-start = (f32[2,256]{1,0:T(2,128)S(1)}, f32[2,256]{1,0:T(2,128)}, u32[]{:S(2)}) copy-start(f32[2,256]{1,0:T(2,128)} %locate.1.rest_0_) | copy-start | bytes 6148
  6.1 4.0 %copy-start.1 = (f32[32,4096]{1,0:T(8,128)S(1)}, f32[32,4096]{1,0:T(8,128)}, u32[]{:S(2)}) copy-start(f32[32,4096]{1,0:T(8,128)} %weight_ref.1) | copy-start | bytes 1572868
  6.1 4.0 %copy-start.5 = (f32[32]{0:T(128)S(1)}, f32[32]{0:T(128)}, u32[]{:S(2)}) copy-start(f32[32]{0:T(128)} %length_ref.3) | copy-start | bytes 388
  6.1 4.0 %copy-start.6 = (f32[32]{0:T(128)S(1)}, f32[32]{0:T(128)}, u32[]{:S(2)}) copy-start(f32[32]{0:T(128)} %var_ref.5) | copy-start | bytes 388
  10.0 21.3 %copy-start.9 = (s32[256]{0:T(256)S(1)}, s32[256]{0:T(256)}, u32[]{:S(2)}) copy-start(s32[256]{0:T(256)} %param.9) | copy-start | bytes 3076
  31.4 14.1 %all-to-all-start = ((f32[16,8,256]{2,1,0:T(8,128)}), f32[16,8,256]{2,1,0:T(8,128)S(1)}, u32[]{:S(2)}, u32[]{:S(2)}) async-start(f32[16,8,256]{2,1,0:T(8,128)} %bitcast.8), calls=%async_computation | async-start | bytes 262144 | tf_op jit(solution)/shard_map/all_to_all | solution.py:422
  37.6 7.9 %copy-start.2 = (bf16[64,4096]{1,0:T(8,128)(2,1)S(1)}, bf16[64,4096]{1,0:T(8,128)(2,1)}, u32[]{:S(2)}) copy-start(bf16[64,4096]{1,0:T(8,128)(2,1)} %mixing_ref.1) | copy-start | bytes 1572868
  37.6 7.9 %copy-start.3 = (f32[4096]{0:T(1024)S(1)}, f32[4096]{0:T(1024)}, u32[]{:S(2)}) copy-start(f32[4096]{0:T(1024)} %param.17) | copy-start | bytes 49156
  45.5 1.6 %copy-start.7 = (bf16[8,256,512]{2,1,0:T(8,128)(2,1)S(1)}, bf16[8,256,512]{2,1,0:T(8,128)(2,1)}, u32[]{:S(2)}) copy-start(bf16[8,256,512]{2,1,0:T(8,128)(2,1)} %observe.1.observed_ref) | copy-start | bytes 6291460
  50.7 3.7 %collective-permute-start.3 = (f32[32,4096]{1,0:T(8,128)S(1)}, f32[32,4096]{1,0:T(8,128)S(1)}, u32[]{:S(2)}, u32[]{:S(2)}) collective-permute-start(f32[32,4096]{1,0:T(8,128)S(1)} %get-tuple-element.19), channel_id=1, source_target_pairs={{1,0},{0,1},{3,2},{2,3},{5,4},{4,5},{7,6},{6,7},{9,8},{8,9},{11,10... | collective-permute-start | bytes 1572872 | tf_op jit(solution)/shard_map/ppermute | solution.py:386
  50.7 11.4 %all-to-all-start.1 = ((f32[16,8,256]{2,1,0:T(8,128)}), f32[16,8,256]{2,1,0:T(8,128)S(1)}, u32[]{:S(2)}, u32[]{:S(2)}) async-start(f32[16,8,256]{2,1,0:T(8,128)} %bitcast.12), calls=%async_computation.1 | async-start | bytes 262144 | tf_op jit(solution)/shard_map/all_to_all | solution.py:431
  54.5 18.3 %collective-permute-start.4 = (f32[32,4096]{1,0:T(8,128)S(1)}, f32[32,4096]{1,0:T(8,128)S(1)}, u32[]{:S(2)}, u32[]{:S(2)}) collective-permute-start(f32[32,4096]{1,0:T(8,128)S(1)} %add.26), channel_id=1, source_target_pairs={{2,0},{0,2},{3,1},{1,3},{6,4},{4,6},{7,5},{5,7},{10,8},{8,10},{11,... | collective-permute-start | bytes 1572872 | tf_op jit(solution)/shard_map/ppermute | solution.py:386
  72.8 15.3 %collective-permute-start.6 = (f32[4,4096]{1,0:T(4,128)S(1)}, f32[4,4096]{1,0:T(4,128)S(1)}, u32[]{:S(2)}, u32[]{:S(2)}) collective-permute-start(f32[4,4096]{1,0:T(4,128)S(1)} %backward.2.refs_0_), channel_id=1, source_target_pairs={{4,0},{0,4},{12,8},{8,12},{5,1},{1,5},{13,9},{9,13},{6,2},{2,6},{1... | collective-permute-start | bytes 196616 | tf_op jit(solution)/shard_map/ppermute | solution.py:386
  72.9 15.3 %collective-permute-start.7 = (f32[4,4096]{1,0:T(4,128)S(1)}, f32[4,4096]{1,0:T(4,128)S(1)}, u32[]{:S(2)}, u32[]{:S(2)}) collective-permute-start(f32[4,4096]{1,0:T(4,128)S(1)} %backward.2.refs_0_), channel_id=1, source_target_pairs={{8,0},{12,4},{0,8},{4,12},{9,1},{13,5},{1,9},{5,13},{10,2},{14,6},... | collective-permute-start | bytes 196616 | tf_op jit(solution)/shard_map/ppermute | solution.py:386
  74.1 14.1 %collective-permute-start.8 = (f32[4,4096]{1,0:T(4,128)S(1)}, f32[4,4096]{1,0:T(4,128)S(1)}, u32[]{:S(2)}, u32[]{:S(2)}) collective-permute-start(f32[4,4096]{1,0:T(4,128)S(1)} %backward.2.refs_0_), channel_id=1, source_target_pairs={{12,0},{8,4},{4,8},{0,12},{13,1},{9,5},{5,9},{1,13},{14,2},{10,6},... | collective-permute-start | bytes 196616 | tf_op jit(solution)/shard_map/ppermute | solution.py:386
  77.4 20.4 %collective-permute-start.5 = (f32[32,4096]{1,0:T(8,128)S(1)}, f32[32,4096]{1,0:T(8,128)S(1)}, u32[]{:S(2)}, u32[]{:S(2)}) collective-permute-start(f32[32,4096]{1,0:T(8,128)S(1)} %get-tuple-element.29), channel_id=1, source_target_pairs={{1,0},{0,1},{3,2},{2,3},{5,4},{4,5},{7,6},{6,7},{9,8},{8,9},{11,10... | collective-permute-start | bytes 1572872 | tf_op jit(solution)/shard_map/ppermute | solution.py:386
  88.2 7.3 %collective-permute-start.10 = (f32[4,4096]{1,0:T(4,128)S(1)}, f32[4,4096]{1,0:T(4,128)S(1)}, u32[]{:S(2)}, u32[]{:S(2)}) collective-permute-start(f32[4,4096]{1,0:T(4,128)S(1)} %backward.3.refs_1_), channel_id=1, source_target_pairs={{8,0},{12,4},{0,8},{4,12},{9,1},{13,5},{1,9},{5,13},{10,2},{14,6},... | collective-permute-start | bytes 196616 | tf_op jit(solution)/shard_map/ppermute | solution.py:386
  88.2 7.2 %collective-permute-start.11 = (f32[4,4096]{1,0:T(4,128)S(1)}, f32[4,4096]{1,0:T(4,128)S(1)}, u32[]{:S(2)}, u32[]{:S(2)}) collective-permute-start(f32[4,4096]{1,0:T(4,128)S(1)} %backward.3.refs_1_), channel_id=1, source_target_pairs={{12,0},{8,4},{4,8},{0,12},{13,1},{9,5},{5,9},{1,13},{14,2},{10,6},... | collective-permute-start | bytes 196616 | tf_op jit(solution)/shard_map/ppermute | solution.py:386
  89.8 6.7 %collective-permute-start.9 = (f32[4,4096]{1,0:T(4,128)S(1)}, f32[4,4096]{1,0:T(4,128)S(1)}, u32[]{:S(2)}, u32[]{:S(2)}) collective-permute-start(f32[4,4096]{1,0:T(4,128)S(1)} %backward.3.refs_1_), channel_id=1, source_target_pairs={{4,0},{0,4},{12,8},{8,12},{5,1},{1,5},{13,9},{9,13},{6,2},{2,6},{1... | collective-permute-start | bytes 196616 | tf_op jit(solution)/shard_map/ppermute | solution.py:386
  97.9 1.0 copy-start.8

commit v5 on v4

--- a/solution.py
+++ b/solution.py
@@ -103,7 +103,7 @@
     local = 2 * pl.program_id(0)
     scale = scale_of(length_ref, first_ref[0] + local)
     row = local if aligned else first_ref[0] + local
-    width = math.gcd(points_ref.shape[2], 2048)
+    width = points_ref.shape[2]
 
     def step(i, _):
         s = pl.ds(pl.multiple_of(i * width, width), width)
@@ -133,7 +133,7 @@
         compiler_params=pltpu.CompilerParams(vmem_limit_bytes=16 << 20),
         cost_estimate=pl.CostEstimate(flops=4_000_000_000, bytes_accessed=4_000_000, transcendentals=0),
         name="build",
-    )(first, lengths, pltpu.with_memory_space_constraint(points, pltpu.HBM))
+    )(first, pltpu.with_memory_space_constraint(lengths, pltpu.HBM), pltpu.with_memory_space_constraint(points, pltpu.HBM))
 
 
 def forward_kernel(first_ref, order_ref, length_ref, var_ref, weight_ref, rhs_ref, *rest, blocks, NB, SB):
@@ -269,6 +269,7 @@
         in_specs=[whole(SMEM)] + [whole(VMEM)] * len(pieces),
         out_specs=whole(VMEM),
         compiler_params=pltpu.CompilerParams(vmem_limit_bytes=16 << 20),
+        cost_estimate=pl.CostEstimate(flops=0, bytes_accessed=2_000_000, transcendentals=0),
         name="gather",
     )(order, *pieces)
     return out.reshape(count * rows, width)
@@ -299,7 +300,7 @@
 def observe(index, expr):
     rows, genes = expr.shape
     cells = index.shape[0]
-    width = math.gcd(genes, 512)
+    width = math.gcd(genes, 1024)
     count = genes // width
     return pl.pallas_call(
         observe_kernel,
@@ -386,16 +387,6 @@
     return lax.ppermute(x, axes, [(partner(i, step, size), i) for i in range(size)])
 
 
-def gather_rows(x, axis):
-    n = lax.axis_size(axis)
-    me = lax.axis_index(axis)
-    rows = x.shape[0]
-    out = lax.dynamic_update_slice_in_dim(jnp.zeros((n * rows, x.shape[1]), x.dtype), x, me * rows, 0)
-    for step in range(1, n):
-        out = lax.dynamic_update_slice_in_dim(out, shifted(x, axis, step, n), partner(me, step, n) * rows, 0)
-    return out
-
-
 def on_device(cell_index, coords_table, expr_table, inducing, ind_weights, lengthscale, variance, mixing, noise_prec):
     genes, lats, subs = (lax.axis_size(name) for name in ("gene", "lat", "sub"))
     blocks = lats * subs
@@ -449,12 +440,14 @@
         inducing_terms.append(term)
         if cell_cuts == 1:
             arrived = arrived + [[shifted(term, "gene", step, genes) for step in range(1, genes)]]
-    grad_mixing = gather_rows(half, "sub")
+    sub_order = jnp.stack([partner(sub, step, subs) for step in range(subs)])
+    grad_mixing = gather(sub_order, [half] + [shifted(half, "sub", step, subs) for step in range(1, subs)])
     if cell_cuts == 1:
         gene_order = jnp.stack([partner(place, step, genes) for step in range(genes)])
         pieces = list(inducing_terms)
         for step in range(genes - 1):
             pieces += [parts[step] for parts in arrived]
+        pieces, grad_mixing = lax.optimization_barrier((pieces, grad_mixing))
         return (grad_mixing, gather(gene_order, pieces))
     gathered = lax.all_gather(inducing_terms[0], "gene", axis=0, tiled=True)
     grad_inducing = gathered.reshape(latent_cuts, cell_cuts, own_q, points).sum(1)

time: 99.3 us -> 97.5 us (0.982)
  waiting for transfers between devices: 14.1 us -> 12.3 us
  local copies, waits for them, and re-layouts: 3.48 us -> 1.76 us
    ppermute x12, waiting for transfers between devices: 4.66 us -> 2.54 us  [shifted(): lax.ppermute(x, axes, [(partner(i, step, size), i) for i in range(size)])]
    unnamed x20 -> x16, local copies, waits for them, and re-layouts: 3.24 us -> 1.62 us
    pallas_call x1 -> x2, Pallas kernels: 1.38 us -> 2.96 us  [gather(): pl.pallas_call(gather_kernel, out_shape=jax.ShapeDtypeStruct((count, rows...]
  transfers between devices with their start and end apart: 14 -> 14, of which waited for: 4 -> 4; matrix products, arithmetic and copies ran while one was open for 0% -> 1% of each run, Pallas kernels for 31% -> 32%
where the time goes in v5:
time: 97.5 us; the launch traced here: 97 us
  Pallas kernels  58.2 us (60%)
  starting transfers between devices  23.6 us (24%)
  waiting for transfers between devices  12.3 us (13%)
  local copies, waits for them, and re-layouts  1.76 us (2%)
    pallas_call x2, Pallas kernels, backward(): pl.pallas_call(functools.partial(backward_kernel, NB=math.gcd(cells, 256)...  21.3 us
    pallas_call x1, Pallas kernels, forward(): pl.pallas_call(functools.partial(forward_kernel, blocks=blocks, NB=math.g...  21.2 us
    ppermute x12, starting transfers between devices, shifted(): lax.ppermute(x, axes, [(partner(i, step, size), i) for i in range(size)])  13.7 us
    all_to_all x1, starting transfers between devices, on_device(): lax.all_to_all(partial.reshape(genes * blocks, own_q, part), every, 0, 0,...  6.16 us
    all_to_all x1, waiting for transfers between devices, on_device(): lax.all_to_all(send.reshape(genes * blocks, own_q, part), every, 0, 0, ti...  5.94 us
    pallas_call x1, Pallas kernels, build(): pl.pallas_call(functools.partial(build_kernel, aligned=aligned), out_shap...  4.06 us
    pallas_call x1, Pallas kernels, observe(): pl.pallas_call(observe_kernel, out_shape=pltpu.HBM((count, cells, width),...  3.93 us
    all_to_all x1, waiting for transfers between devices, on_device(): lax.all_to_all(partial.reshape(genes * blocks, own_q, part), every, 0, 0,...  3.82 us
  transfers between devices with their start and end apart: 14, of which 4 were waited for; matrix products, arithmetic and copies ran while one was open for 1% of the time, Pallas kernels for 32%

profile of v5, /device:TPU:0, one launch (start us, length us, event | category | flops | bytes accessed | tf_op | source)
XLA Modules:
  0.0 97.0 jit_solution(5460022090528118208)
XLA Ops:
  0.6 1.6 %locate.1.rest_0_ = f32[2,256]{1,0:T(2,128)} custom-call(s32[1,256]{1,0:T(1,128)} %bitcast.26, f32[2,512]{1,0:T(2,128)} %table_ref.1), custom_call_target="tpu_custom_call" | custom-call | tf_op jit(solution)/shard_map/locate/pallas_call | solution.py:90
  2.3 2.4 %collective-permute-start.2 = (f32[2,256]{1,0:T(2,128)}, f32[2,256]{1,0:T(2,128)S(1)}, u32[]{:S(2)}, u32[]{:S(2)}) collective-permute-start(f32[2,256]{1,0:T(2,128)} %locate.1.rest_0_), channel_id=1, source_target_pairs={{3,0},{2,1},{1,2},{0,3},{7,4},{6,5},{5,6},{4,7},{11,8},{10,9},{9,1... | collective-permute-start | bytes 6152 | tf_op jit(solution)/shard_map/ppermute | solution.py:387
  4.6 0.6 collective-permute-start.1
  5.2 0.1 collective-permute-start
  5.3 0.1 pad_add_fusion.1.rows_ref.order_ref
  5.4 4.1 %build.1.rhs_ref = bf16[4,80,4096]{2,1,0:T(8,128)(2,1)} custom-call(s32[1]{0:T(128)} %bitcast.first_ref, f32[32]{0:T(128)} %length_ref.3, f32[2,32,4096]{2,1,0:T(8,128)} %points_ref.1), custom_call_target="tpu_custom_call" | custom-call | flops 4000000000 | bytes 4000000 | tf_op jit(solution)/shard_map/build/pallas_call | solution.py:124
  9.5 0.1 pad_add_fusion.order_ref
  9.6 21.2 %forward.1 = (f32[4,4,8,256]{3,2,1,0:T(8,128)}, bf16[4,2,1024,80]{3,2,1,0:T(8,128)(2,1)}) custom-call(s32[1]{0:T(128)} %bitcast.first_ref, s32[4]{0:T(128)S(1)} %pad_add_fusion.order_ref, f32[32]{0:T(128)S(1)} %copy-done.4, f32[32]{0:T(128)S(1)} %copy-done.5, f32[32,4096]{1,0:T(8,128)S(1)} %copy-done.1, bf16[4,80,4096]{2,1,0:T(8,128)(2,1)} %build.1.rhs_ref, ...), custom_call_target="tpu_custom_call" | custom-call | flops 24999999488 | bytes 4000000 | tf_op jit(solution)/shard_map/forward/pallas_call | solution.py:180
  30.8 6.2 %all-to-all-start = ((f32[16,8,256]{2,1,0:T(8,128)}), f32[16,8,256]{2,1,0:T(8,128)S(1)}, u32[]{:S(2)}, u32[]{:S(2)}) async-start(f32[16,8,256]{2,1,0:T(8,128)} %bitcast.8), calls=%async_computation | async-start | bytes 262144 | tf_op jit(solution)/shard_map/all_to_all | solution.py:413
  37.0 0.1 copy.11.index_ref
  37.2 3.9 %observe.1.observed_ref = bf16[4,256,1024]{2,1,0:T(8,128)(2,1)} custom-call(s32[256,1]{1,0:T(8,128)S(1)} %copy.11.index_ref, bf16[512,4096]{1,0:T(8,128)(2,1)} %expr_hbm.1), custom_call_target="tpu_custom_call" | custom-call | flops 3000000000 | bytes 6000000 | tf_op jit(solution)/shard_map/observe/pallas_call | solution.py:305
  41.1 3.8 %all-to-all-done = f32[16,8,256]{2,1,0:T(8,128)S(1)} async-done(((f32[16,8,256]{2,1,0:T(8,128)}), f32[16,8,256]{2,1,0:T(8,128)S(1)}, u32[]{:S(2)}, u32[]{:S(2)}) %all-to-all-start) | async-done | bytes 131104 | tf_op jit(solution)/shard_map/all_to_all | solution.py:413
  44.9 1.6 %copy-done.6 = bf16[4,256,1024]{2,1,0:T(8,128)(2,1)S(1)} copy-done((bf16[4,256,1024]{2,1,0:T(8,128)(2,1)S(1)}, bf16[4,256,1024]{2,1,0:T(8,128)(2,1)}, u32[]{:S(2)}) %copy-start.6) | copy-done | bytes 2097176
  46.5 3.2 %middle.1 = (f32[32,4096]{1,0:T(8,128)S(1)}, f32[32,4096]{1,0:T(8,128)S(1)}, f32[4,4,8,256]{3,2,1,0:T(8,128)}) custom-call(s32[2]{0:T(128)S(1)} %pad_add_fusion.1.rows_ref.order_ref, f32[4,4,8,256]{3,2,1,0:T(8,128)S(1)} %bitcast.22, bf16[64,4096]{1,0:T(8,128)(2,1)S(1)} %copy-done.2, f32[1,4096]{1,0:T(1,128)S(1)} %bitcast.23, bf16[4,256,1024]{2,1,0:T(8,128)(2,1)S(1)} %copy-done.6), custom_call_target="tpu_custom_call" | custom-call | flops 3000000000 | bytes 4000000 | tf_op jit(solution)/shard_map/middle/pallas_call | solution.py:364
  49.7 3.7 %all-to-all-start.1 = ((f32[16,8,256]{2,1,0:T(8,128)}), f32[16,8,256]{2,1,0:T(8,128)S(1)}, u32[]{:S(2)}, u32[]{:S(2)}) async-start(f32[16,8,256]{2,1,0:T(8,128)} %bitcast.12), calls=%async_computation.1 | async-start | bytes 262144 | tf_op jit(solution)/shard_map/all_to_all | solution.py:422
  53.4 0.1 add.20
  53.5 1.7 %collective-permute-start.4 = (f32[32,4096]{1,0:T(8,128)S(1)}, f32[32,4096]{1,0:T(8,128)S(1)}, u32[]{:S(2)}, u32[]{:S(2)}) collective-permute-start(f32[32,4096]{1,0:T(8,128)S(1)} %add.20), channel_id=1, source_target_pairs={{2,0},{0,2},{3,1},{1,3},{6,4},{4,6},{7,5},{5,7},{10,8},{8,10},{11,... | collective-permute-start | bytes 1572872 | tf_op jit(solution)/shard_map/ppermute | solution.py:387
  55.2 5.9 %all-to-all-done.1 = f32[16,8,256]{2,1,0:T(8,128)S(1)} async-done(((f32[16,8,256]{2,1,0:T(8,128)}), f32[16,8,256]{2,1,0:T(8,128)S(1)}, u32[]{:S(2)}, u32[]{:S(2)}) %all-to-all-start.1) | async-done | bytes 131104 | tf_op jit(solution)/shard_map/all_to_all | solution.py:422
  61.1 10.6 %backward.2.refs_0_ = f32[4,4096]{1,0:T(4,128)S(1)} custom-call(s32[1]{0:T(128)} %bitcast.first_ref, s32[4]{0:T(128)S(1)} %pad_add_fusion.order_ref, f32[32]{0:T(128)S(1)} %copy-done.5, f32[4,4,8,256]{3,2,1,0:T(8,128)S(1)} %bitcast.20, bf16[4,80,4096]{2,1,0:T(8,128)(2,1)} %build.1.rhs_ref, bf16[4,2,1024,80]{3,2,1,0:T(8,128)(2,1)} %get-tuple-element.28.lhs_ref), custom_call_target="tpu_custom_call" | custom-call | flops 24999999488 | bytes 4000000 | tf_op jit(solution)/shard_map/backward/pallas_call | solution.py:236
  71.7 0.7 collective-permute-start.7
  72.5 0.2 collective-permute-start.6
  72.7 3.5 %collective-permute-start.5 = (f32[4,4096]{1,0:T(4,128)S(1)}, f32[4,4096]{1,0:T(4,128)S(1)}, u32[]{:S(2)}, u32[]{:S(2)}) collective-permute-start(f32[4,4096]{1,0:T(4,128)S(1)} %backward.2.refs_0_), channel_id=1, source_target_pairs={{4,0},{0,4},{12,8},{8,12},{5,1},{1,5},{13,9},{9,13},{6,2},{2,6},{1... | collective-permute-start | bytes 196616 | tf_op jit(solution)/shard_map/ppermute | solution.py:387
  76.3 0.1 collective-permute-start.11
  76.3 10.6 %backward.3.refs_1_ = f32[4,4096]{1,0:T(4,128)S(1)} custom-call(s32[1]{0:T(128)} %bitcast.first_ref, s32[4]{0:T(128)S(1)} %pad_add_fusion.order_ref, f32[32]{0:T(128)S(1)} %copy-done.5, f32[4,4,8,256]{3,2,1,0:T(8,128)S(1)} %bitcast.21, bf16[4,80,4096]{2,1,0:T(8,128)(2,1)} %build.1.rhs_ref, bf16[4,2,1024,80]{3,2,1,0:T(8,128)(2,1)} %get-tuple-element.28.lhs_ref), custom_call_target="tpu_custom_call" | custom-call | flops 24999999488 | bytes 4000000 | tf_op jit(solution)/shard_map/backward/pallas_call | solution.py:236
  87.0 0.7 collective-permute-start.10
  87.7 0.8 collective-permute-start.9
  88.6 2.9 %collective-permute-start.8 = (f32[4,4096]{1,0:T(4,128)S(1)}, f32[4,4096]{1,0:T(4,128)S(1)}, u32[]{:S(2)}, u32[]{:S(2)}) collective-permute-start(f32[4,4096]{1,0:T(4,128)S(1)} %backward.3.refs_1_), channel_id=1, source_target_pairs={{4,0},{0,4},{12,8},{8,12},{5,1},{1,5},{13,9},{9,13},{6,2},{2,6},{1... | collective-permute-start | bytes 196616 | tf_op jit(solution)/shard_map/ppermute | solution.py:387
  91.5 0.1 pad_add_fusion.2.order_ref
  91.6 1.6 %gather.2 = f32[2,32,4096]{2,1,0:T(8,128)} custom-call(s32[2]{0:T(128)S(1)} %pad_add_fusion.1.rows_ref.order_ref, f32[32,4096]{1,0:T(8,128)S(1)} %add.21.refs_0_, f32[32,4096]{1,0:T(8,128)S(1)} %collective-permute-done.11.refs_1_), custom_call_target="tpu_custom_call" | custom-call | bytes 2000000 | tf_op jit(solution)/shard_map/gather/pallas_call | solution.py:266
  93.1 0.7 collective-permute-done.10.refs_7_
  93.9 1.8 %collective-permute-done.9.refs_5_ = f32[4,4096]{1,0:T(4,128)S(1)} collective-permute-done((f32[4,4096]{1,0:T(4,128)S(1)}, f32[4,4096]{1,0:T(4,128)S(1)}, u32[]{:S(2)}, u32[]{:S(2)}) %collective-permute-start.9) | collective-permute-done | bytes 65568 | tf_op jit(solution)/shard_map/ppermute | solution.py:387
  95.7 1.4 %gather.3 = f32[4,8,4096]{2,1,0:T(8,128)} custom-call(s32[4]{0:T(128)S(1)} %pad_add_fusion.2.order_ref, f32[4,4096]{1,0:T(4,128)S(1)} %backward.2.refs_0_, f32[4,4096]{1,0:T(4,128)S(1)} %backward.3.refs_1_, f32[4,4096]{1,0:T(4,128)S(1)} %collective-permute-done.5.refs_2_, f32[4,4096]{1,0:T(4,128)S(1)} %collective-permute-done.8.refs_3_, ...), custom_call_target="tpu_custom_call" | custom-call | bytes 2000000 | tf_op jit(solution)/shard_map/gather/pallas_call | solution.py:266
  (27 shorter events, 0.1 us)
Async XLA Ops:
  2.3 7.3 %collective-permute-start.2 = (f32[2,256]{1,0:T(2,128)}, f32[2,256]{1,0:T(2,128)S(1)}, u32[]{:S(2)}, u32[]{:S(2)}) collective-permute-start(f32[2,256]{1,0:T(2,128)} %locate.1.rest_0_), channel_id=1, source_target_pairs={{3,0},{2,1},{1,2},{0,3},{7,4},{6,5},{5,6},{4,7},{11,8},{10,9},{9,1... | collective-permute-start | bytes 6152 | tf_op jit(solution)/shard_map/ppermute | solution.py:387
  4.6 4.9 %collective-permute-start.1 = (f32[2,256]{1,0:T(2,128)}, f32[2,256]{1,0:T(2,128)S(1)}, u32[]{:S(2)}, u32[]{:S(2)}) collective-permute-start(f32[2,256]{1,0:T(2,128)} %locate.1.rest_0_), channel_id=1, source_target_pairs={{2,0},{3,1},{0,2},{1,3},{6,4},{7,5},{4,6},{5,7},{10,8},{11,9},{8,1... | collective-permute-start | bytes 6152 | tf_op jit(solution)/shard_map/ppermute | solution.py:387
  5.2 4.3 %collective-permute-start = (f32[2,256]{1,0:T(2,128)}, f32[2,256]{1,0:T(2,128)S(1)}, u32[]{:S(2)}, u32[]{:S(2)}) collective-permute-start(f32[2,256]{1,0:T(2,128)} %locate.1.rest_0_), channel_id=1, source_target_pairs={{1,0},{0,1},{3,2},{2,3},{5,4},{4,5},{7,6},{6,7},{9,8},{8,9},{11,10... | collective-permute-start | bytes 6152 | tf_op jit(solution)/shard_map/ppermute | solution.py:387
  5.4 4.2 %copy-start = (f32[2,256]{1,0:T(2,128)S(1)}, f32[2,256]{1,0:T(2,128)}, u32[]{:S(2)}) copy-start(f32[2,256]{1,0:T(2,128)} %locate.1.rest_0_) | copy-start | bytes 6148
  5.4 4.2 %copy-start.1 = (f32[32,4096]{1,0:T(8,128)S(1)}, f32[32,4096]{1,0:T(8,128)}, u32[]{:S(2)}) copy-start(f32[32,4096]{1,0:T(8,128)} %weight_ref.1) | copy-start | bytes 1572868
  5.4 4.2 %copy-start.4 = (f32[32]{0:T(128)S(1)}, f32[32]{0:T(128)}, u32[]{:S(2)}) copy-start(f32[32]{0:T(128)} %length_ref.3) | copy-start | bytes 388
  5.4 4.2 %copy-start.5 = (f32[32]{0:T(128)S(1)}, f32[32]{0:T(128)}, u32[]{:S(2)}) copy-start(f32[32]{0:T(128)} %var_ref.5) | copy-start | bytes 388
  9.5 27.5 %copy-start.7 = (s32[256]{0:T(256)S(1)}, s32[256]{0:T(256)}, u32[]{:S(2)}) copy-start(s32[256]{0:T(256)} %param.9) | copy-start | bytes 3076
  30.8 14.1 %all-to-all-start = ((f32[16,8,256]{2,1,0:T(8,128)}), f32[16,8,256]{2,1,0:T(8,128)S(1)}, u32[]{:S(2)}, u32[]{:S(2)}) async-start(f32[16,8,256]{2,1,0:T(8,128)} %bitcast.8), calls=%async_computation | async-start | bytes 262144 | tf_op jit(solution)/shard_map/all_to_all | solution.py:413
  37.1 7.8 %copy-start.2 = (bf16[64,4096]{1,0:T(8,128)(2,1)S(1)}, bf16[64,4096]{1,0:T(8,128)(2,1)}, u32[]{:S(2)}) copy-start(bf16[64,4096]{1,0:T(8,128)(2,1)} %mixing_ref.1) | copy-start | bytes 1572868
  37.2 7.8 %copy-start.3 = (f32[4096]{0:T(1024)S(1)}, f32[4096]{0:T(1024)}, u32[]{:S(2)}) copy-start(f32[4096]{0:T(1024)} %param.17) | copy-start | bytes 49156
  44.9 1.6 %copy-start.6 = (bf16[4,256,1024]{2,1,0:T(8,128)(2,1)S(1)}, bf16[4,256,1024]{2,1,0:T(8,128)(2,1)}, u32[]{:S(2)}) copy-start(bf16[4,256,1024]{2,1,0:T(8,128)(2,1)} %observe.1.observed_ref) | copy-start | bytes 6291460
  49.7 3.7 %collective-permute-start.3 = (f32[32,4096]{1,0:T(8,128)S(1)}, f32[32,4096]{1,0:T(8,128)S(1)}, u32[]{:S(2)}, u32[]{:S(2)}) collective-permute-start(f32[32,4096]{1,0:T(8,128)S(1)} %get-tuple-element.30), channel_id=1, source_target_pairs={{1,0},{0,1},{3,2},{2,3},{5,4},{4,5},{7,6},{6,7},{9,8},{8,9},{11,10... | collective-permute-start | bytes 1572872 | tf_op jit(solution)/shard_map/ppermute | solution.py:387
  49.7 11.4 %all-to-all-start.1 = ((f32[16,8,256]{2,1,0:T(8,128)}), f32[16,8,256]{2,1,0:T(8,128)S(1)}, u32[]{:S(2)}, u32[]{:S(2)}) async-start(f32[16,8,256]{2,1,0:T(8,128)} %bitcast.12), calls=%async_computation.1 | async-start | bytes 262144 | tf_op jit(solution)/shard_map/all_to_all | solution.py:422
  53.5 18.3 %collective-permute-start.4 = (f32[32,4096]{1,0:T(8,128)S(1)}, f32[32,4096]{1,0:T(8,128)S(1)}, u32[]{:S(2)}, u32[]{:S(2)}) collective-permute-start(f32[32,4096]{1,0:T(8,128)S(1)} %add.20), channel_id=1, source_target_pairs={{2,0},{0,2},{3,1},{1,3},{6,4},{4,6},{7,5},{5,7},{10,8},{8,10},{11,... | collective-permute-start | bytes 1572872 | tf_op jit(solution)/shard_map/ppermute | solution.py:387
  71.7 15.2 %collective-permute-start.7 = (f32[4,4096]{1,0:T(4,128)S(1)}, f32[4,4096]{1,0:T(4,128)S(1)}, u32[]{:S(2)}, u32[]{:S(2)}) collective-permute-start(f32[4,4096]{1,0:T(4,128)S(1)} %backward.2.refs_0_), channel_id=1, source_target_pairs={{12,0},{8,4},{4,8},{0,12},{13,1},{9,5},{5,9},{1,13},{14,2},{10,6},... | collective-permute-start | bytes 196616 | tf_op jit(solution)/shard_map/ppermute | solution.py:387
  72.5 14.5 %collective-permute-start.6 = (f32[4,4096]{1,0:T(4,128)S(1)}, f32[4,4096]{1,0:T(4,128)S(1)}, u32[]{:S(2)}, u32[]{:S(2)}) collective-permute-start(f32[4,4096]{1,0:T(4,128)S(1)} %backward.2.refs_0_), channel_id=1, source_target_pairs={{8,0},{12,4},{0,8},{4,12},{9,1},{13,5},{1,9},{5,13},{10,2},{14,6},... | collective-permute-start | bytes 196616 | tf_op jit(solution)/shard_map/ppermute | solution.py:387
  72.7 14.3 %collective-permute-start.5 = (f32[4,4096]{1,0:T(4,128)S(1)}, f32[4,4096]{1,0:T(4,128)S(1)}, u32[]{:S(2)}, u32[]{:S(2)}) collective-permute-start(f32[4,4096]{1,0:T(4,128)S(1)} %backward.2.refs_0_), channel_id=1, source_target_pairs={{4,0},{0,4},{12,8},{8,12},{5,1},{1,5},{13,9},{9,13},{6,2},{2,6},{1... | collective-permute-start | bytes 196616 | tf_op jit(solution)/shard_map/ppermute | solution.py:387
  76.3 15.3 %collective-permute-start.11 = (f32[32,4096]{1,0:T(8,128)S(1)}, f32[32,4096]{1,0:T(8,128)S(1)}, u32[]{:S(2)}, u32[]{:S(2)}) collective-permute-start(f32[32,4096]{1,0:T(8,128)S(1)} %add.21.refs_0_), channel_id=1, source_target_pairs={{1,0},{0,1},{3,2},{2,3},{5,4},{4,5},{7,6},{6,7},{9,8},{8,9},{11,10... | collective-permute-start | bytes 1572872 | tf_op jit(solution)/shard_map/ppermute | solution.py:387
  87.0 6.9 %collective-permute-start.10 = (f32[4,4096]{1,0:T(4,128)S(1)}, f32[4,4096]{1,0:T(4,128)S(1)}, u32[]{:S(2)}, u32[]{:S(2)}) collective-permute-start(f32[4,4096]{1,0:T(4,128)S(1)} %backward.3.refs_1_), channel_id=1, source_target_pairs={{12,0},{8,4},{4,8},{0,12},{13,1},{9,5},{5,9},{1,13},{14,2},{10,6},... | collective-permute-start | bytes 196616 | tf_op jit(solution)/shard_map/ppermute | solution.py:387
  87.7 7.9 %collective-permute-start.9 = (f32[4,4096]{1,0:T(4,128)S(1)}, f32[4,4096]{1,0:T(4,128)S(1)}, u32[]{:S(2)}, u32[]{:S(2)}) collective-permute-start(f32[4,4096]{1,0:T(4,128)S(1)} %backward.3.refs_1_), channel_id=1, source_target_pairs={{8,0},{12,4},{0,8},{4,12},{9,1},{13,5},{1,9},{5,13},{10,2},{14,6},... | collective-permute-start | bytes 196616 | tf_op jit(solution)/shard_map/ppermute | solution.py:387
  88.6 7.1 %collective-permute-start.8 = (f32[4,4096]{1,0:T(4,128)S(1)}, f32[4,4096]{1,0:T(4,128)S(1)}, u32[]{:S(2)}, u32[]{:S(2)}) collective-permute-start(f32[4,4096]{1,0:T(4,128)S(1)} %backward.3.refs_1_), channel_id=1, source_target_pairs={{4,0},{0,4},{12,8},{8,12},{5,1},{1,5},{13,9},{9,13},{6,2},{2,6},{1... | collective-permute-start | bytes 196616 | tf_op jit(solution)/shard_map/ppermute | solution.py:387

commit v6 on v5

--- a/solution.py
+++ b/solution.py
@@ -379,7 +379,7 @@
         pieces,
         mixing,
         noise[None, :],
-        observed,
+        pltpu.with_memory_space_constraint(observed, pltpu.HBM),
     )
 
 

time: 97.5 us -> 97 us (level)
  local copies, waits for them, and re-layouts: 1.76 us -> 0.16 us
  Pallas kernels: 58.2 us -> 59.3 us
    unnamed x16 -> x14, local copies, waits for them, and re-layouts: 1.62 us -> 0.03 us
    pallas_call x1, Pallas kernels: 3.15 us -> 4.22 us  [middle(): pl.pallas_call(functools.partial(middle_kernel, scale=scale, cuts=cuts, s...]
where the time goes in v6:
time: 97 us; the launch traced here: 96.5 us
  Pallas kernels  59.3 us (61%)
  starting transfers between devices  23.6 us (24%)
  waiting for transfers between devices  12.3 us (13%)
    pallas_call x2, Pallas kernels, backward(): pl.pallas_call(functools.partial(backward_kernel, NB=math.gcd(cells, 256)...  21.3 us
    pallas_call x1, Pallas kernels, forward(): pl.pallas_call(functools.partial(forward_kernel, blocks=blocks, NB=math.g...  21.2 us
    ppermute x12, starting transfers between devices, shifted(): lax.ppermute(x, axes, [(partner(i, step, size), i) for i in range(size)])  13.7 us
    all_to_all x1, starting transfers between devices, on_device(): lax.all_to_all(partial.reshape(genes * blocks, own_q, part), every, 0, 0,...  6.16 us
    all_to_all x1, waiting for transfers between devices, on_device(): lax.all_to_all(send.reshape(genes * blocks, own_q, part), every, 0, 0, ti...  5.94 us
    pallas_call x1, Pallas kernels, middle(): pl.pallas_call(functools.partial(middle_kernel, scale=scale, cuts=cuts, s...  4.22 us
    pallas_call x1, Pallas kernels, build(): pl.pallas_call(functools.partial(build_kernel, aligned=aligned), out_shap...  4.07 us
    pallas_call x1, Pallas kernels, observe(): pl.pallas_call(observe_kernel, out_shape=pltpu.HBM((count, cells, width),...  3.93 us
  transfers between devices with their start and end apart: 14, of which 4 were waited for; matrix products, arithmetic and copies ran while one was open for 1% of the time, Pallas kernels for 32%

profile of v6, /device:TPU:0, one launch (start us, length us, event | category | flops | bytes accessed | tf_op | source)
XLA Modules:
  0.0 96.5 jit_solution(4961216830606789387)
XLA Ops:
  0.6 1.6 %locate.1.rest_0_ = f32[2,256]{1,0:T(2,128)} custom-call(s32[1,256]{1,0:T(1,128)} %bitcast.26, f32[2,512]{1,0:T(2,128)} %table_ref.1), custom_call_target="tpu_custom_call" | custom-call | tf_op jit(solution)/shard_map/locate/pallas_call | solution.py:90
  2.3 2.4 %collective-permute-start.2 = (f32[2,256]{1,0:T(2,128)}, f32[2,256]{1,0:T(2,128)S(1)}, u32[]{:S(2)}, u32[]{:S(2)}) collective-permute-start(f32[2,256]{1,0:T(2,128)} %locate.1.rest_0_), channel_id=1, source_target_pairs={{3,0},{2,1},{1,2},{0,3},{7,4},{6,5},{5,6},{4,7},{11,8},{10,9},{9,1... | collective-permute-start | bytes 6152 | tf_op jit(solution)/shard_map/ppermute | solution.py:387
  4.6 0.6 collective-permute-start.1
  5.2 0.1 collective-permute-start
  5.3 0.1 pad_add_fusion.1.rows_ref.order_ref
  5.4 4.1 %build.1.rhs_ref = bf16[4,80,4096]{2,1,0:T(8,128)(2,1)} custom-call(s32[1]{0:T(128)} %bitcast.first_ref, f32[32]{0:T(128)} %length_ref.3, f32[2,32,4096]{2,1,0:T(8,128)} %points_ref.1), custom_call_target="tpu_custom_call" | custom-call | flops 4000000000 | bytes 4000000 | tf_op jit(solution)/shard_map/build/pallas_call | solution.py:124
  9.5 0.1 pad_add_fusion.order_ref
  9.6 21.2 %forward.1 = (f32[4,4,8,256]{3,2,1,0:T(8,128)}, bf16[4,2,1024,80]{3,2,1,0:T(8,128)(2,1)}) custom-call(s32[1]{0:T(128)} %bitcast.first_ref, s32[4]{0:T(128)S(1)} %pad_add_fusion.order_ref, f32[32]{0:T(128)S(1)} %copy-done.4, f32[32]{0:T(128)S(1)} %copy-done.5, f32[32,4096]{1,0:T(8,128)S(1)} %copy-done.1, bf16[4,80,4096]{2,1,0:T(8,128)(2,1)} %build.1.rhs_ref, ...), custom_call_target="tpu_custom_call" | custom-call | flops 24999999488 | bytes 4000000 | tf_op jit(solution)/shard_map/forward/pallas_call | solution.py:180
  30.8 6.2 %all-to-all-start = ((f32[16,8,256]{2,1,0:T(8,128)}), f32[16,8,256]{2,1,0:T(8,128)S(1)}, u32[]{:S(2)}, u32[]{:S(2)}) async-start(f32[16,8,256]{2,1,0:T(8,128)} %bitcast.8), calls=%async_computation | async-start | bytes 262144 | tf_op jit(solution)/shard_map/all_to_all | solution.py:413
  37.0 0.1 copy.11.index_ref
  37.2 3.9 %observe.1.observed_ref = bf16[4,256,1024]{2,1,0:T(8,128)(2,1)} custom-call(s32[256,1]{1,0:T(8,128)S(1)} %copy.11.index_ref, bf16[512,4096]{1,0:T(8,128)(2,1)} %expr_hbm.1), custom_call_target="tpu_custom_call" | custom-call | flops 3000000000 | bytes 6000000 | tf_op jit(solution)/shard_map/observe/pallas_call | solution.py:305
  41.1 3.8 %all-to-all-done = f32[16,8,256]{2,1,0:T(8,128)S(1)} async-done(((f32[16,8,256]{2,1,0:T(8,128)}), f32[16,8,256]{2,1,0:T(8,128)S(1)}, u32[]{:S(2)}, u32[]{:S(2)}) %all-to-all-start) | async-done | bytes 131104 | tf_op jit(solution)/shard_map/all_to_all | solution.py:413
  44.9 4.2 %middle.1 = (f32[32,4096]{1,0:T(8,128)S(1)}, f32[32,4096]{1,0:T(8,128)S(1)}, f32[4,4,8,256]{3,2,1,0:T(8,128)}) custom-call(s32[2]{0:T(128)S(1)} %pad_add_fusion.1.rows_ref.order_ref, f32[4,4,8,256]{3,2,1,0:T(8,128)S(1)} %bitcast.22, bf16[64,4096]{1,0:T(8,128)(2,1)S(1)} %copy-done.2, f32[1,4096]{1,0:T(1,128)S(1)} %bitcast.23, ...), custom_call_target="tpu_custom_call" | custom-call | flops 3000000000 | bytes 4000000 | tf_op jit(solution)/shard_map/middle/pallas_call | solution.py:364
  49.2 3.7 %all-to-all-start.1 = ((f32[16,8,256]{2,1,0:T(8,128)}), f32[16,8,256]{2,1,0:T(8,128)S(1)}, u32[]{:S(2)}, u32[]{:S(2)}) async-start(f32[16,8,256]{2,1,0:T(8,128)} %bitcast.12), calls=%async_computation.1 | async-start | bytes 262144 | tf_op jit(solution)/shard_map/all_to_all | solution.py:422
  52.9 0.1 add.20
  53.0 1.7 %collective-permute-start.4 = (f32[32,4096]{1,0:T(8,128)S(1)}, f32[32,4096]{1,0:T(8,128)S(1)}, u32[]{:S(2)}, u32[]{:S(2)}) collective-permute-start(f32[32,4096]{1,0:T(8,128)S(1)} %add.20), channel_id=1, source_target_pairs={{2,0},{0,2},{3,1},{1,3},{6,4},{4,6},{7,5},{5,7},{10,8},{8,10},{11,... | collective-permute-start | bytes 1572872 | tf_op jit(solution)/shard_map/ppermute | solution.py:387
  54.6 5.9 %all-to-all-done.1 = f32[16,8,256]{2,1,0:T(8,128)S(1)} async-done(((f32[16,8,256]{2,1,0:T(8,128)}), f32[16,8,256]{2,1,0:T(8,128)S(1)}, u32[]{:S(2)}, u32[]{:S(2)}) %all-to-all-start.1) | async-done | bytes 131104 | tf_op jit(solution)/shard_map/all_to_all | solution.py:422
  60.6 10.6 %backward.2.refs_0_ = f32[4,4096]{1,0:T(4,128)S(1)} custom-call(s32[1]{0:T(128)} %bitcast.first_ref, s32[4]{0:T(128)S(1)} %pad_add_fusion.order_ref, f32[32]{0:T(128)S(1)} %copy-done.5, f32[4,4,8,256]{3,2,1,0:T(8,128)S(1)} %bitcast.20, bf16[4,80,4096]{2,1,0:T(8,128)(2,1)} %build.1.rhs_ref, bf16[4,2,1024,80]{3,2,1,0:T(8,128)(2,1)} %get-tuple-element.28.lhs_ref), custom_call_target="tpu_custom_call" | custom-call | flops 24999999488 | bytes 4000000 | tf_op jit(solution)/shard_map/backward/pallas_call | solution.py:236
  71.2 0.7 collective-permute-start.7
  72.0 0.2 collective-permute-start.6
  72.2 3.5 %collective-permute-start.5 = (f32[4,4096]{1,0:T(4,128)S(1)}, f32[4,4096]{1,0:T(4,128)S(1)}, u32[]{:S(2)}, u32[]{:S(2)}) collective-permute-start(f32[4,4096]{1,0:T(4,128)S(1)} %backward.2.refs_0_), channel_id=1, source_target_pairs={{4,0},{0,4},{12,8},{8,12},{5,1},{1,5},{13,9},{9,13},{6,2},{2,6},{1... | collective-permute-start | bytes 196616 | tf_op jit(solution)/shard_map/ppermute | solution.py:387
  75.7 0.1 add.21.refs_0_
  75.7 0.1 collective-permute-start.11
  75.8 10.6 %backward.3.refs_1_ = f32[4,4096]{1,0:T(4,128)S(1)} custom-call(s32[1]{0:T(128)} %bitcast.first_ref, s32[4]{0:T(128)S(1)} %pad_add_fusion.order_ref, f32[32]{0:T(128)S(1)} %copy-done.5, f32[4,4,8,256]{3,2,1,0:T(8,128)S(1)} %bitcast.21, bf16[4,80,4096]{2,1,0:T(8,128)(2,1)} %build.1.rhs_ref, bf16[4,2,1024,80]{3,2,1,0:T(8,128)(2,1)} %get-tuple-element.28.lhs_ref), custom_call_target="tpu_custom_call" | custom-call | flops 24999999488 | bytes 4000000 | tf_op jit(solution)/shard_map/backward/pallas_call | solution.py:236
  86.5 0.7 collective-permute-start.10
  87.2 0.8 collective-permute-start.9
  88.0 2.9 %collective-permute-start.8 = (f32[4,4096]{1,0:T(4,128)S(1)}, f32[4,4096]{1,0:T(4,128)S(1)}, u32[]{:S(2)}, u32[]{:S(2)}) collective-permute-start(f32[4,4096]{1,0:T(4,128)S(1)} %backward.3.refs_1_), channel_id=1, source_target_pairs={{4,0},{0,4},{12,8},{8,12},{5,1},{1,5},{13,9},{9,13},{6,2},{2,6},{1... | collective-permute-start | bytes 196616 | tf_op jit(solution)/shard_map/ppermute | solution.py:387
  91.0 0.1 pad_add_fusion.2.order_ref
  91.0 1.6 %gather.2 = f32[2,32,4096]{2,1,0:T(8,128)} custom-call(s32[2]{0:T(128)S(1)} %pad_add_fusion.1.rows_ref.order_ref, f32[32,4096]{1,0:T(8,128)S(1)} %add.21.refs_0_, f32[32,4096]{1,0:T(8,128)S(1)} %collective-permute-done.11.refs_1_), custom_call_target="tpu_custom_call" | custom-call | bytes 2000000 | tf_op jit(solution)/shard_map/gather/pallas_call | solution.py:266
  92.6 0.7 collective-permute-done.10.refs_7_
  93.4 1.8 %collective-permute-done.9.refs_5_ = f32[4,4096]{1,0:T(4,128)S(1)} collective-permute-done((f32[4,4096]{1,0:T(4,128)S(1)}, f32[4,4096]{1,0:T(4,128)S(1)}, u32[]{:S(2)}, u32[]{:S(2)}) %collective-permute-start.9) | collective-permute-done | bytes 65568 | tf_op jit(solution)/shard_map/ppermute | solution.py:387
  95.1 1.4 %gather.3 = f32[4,8,4096]{2,1,0:T(8,128)} custom-call(s32[4]{0:T(128)S(1)} %pad_add_fusion.2.order_ref, f32[4,4096]{1,0:T(4,128)S(1)} %backward.2.refs_0_, f32[4,4096]{1,0:T(4,128)S(1)} %backward.3.refs_1_, f32[4,4096]{1,0:T(4,128)S(1)} %collective-permute-done.5.refs_2_, f32[4,4096]{1,0:T(4,128)S(1)} %collective-permute-done.8.refs_3_, ...), custom_call_target="tpu_custom_call" | custom-call | bytes 2000000 | tf_op jit(solution)/shard_map/gather/pallas_call | solution.py:266
  (25 shorter events, 0.1 us)
Async XLA Ops:
  2.3 7.3 %collective-permute-start.2 = (f32[2,256]{1,0:T(2,128)}, f32[2,256]{1,0:T(2,128)S(1)}, u32[]{:S(2)}, u32[]{:S(2)}) collective-permute-start(f32[2,256]{1,0:T(2,128)} %locate.1.rest_0_), channel_id=1, source_target_pairs={{3,0},{2,1},{1,2},{0,3},{7,4},{6,5},{5,6},{4,7},{11,8},{10,9},{9,1... | collective-permute-start | bytes 6152 | tf_op jit(solution)/shard_map/ppermute | solution.py:387
  4.6 4.9 %collective-permute-start.1 = (f32[2,256]{1,0:T(2,128)}, f32[2,256]{1,0:T(2,128)S(1)}, u32[]{:S(2)}, u32[]{:S(2)}) collective-permute-start(f32[2,256]{1,0:T(2,128)} %locate.1.rest_0_), channel_id=1, source_target_pairs={{2,0},{3,1},{0,2},{1,3},{6,4},{7,5},{4,6},{5,7},{10,8},{11,9},{8,1... | collective-permute-start | bytes 6152 | tf_op jit(solution)/shard_map/ppermute | solution.py:387
  5.2 4.3 %collective-permute-start = (f32[2,256]{1,0:T(2,128)}, f32[2,256]{1,0:T(2,128)S(1)}, u32[]{:S(2)}, u32[]{:S(2)}) collective-permute-start(f32[2,256]{1,0:T(2,128)} %locate.1.rest_0_), channel_id=1, source_target_pairs={{1,0},{0,1},{3,2},{2,3},{5,4},{4,5},{7,6},{6,7},{9,8},{8,9},{11,10... | collective-permute-start | bytes 6152 | tf_op jit(solution)/shard_map/ppermute | solution.py:387
  5.4 4.2 %copy-start = (f32[2,256]{1,0:T(2,128)S(1)}, f32[2,256]{1,0:T(2,128)}, u32[]{:S(2)}) copy-start(f32[2,256]{1,0:T(2,128)} %locate.1.rest_0_) | copy-start | bytes 6148
  5.4 4.2 %copy-start.1 = (f32[32,4096]{1,0:T(8,128)S(1)}, f32[32,4096]{1,0:T(8,128)}, u32[]{:S(2)}) copy-start(f32[32,4096]{1,0:T(8,128)} %weight_ref.1) | copy-start | bytes 1572868
  5.4 4.2 %copy-start.4 = (f32[32]{0:T(128)S(1)}, f32[32]{0:T(128)}, u32[]{:S(2)}) copy-start(f32[32]{0:T(128)} %length_ref.3) | copy-start | bytes 388
  5.4 4.2 %copy-start.5 = (f32[32]{0:T(128)S(1)}, f32[32]{0:T(128)}, u32[]{:S(2)}) copy-start(f32[32]{0:T(128)} %var_ref.5) | copy-start | bytes 388
  9.6 27.4 %copy-start.6 = (s32[256]{0:T(256)S(1)}, s32[256]{0:T(256)}, u32[]{:S(2)}) copy-start(s32[256]{0:T(256)} %param.9) | copy-start | bytes 3076
  30.8 14.1 %all-to-all-start = ((f32[16,8,256]{2,1,0:T(8,128)}), f32[16,8,256]{2,1,0:T(8,128)S(1)}, u32[]{:S(2)}, u32[]{:S(2)}) async-start(f32[16,8,256]{2,1,0:T(8,128)} %bitcast.8), calls=%async_computation | async-start | bytes 262144 | tf_op jit(solution)/shard_map/all_to_all | solution.py:413
  37.1 7.8 %copy-start.2 = (bf16[64,4096]{1,0:T(8,128)(2,1)S(1)}, bf16[64,4096]{1,0:T(8,128)(2,1)}, u32[]{:S(2)}) copy-start(bf16[64,4096]{1,0:T(8,128)(2,1)} %mixing_ref.1) | copy-start | bytes 1572868
  37.2 7.8 %copy-start.3 = (f32[4096]{0:T(1024)S(1)}, f32[4096]{0:T(1024)}, u32[]{:S(2)}) copy-start(f32[4096]{0:T(1024)} %param.17) | copy-start | bytes 49156
  49.2 3.7 %collective-permute-start.3 = (f32[32,4096]{1,0:T(8,128)S(1)}, f32[32,4096]{1,0:T(8,128)S(1)}, u32[]{:S(2)}, u32[]{:S(2)}) collective-permute-start(f32[32,4096]{1,0:T(8,128)S(1)} %get-tuple-element.30), channel_id=1, source_target_pairs={{1,0},{0,1},{3,2},{2,3},{5,4},{4,5},{7,6},{6,7},{9,8},{8,9},{11,10... | collective-permute-start | bytes 1572872 | tf_op jit(solution)/shard_map/ppermute | solution.py:387
  49.2 11.4 %all-to-all-start.1 = ((f32[16,8,256]{2,1,0:T(8,128)}), f32[16,8,256]{2,1,0:T(8,128)S(1)}, u32[]{:S(2)}, u32[]{:S(2)}) async-start(f32[16,8,256]{2,1,0:T(8,128)} %bitcast.12), calls=%async_computation.1 | async-start | bytes 262144 | tf_op jit(solution)/shard_map/all_to_all | solution.py:422
  53.0 18.3 %collective-permute-start.4 = (f32[32,4096]{1,0:T(8,128)S(1)}, f32[32,4096]{1,0:T(8,128)S(1)}, u32[]{:S(2)}, u32[]{:S(2)}) collective-permute-start(f32[32,4096]{1,0:T(8,128)S(1)} %add.20), channel_id=1, source_target_pairs={{2,0},{0,2},{3,1},{1,3},{6,4},{4,6},{7,5},{5,7},{10,8},{8,10},{11,... | collective-permute-start | bytes 1572872 | tf_op jit(solution)/shard_map/ppermute | solution.py:387
  71.2 15.2 %collective-permute-start.7 = (f32[4,4096]{1,0:T(4,128)S(1)}, f32[4,4096]{1,0:T(4,128)S(1)}, u32[]{:S(2)}, u32[]{:S(2)}) collective-permute-start(f32[4,4096]{1,0:T(4,128)S(1)} %backward.2.refs_0_), channel_id=1, source_target_pairs={{12,0},{8,4},{4,8},{0,12},{13,1},{9,5},{5,9},{1,13},{14,2},{10,6},... | collective-permute-start | bytes 196616 | tf_op jit(solution)/shard_map/ppermute | solution.py:387
  72.0 14.5 %collective-permute-start.6 = (f32[4,4096]{1,0:T(4,128)S(1)}, f32[4,4096]{1,0:T(4,128)S(1)}, u32[]{:S(2)}, u32[]{:S(2)}) collective-permute-start(f32[4,4096]{1,0:T(4,128)S(1)} %backward.2.refs_0_), channel_id=1, source_target_pairs={{8,0},{12,4},{0,8},{4,12},{9,1},{13,5},{1,9},{5,13},{10,2},{14,6},... | collective-permute-start | bytes 196616 | tf_op jit(solution)/shard_map/ppermute | solution.py:387
  72.2 14.3 %collective-permute-start.5 = (f32[4,4096]{1,0:T(4,128)S(1)}, f32[4,4096]{1,0:T(4,128)S(1)}, u32[]{:S(2)}, u32[]{:S(2)}) collective-permute-start(f32[4,4096]{1,0:T(4,128)S(1)} %backward.2.refs_0_), channel_id=1, source_target_pairs={{4,0},{0,4},{12,8},{8,12},{5,1},{1,5},{13,9},{9,13},{6,2},{2,6},{1... | collective-permute-start | bytes 196616 | tf_op jit(solution)/shard_map/ppermute | solution.py:387
  75.7 15.3 %collective-permute-start.11 = (f32[32,4096]{1,0:T(8,128)S(1)}, f32[32,4096]{1,0:T(8,128)S(1)}, u32[]{:S(2)}, u32[]{:S(2)}) collective-permute-start(f32[32,4096]{1,0:T(8,128)S(1)} %add.21.refs_0_), channel_id=1, source_target_pairs={{1,0},{0,1},{3,2},{2,3},{5,4},{4,5},{7,6},{6,7},{9,8},{8,9},{11,10... | collective-permute-start | bytes 1572872 | tf_op jit(solution)/shard_map/ppermute | solution.py:387
  86.5 6.9 %collective-permute-start.10 = (f32[4,4096]{1,0:T(4,128)S(1)}, f32[4,4096]{1,0:T(4,128)S(1)}, u32[]{:S(2)}, u32[]{:S(2)}) collective-permute-start(f32[4,4096]{1,0:T(4,128)S(1)} %backward.3.refs_1_), channel_id=1, source_target_pairs={{12,0},{8,4},{4,8},{0,12},{13,1},{9,5},{5,9},{1,13},{14,2},{10,6},... | collective-permute-start | bytes 196616 | tf_op jit(solution)/shard_map/ppermute | solution.py:387
  87.2 7.9 %collective-permute-start.9 = (f32[4,4096]{1,0:T(4,128)S(1)}, f32[4,4096]{1,0:T(4,128)S(1)}, u32[]{:S(2)}, u32[]{:S(2)}) collective-permute-start(f32[4,4096]{1,0:T(4,128)S(1)} %backward.3.refs_1_), channel_id=1, source_target_pairs={{8,0},{12,4},{0,8},{4,12},{9,1},{13,5},{1,9},{5,13},{10,2},{14,6},... | collective-permute-start | bytes 196616 | tf_op jit(solution)/shard_map/ppermute | solution.py:387
  88.0 7.1 %collective-permute-start.8 = (f32[4,4096]{1,0:T(4,128)S(1)}, f32[4,4096]{1,0:T(4,128)S(1)}, u32[]{:S(2)}, u32[]{:S(2)}) collective-permute-start(f32[4,4096]{1,0:T(4,128)S(1)} %backward.3.refs_1_), channel_id=1, source_target_pairs={{4,0},{0,4},{12,8},{8,12},{5,1},{1,5},{13,9},{9,13},{6,2},{2,6},{1... | collective-permute-start | bytes 196616 | tf_op jit(solution)/shard_map/ppermute | solution.py:387

commit v7 on v6

--- a/solution.py
+++ b/solution.py
@@ -37,8 +37,12 @@
 
 def point_rows(u, w, a):
     T1, T2, T3 = parts(u, w, a)
-    one = jnp.ones_like(T1)
-    return jnp.concatenate([T1, T1, T2, T2, T1, T2, T3, T3, one, jnp.zeros_like(one)], 0).astype(jnp.bfloat16)
+    return jnp.concatenate([T1, T2, T3, jnp.ones_like(T1)], 0).astype(jnp.bfloat16)
+
+
+def spread_rows(rows):
+    first, second = rows[:16], rows[16:]
+    return jnp.concatenate([first, first, first, second, second], 0)
 
 def cell_rows(u, w, a):
     T1, T2, T3 = parts(u, w, a)
@@ -57,7 +61,7 @@
         z = jnp.zeros_like(n(T1, 0))
         norm = jnp.concatenate([n(T1, 2), n(T2, 2), n(T1, 3), n(T2, 3), n(T3, 3), z, z, z], 0)
         G1, G2, G3 = G
-        outs.append(jnp.concatenate([G1, G2, G1, G2, G3, G3, G1, G2, norm, jnp.zeros_like(norm)], 0))
+        outs.append(jnp.concatenate([G1, G1, G2, G2, G3, G3, G1, norm, G2, jnp.zeros_like(norm)], 0))
     return outs
 
 VMEM = pltpu.VMEM
@@ -123,12 +127,12 @@
     block = (axes, own_q if aligned else local_q, count)
     return pl.pallas_call(
         functools.partial(build_kernel, aligned=aligned),
-        out_shape=pltpu.HBM((own_q // 2, 80, count), jnp.bfloat16),
+        out_shape=pltpu.HBM((own_q // 2, 32, count), jnp.bfloat16),
         grid_spec=pltpu.PrefetchScalarGridSpec(
             num_scalar_prefetch=2,
             grid=(own_q // 2,),
             in_specs=[pl.BlockSpec(block, lambda i, first, _: (0, first[0] // own_q if aligned else 0, 0))],
-            out_specs=pl.BlockSpec((1, 80, count), lambda i, *_: (i, 0, 0)),
+            out_specs=pl.BlockSpec((1, 32, count), lambda i, *_: (i, 0, 0)),
         ),
         compiler_params=pltpu.CompilerParams(vmem_limit_bytes=16 << 20),
         cost_estimate=pl.CostEstimate(flops=4_000_000_000, bytes_accessed=4_000_000, transcendentals=0),
@@ -157,7 +161,7 @@
             total = jnp.zeros((NB, 128), jnp.float32)
             for j in range(points // SB):
                 s = slice(j * SB, (j + 1) * SB)
-                e = jnp.exp2(jnp.dot(cell, rhs_ref[0, :, s], preferred_element_type=jnp.float32))
+                e = jnp.exp2(jnp.dot(cell, spread_rows(rhs_ref[0, :, s]), preferred_element_type=jnp.float32))
                 weight = weight_ref[pl.ds(q + k, 1), s]
                 for c in range(SB // 128):
                     total = total + e[:, c * 128 : (c + 1) * 128] * weight[:, c * 128 : (c + 1) * 128]
@@ -185,7 +189,7 @@
             pltpu.HBM((own_q // 2, 2, cells, 80), jnp.bfloat16),
         ),
         in_specs=[whole(SMEM)] * 4
-        + [whole(VMEM), pl.BlockSpec((1, 80, points), lambda i: (i, 0, 0))]
+        + [whole(VMEM), pl.BlockSpec((1, 32, points), lambda i: (i, 0, 0))]
         + [whole(VMEM)] * blocks,
         out_specs=(whole(VMEM), pl.BlockSpec((1, 2, cells, 80), lambda i: (i, 0, 0, 0))),
         scratch_shapes=[VMEM((cells, 128), jnp.float32)],
@@ -216,7 +220,7 @@
         for nb in range(cells // NB):
             rows = slice(nb * NB, (nb + 1) * NB)
             cell = lhs_ref[0, k, rows, :]
-            e = jnp.exp2(jnp.dot(cell, rhs_ref[0], preferred_element_type=jnp.float32))
+            e = jnp.exp2(jnp.dot(cell, spread_rows(rhs_ref[0]), preferred_element_type=jnp.float32))
             grad = spread[rows, :]
             for c in range(points // 128):
                 term = (e[:, c * 128 : (c + 1) * 128] * grad).reshape(NB // 8, 8, 128)
@@ -240,7 +244,7 @@
         in_specs=[whole(SMEM)] * 3
         + [
             whole(VMEM),
-            pl.BlockSpec((1, 80, points), lambda i: (i + start, 0, 0)),
+            pl.BlockSpec((1, 32, points), lambda i: (i + start, 0, 0)),
             pl.BlockSpec((1, 2, cells, 80), lambda i: (i + start, 0, 0, 0)),
         ],
         out_specs=whole(VMEM),

time: 97 us -> 96.1 us (level)
  no operation moved by 1% of the time
where the time goes in v7:
time: 96.1 us; the launch traced here: 95.7 us
  Pallas kernels  58.4 us (61%)
  starting transfers between devices  23.6 us (25%)
  waiting for transfers between devices  12.3 us (13%)
    pallas_call x2, Pallas kernels, backward(): pl.pallas_call(functools.partial(backward_kernel, NB=math.gcd(cells, 256)...  21 us
    pallas_call x1, Pallas kernels, forward(): pl.pallas_call(functools.partial(forward_kernel, blocks=blocks, NB=math.g...  21 us
    ppermute x12, starting transfers between devices, shifted(): lax.ppermute(x, axes, [(partner(i, step, size), i) for i in range(size)])  13.7 us
    all_to_all x1, starting transfers between devices, on_device(): lax.all_to_all(partial.reshape(genes * blocks, own_q, part), every, 0, 0,...  6.16 us
    all_to_all x1, waiting for transfers between devices, on_device(): lax.all_to_all(send.reshape(genes * blocks, own_q, part), every, 0, 0, ti...  5.94 us
    pallas_call x1, Pallas kernels, middle(): pl.pallas_call(functools.partial(middle_kernel, scale=scale, cuts=cuts, s...  4.22 us
    pallas_call x1, Pallas kernels, observe(): pl.pallas_call(observe_kernel, out_shape=pltpu.HBM((count, cells, width),...  3.92 us
    all_to_all x1, waiting for transfers between devices, on_device(): lax.all_to_all(partial.reshape(genes * blocks, own_q, part), every, 0, 0,...  3.84 us
  transfers between devices with their start and end apart: 14, of which 4 were waited for; matrix products, arithmetic and copies ran while one was open for 1% of the time, Pallas kernels for 32%

profile of v7, /device:TPU:0, one launch (start us, length us, event | category | flops | bytes accessed | tf_op | source)
XLA Modules:
  0.0 95.7 jit_solution(8542036686307354111)
XLA Ops:
  0.6 1.6 %locate.1.rest_0_ = f32[2,256]{1,0:T(2,128)} custom-call(s32[1,256]{1,0:T(1,128)} %bitcast.26, f32[2,512]{1,0:T(2,128)} %table_ref.1), custom_call_target="tpu_custom_call" | custom-call | tf_op jit(solution)/shard_map/locate/pallas_call | solution.py:94
  2.3 2.4 %collective-permute-start.2 = (f32[2,256]{1,0:T(2,128)}, f32[2,256]{1,0:T(2,128)S(1)}, u32[]{:S(2)}, u32[]{:S(2)}) collective-permute-start(f32[2,256]{1,0:T(2,128)} %locate.1.rest_0_), channel_id=1, source_target_pairs={{3,0},{2,1},{1,2},{0,3},{7,4},{6,5},{5,6},{4,7},{11,8},{10,9},{9,1... | collective-permute-start | bytes 6152 | tf_op jit(solution)/shard_map/ppermute | solution.py:391
  4.6 0.6 collective-permute-start.1
  5.2 0.1 collective-permute-start
  5.3 0.1 pad_add_fusion.1.rows_ref.order_ref
  5.4 3.7 %build.1.rhs_ref = bf16[4,32,4096]{2,1,0:T(8,128)(2,1)} custom-call(s32[1]{0:T(128)} %bitcast.first_ref, f32[32]{0:T(128)} %length_ref.3, f32[2,32,4096]{2,1,0:T(8,128)} %points_ref.1), custom_call_target="tpu_custom_call" | custom-call | flops 4000000000 | bytes 4000000 | tf_op jit(solution)/shard_map/build/pallas_call | solution.py:128
  9.1 0.1 pad_add_fusion.order_ref
  9.3 21.0 %forward.1 = (f32[4,4,8,256]{3,2,1,0:T(8,128)}, bf16[4,2,1024,80]{3,2,1,0:T(8,128)(2,1)}) custom-call(s32[1]{0:T(128)} %bitcast.first_ref, s32[4]{0:T(128)S(1)} %pad_add_fusion.order_ref, f32[32]{0:T(128)S(1)} %copy-done.4, f32[32]{0:T(128)S(1)} %copy-done.5, f32[32,4096]{1,0:T(8,128)S(1)} %copy-done.1, bf16[4,32,4096]{2,1,0:T(8,128)(2,1)} %build.1.rhs_ref, ...), custom_call_target="tpu_custom_call" | custom-call | flops 24999999488 | bytes 4000000 | tf_op jit(solution)/shard_map/forward/pallas_call | solution.py:184
  30.2 6.2 %all-to-all-start = ((f32[16,8,256]{2,1,0:T(8,128)}), f32[16,8,256]{2,1,0:T(8,128)S(1)}, u32[]{:S(2)}, u32[]{:S(2)}) async-start(f32[16,8,256]{2,1,0:T(8,128)} %bitcast.8), calls=%async_computation | async-start | bytes 262144 | tf_op jit(solution)/shard_map/all_to_all | solution.py:417
  36.4 0.1 copy.11.index_ref
  36.6 3.9 %observe.1.observed_ref = bf16[4,256,1024]{2,1,0:T(8,128)(2,1)} custom-call(s32[256,1]{1,0:T(8,128)S(1)} %copy.11.index_ref, bf16[512,4096]{1,0:T(8,128)(2,1)} %expr_hbm.1), custom_call_target="tpu_custom_call" | custom-call | flops 3000000000 | bytes 6000000 | tf_op jit(solution)/shard_map/observe/pallas_call | solution.py:309
  40.5 3.8 %all-to-all-done = f32[16,8,256]{2,1,0:T(8,128)S(1)} async-done(((f32[16,8,256]{2,1,0:T(8,128)}), f32[16,8,256]{2,1,0:T(8,128)S(1)}, u32[]{:S(2)}, u32[]{:S(2)}) %all-to-all-start) | async-done | bytes 131104 | tf_op jit(solution)/shard_map/all_to_all | solution.py:417
  44.4 4.2 %middle.1 = (f32[32,4096]{1,0:T(8,128)S(1)}, f32[32,4096]{1,0:T(8,128)S(1)}, f32[4,4,8,256]{3,2,1,0:T(8,128)}) custom-call(s32[2]{0:T(128)S(1)} %pad_add_fusion.1.rows_ref.order_ref, f32[4,4,8,256]{3,2,1,0:T(8,128)S(1)} %bitcast.22, bf16[64,4096]{1,0:T(8,128)(2,1)S(1)} %copy-done.2, f32[1,4096]{1,0:T(1,128)S(1)} %bitcast.23, ...), custom_call_target="tpu_custom_call" | custom-call | flops 3000000000 | bytes 4000000 | tf_op jit(solution)/shard_map/middle/pallas_call | solution.py:368
  48.6 3.7 %all-to-all-start.1 = ((f32[16,8,256]{2,1,0:T(8,128)}), f32[16,8,256]{2,1,0:T(8,128)S(1)}, u32[]{:S(2)}, u32[]{:S(2)}) async-start(f32[16,8,256]{2,1,0:T(8,128)} %bitcast.12), calls=%async_computation.1 | async-start | bytes 262144 | tf_op jit(solution)/shard_map/all_to_all | solution.py:426
  52.3 0.1 add.20
  52.4 1.7 %collective-permute-start.4 = (f32[32,4096]{1,0:T(8,128)S(1)}, f32[32,4096]{1,0:T(8,128)S(1)}, u32[]{:S(2)}, u32[]{:S(2)}) collective-permute-start(f32[32,4096]{1,0:T(8,128)S(1)} %add.20), channel_id=1, source_target_pairs={{2,0},{0,2},{3,1},{1,3},{6,4},{4,6},{7,5},{5,7},{10,8},{8,10},{11,... | collective-permute-start | bytes 1572872 | tf_op jit(solution)/shard_map/ppermute | solution.py:391
  54.1 5.9 %all-to-all-done.1 = f32[16,8,256]{2,1,0:T(8,128)S(1)} async-done(((f32[16,8,256]{2,1,0:T(8,128)}), f32[16,8,256]{2,1,0:T(8,128)S(1)}, u32[]{:S(2)}, u32[]{:S(2)}) %all-to-all-start.1) | async-done | bytes 131104 | tf_op jit(solution)/shard_map/all_to_all | solution.py:426
  60.0 10.5 %backward.2.refs_0_ = f32[4,4096]{1,0:T(4,128)S(1)} custom-call(s32[1]{0:T(128)} %bitcast.first_ref, s32[4]{0:T(128)S(1)} %pad_add_fusion.order_ref, f32[32]{0:T(128)S(1)} %copy-done.5, f32[4,4,8,256]{3,2,1,0:T(8,128)S(1)} %bitcast.20, bf16[4,32,4096]{2,1,0:T(8,128)(2,1)} %build.1.rhs_ref, bf16[4,2,1024,80]{3,2,1,0:T(8,128)(2,1)} %get-tuple-element.28.lhs_ref), custom_call_target="tpu_custom_call" | custom-call | flops 24999999488 | bytes 4000000 | tf_op jit(solution)/shard_map/backward/pallas_call | solution.py:240
  70.5 0.7 collective-permute-start.7
  71.2 0.2 collective-permute-start.6
  71.4 3.5 %collective-permute-start.5 = (f32[4,4096]{1,0:T(4,128)S(1)}, f32[4,4096]{1,0:T(4,128)S(1)}, u32[]{:S(2)}, u32[]{:S(2)}) collective-permute-start(f32[4,4096]{1,0:T(4,128)S(1)} %backward.2.refs_0_), channel_id=1, source_target_pairs={{4,0},{0,4},{12,8},{8,12},{5,1},{1,5},{13,9},{9,13},{6,2},{2,6},{1... | collective-permute-start | bytes 196616 | tf_op jit(solution)/shard_map/ppermute | solution.py:391
  75.0 0.1 add.21.refs_0_
  75.0 0.1 collective-permute-start.11
  75.1 10.5 %backward.3.refs_1_ = f32[4,4096]{1,0:T(4,128)S(1)} custom-call(s32[1]{0:T(128)} %bitcast.first_ref, s32[4]{0:T(128)S(1)} %pad_add_fusion.order_ref, f32[32]{0:T(128)S(1)} %copy-done.5, f32[4,4,8,256]{3,2,1,0:T(8,128)S(1)} %bitcast.21, bf16[4,32,4096]{2,1,0:T(8,128)(2,1)} %build.1.rhs_ref, bf16[4,2,1024,80]{3,2,1,0:T(8,128)(2,1)} %get-tuple-element.28.lhs_ref), custom_call_target="tpu_custom_call" | custom-call | flops 24999999488 | bytes 4000000 | tf_op jit(solution)/shard_map/backward/pallas_call | solution.py:240
  85.7 0.7 collective-permute-start.10
  86.4 0.8 collective-permute-start.9
  87.2 2.9 %collective-permute-start.8 = (f32[4,4096]{1,0:T(4,128)S(1)}, f32[4,4096]{1,0:T(4,128)S(1)}, u32[]{:S(2)}, u32[]{:S(2)}) collective-permute-start(f32[4,4096]{1,0:T(4,128)S(1)} %backward.3.refs_1_), channel_id=1, source_target_pairs={{4,0},{0,4},{12,8},{8,12},{5,1},{1,5},{13,9},{9,13},{6,2},{2,6},{1... | collective-permute-start | bytes 196616 | tf_op jit(solution)/shard_map/ppermute | solution.py:391
  90.1 0.1 pad_add_fusion.2.order_ref
  90.2 1.6 %gather.2 = f32[2,32,4096]{2,1,0:T(8,128)} custom-call(s32[2]{0:T(128)S(1)} %pad_add_fusion.1.rows_ref.order_ref, f32[32,4096]{1,0:T(8,128)S(1)} %add.21.refs_0_, f32[32,4096]{1,0:T(8,128)S(1)} %collective-permute-done.11.refs_1_), custom_call_target="tpu_custom_call" | custom-call | bytes 2000000 | tf_op jit(solution)/shard_map/gather/pallas_call | solution.py:270
  91.8 0.7 collective-permute-done.10.refs_7_
  92.5 1.8 %collective-permute-done.9.refs_5_ = f32[4,4096]{1,0:T(4,128)S(1)} collective-permute-done((f32[4,4096]{1,0:T(4,128)S(1)}, f32[4,4096]{1,0:T(4,128)S(1)}, u32[]{:S(2)}, u32[]{:S(2)}) %collective-permute-start.9) | collective-permute-done | bytes 65568 | tf_op jit(solution)/shard_map/ppermute | solution.py:391
  94.3 1.4 %gather.3 = f32[4,8,4096]{2,1,0:T(8,128)} custom-call(s32[4]{0:T(128)S(1)} %pad_add_fusion.2.order_ref, f32[4,4096]{1,0:T(4,128)S(1)} %backward.2.refs_0_, f32[4,4096]{1,0:T(4,128)S(1)} %backward.3.refs_1_, f32[4,4096]{1,0:T(4,128)S(1)} %collective-permute-done.5.refs_2_, f32[4,4096]{1,0:T(4,128)S(1)} %collective-permute-done.8.refs_3_, ...), custom_call_target="tpu_custom_call" | custom-call | bytes 2000000 | tf_op jit(solution)/shard_map/gather/pallas_call | solution.py:270
  (25 shorter events, 0.1 us)
Async XLA Ops:
  2.3 7.0 %collective-permute-start.2 = (f32[2,256]{1,0:T(2,128)}, f32[2,256]{1,0:T(2,128)S(1)}, u32[]{:S(2)}, u32[]{:S(2)}) collective-permute-start(f32[2,256]{1,0:T(2,128)} %locate.1.rest_0_), channel_id=1, source_target_pairs={{3,0},{2,1},{1,2},{0,3},{7,4},{6,5},{5,6},{4,7},{11,8},{10,9},{9,1... | collective-permute-start | bytes 6152 | tf_op jit(solution)/shard_map/ppermute | solution.py:391
  4.6 4.6 %collective-permute-start.1 = (f32[2,256]{1,0:T(2,128)}, f32[2,256]{1,0:T(2,128)S(1)}, u32[]{:S(2)}, u32[]{:S(2)}) collective-permute-start(f32[2,256]{1,0:T(2,128)} %locate.1.rest_0_), channel_id=1, source_target_pairs={{2,0},{3,1},{0,2},{1,3},{6,4},{7,5},{4,6},{5,7},{10,8},{11,9},{8,1... | collective-permute-start | bytes 6152 | tf_op jit(solution)/shard_map/ppermute | solution.py:391
  5.2 4.0 %collective-permute-start = (f32[2,256]{1,0:T(2,128)}, f32[2,256]{1,0:T(2,128)S(1)}, u32[]{:S(2)}, u32[]{:S(2)}) collective-permute-start(f32[2,256]{1,0:T(2,128)} %locate.1.rest_0_), channel_id=1, source_target_pairs={{1,0},{0,1},{3,2},{2,3},{5,4},{4,5},{7,6},{6,7},{9,8},{8,9},{11,10... | collective-permute-start | bytes 6152 | tf_op jit(solution)/shard_map/ppermute | solution.py:391
  5.4 3.8 %copy-start = (f32[2,256]{1,0:T(2,128)S(1)}, f32[2,256]{1,0:T(2,128)}, u32[]{:S(2)}) copy-start(f32[2,256]{1,0:T(2,128)} %locate.1.rest_0_) | copy-start | bytes 6148
  5.4 3.8 %copy-start.1 = (f32[32,4096]{1,0:T(8,128)S(1)}, f32[32,4096]{1,0:T(8,128)}, u32[]{:S(2)}) copy-start(f32[32,4096]{1,0:T(8,128)} %weight_ref.1) | copy-start | bytes 1572868
  5.4 3.9 %copy-start.4 = (f32[32]{0:T(128)S(1)}, f32[32]{0:T(128)}, u32[]{:S(2)}) copy-start(f32[32]{0:T(128)} %length_ref.3) | copy-start | bytes 388
  5.4 3.9 %copy-start.5 = (f32[32]{0:T(128)S(1)}, f32[32]{0:T(128)}, u32[]{:S(2)}) copy-start(f32[32]{0:T(128)} %var_ref.5) | copy-start | bytes 388
  9.2 27.2 %copy-start.6 = (s32[256]{0:T(256)S(1)}, s32[256]{0:T(256)}, u32[]{:S(2)}) copy-start(s32[256]{0:T(256)} %param.9) | copy-start | bytes 3076
  30.2 14.1 %all-to-all-start = ((f32[16,8,256]{2,1,0:T(8,128)}), f32[16,8,256]{2,1,0:T(8,128)S(1)}, u32[]{:S(2)}, u32[]{:S(2)}) async-start(f32[16,8,256]{2,1,0:T(8,128)} %bitcast.8), calls=%async_computation | async-start | bytes 262144 | tf_op jit(solution)/shard_map/all_to_all | solution.py:417
  36.6 7.8 %copy-start.2 = (bf16[64,4096]{1,0:T(8,128)(2,1)S(1)}, bf16[64,4096]{1,0:T(8,128)(2,1)}, u32[]{:S(2)}) copy-start(bf16[64,4096]{1,0:T(8,128)(2,1)} %mixing_ref.1) | copy-start | bytes 1572868
  36.6 7.8 %copy-start.3 = (f32[4096]{0:T(1024)S(1)}, f32[4096]{0:T(1024)}, u32[]{:S(2)}) copy-start(f32[4096]{0:T(1024)} %param.17) | copy-start | bytes 49156
  48.6 3.7 %collective-permute-start.3 = (f32[32,4096]{1,0:T(8,128)S(1)}, f32[32,4096]{1,0:T(8,128)S(1)}, u32[]{:S(2)}, u32[]{:S(2)}) collective-permute-start(f32[32,4096]{1,0:T(8,128)S(1)} %get-tuple-element.30), channel_id=1, source_target_pairs={{1,0},{0,1},{3,2},{2,3},{5,4},{4,5},{7,6},{6,7},{9,8},{8,9},{11,10... | collective-permute-start | bytes 1572872 | tf_op jit(solution)/shard_map/ppermute | solution.py:391
  48.6 11.4 %all-to-all-start.1 = ((f32[16,8,256]{2,1,0:T(8,128)}), f32[16,8,256]{2,1,0:T(8,128)S(1)}, u32[]{:S(2)}, u32[]{:S(2)}) async-start(f32[16,8,256]{2,1,0:T(8,128)} %bitcast.12), calls=%async_computation.1 | async-start | bytes 262144 | tf_op jit(solution)/shard_map/all_to_all | solution.py:426
  52.4 18.1 %collective-permute-start.4 = (f32[32,4096]{1,0:T(8,128)S(1)}, f32[32,4096]{1,0:T(8,128)S(1)}, u32[]{:S(2)}, u32[]{:S(2)}) collective-permute-start(f32[32,4096]{1,0:T(8,128)S(1)} %add.20), channel_id=1, source_target_pairs={{2,0},{0,2},{3,1},{1,3},{6,4},{4,6},{7,5},{5,7},{10,8},{8,10},{11,... | collective-permute-start | bytes 1572872 | tf_op jit(solution)/shard_map/ppermute | solution.py:391
  70.5 15.1 %collective-permute-start.7 = (f32[4,4096]{1,0:T(4,128)S(1)}, f32[4,4096]{1,0:T(4,128)S(1)}, u32[]{:S(2)}, u32[]{:S(2)}) collective-permute-start(f32[4,4096]{1,0:T(4,128)S(1)} %backward.2.refs_0_), channel_id=1, source_target_pairs={{12,0},{8,4},{4,8},{0,12},{13,1},{9,5},{5,9},{1,13},{14,2},{10,6},... | collective-permute-start | bytes 196616 | tf_op jit(solution)/shard_map/ppermute | solution.py:391
  71.2 14.4 %collective-permute-start.6 = (f32[4,4096]{1,0:T(4,128)S(1)}, f32[4,4096]{1,0:T(4,128)S(1)}, u32[]{:S(2)}, u32[]{:S(2)}) collective-permute-start(f32[4,4096]{1,0:T(4,128)S(1)} %backward.2.refs_0_), channel_id=1, source_target_pairs={{8,0},{12,4},{0,8},{4,12},{9,1},{13,5},{1,9},{5,13},{10,2},{14,6},... | collective-permute-start | bytes 196616 | tf_op jit(solution)/shard_map/ppermute | solution.py:391
  71.4 14.2 %collective-permute-start.5 = (f32[4,4096]{1,0:T(4,128)S(1)}, f32[4,4096]{1,0:T(4,128)S(1)}, u32[]{:S(2)}, u32[]{:S(2)}) collective-permute-start(f32[4,4096]{1,0:T(4,128)S(1)} %backward.2.refs_0_), channel_id=1, source_target_pairs={{4,0},{0,4},{12,8},{8,12},{5,1},{1,5},{13,9},{9,13},{6,2},{2,6},{1... | collective-permute-start | bytes 196616 | tf_op jit(solution)/shard_map/ppermute | solution.py:391
  75.0 15.2 %collective-permute-start.11 = (f32[32,4096]{1,0:T(8,128)S(1)}, f32[32,4096]{1,0:T(8,128)S(1)}, u32[]{:S(2)}, u32[]{:S(2)}) collective-permute-start(f32[32,4096]{1,0:T(8,128)S(1)} %add.21.refs_0_), channel_id=1, source_target_pairs={{1,0},{0,1},{3,2},{2,3},{5,4},{4,5},{7,6},{6,7},{9,8},{8,9},{11,10... | collective-permute-start | bytes 1572872 | tf_op jit(solution)/shard_map/ppermute | solution.py:391
  85.7 6.9 %collective-permute-start.10 = (f32[4,4096]{1,0:T(4,128)S(1)}, f32[4,4096]{1,0:T(4,128)S(1)}, u32[]{:S(2)}, u32[]{:S(2)}) collective-permute-start(f32[4,4096]{1,0:T(4,128)S(1)} %backward.3.refs_1_), channel_id=1, source_target_pairs={{12,0},{8,4},{4,8},{0,12},{13,1},{9,5},{5,9},{1,13},{14,2},{10,6},... | collective-permute-start | bytes 196616 | tf_op jit(solution)/shard_map/ppermute | solution.py:391
  86.4 7.9 %collective-permute-start.9 = (f32[4,4096]{1,0:T(4,128)S(1)}, f32[4,4096]{1,0:T(4,128)S(1)}, u32[]{:S(2)}, u32[]{:S(2)}) collective-permute-start(f32[4,4096]{1,0:T(4,128)S(1)} %backward.3.refs_1_), channel_id=1, source_target_pairs={{8,0},{12,4},{0,8},{4,12},{9,1},{13,5},{1,9},{5,13},{10,2},{14,6},... | collective-permute-start | bytes 196616 | tf_op jit(solution)/shard_map/ppermute | solution.py:391
  87.2 7.1 %collective-permute-start.8 = (f32[4,4096]{1,0:T(4,128)S(1)}, f32[4,4096]{1,0:T(4,128)S(1)}, u32[]{:S(2)}, u32[]{:S(2)}) collective-permute-start(f32[4,4096]{1,0:T(4,128)S(1)} %backward.3.refs_1_), channel_id=1, source_target_pairs={{4,0},{0,4},{12,8},{8,12},{5,1},{1,5},{13,9},{9,13},{6,2},{2,6},{1... | collective-permute-start | bytes 196616 | tf_op jit(solution)/shard_map/ppermute | solution.py:391

commit v8 on v7

--- a/solution.py
+++ b/solution.py
@@ -104,21 +104,15 @@
 
 
 def build_kernel(first_ref, length_ref, points_ref, rhs_ref, *, aligned):
-    local = 2 * pl.program_id(0)
-    scale = scale_of(length_ref, first_ref[0] + local)
-    row = local if aligned else first_ref[0] + local
-    width = points_ref.shape[2]
-
-    def step(i, _):
-        s = pl.ds(pl.multiple_of(i * width, width), width)
-        low = row_of((8, width)) < 4
+    low = row_of((8, points_ref.shape[2])) < 4
+    for pair in range(rhs_ref.shape[0]):
+        local = 2 * pair
+        scale = scale_of(length_ref, first_ref[0] + local)
+        row = local if aligned else first_ref[0] + local
         u, w = (
-            jnp.where(low, points_ref[d, pl.ds(row, 1), s], points_ref[d, pl.ds(row + 1, 1), s]) for d in (0, 1)
+            jnp.where(low, points_ref[d, pl.ds(row, 1), :], points_ref[d, pl.ds(row + 1, 1), :]) for d in (0, 1)
         )
-        rhs_ref[0, :, s] = point_rows(u, w, scale)
-        return 0
-
-    lax.fori_loop(0, points_ref.shape[2] // width, step, 0)
+        rhs_ref[pair] = point_rows(u, w, scale)
 
 
 def build(first, lengths, points, own_q):
@@ -130,9 +124,9 @@
         out_shape=pltpu.HBM((own_q // 2, 32, count), jnp.bfloat16),
         grid_spec=pltpu.PrefetchScalarGridSpec(
             num_scalar_prefetch=2,
-            grid=(own_q // 2,),
+            grid=(1,),
             in_specs=[pl.BlockSpec(block, lambda i, first, _: (0, first[0] // own_q if aligned else 0, 0))],
-            out_specs=pl.BlockSpec((1, 32, count), lambda i, *_: (i, 0, 0)),
+            out_specs=pl.BlockSpec((own_q // 2, 32, count), lambda i, *_: (0, 0, 0)),
         ),
         compiler_params=pltpu.CompilerParams(vmem_limit_bytes=16 << 20),
         cost_estimate=pl.CostEstimate(flops=4_000_000_000, bytes_accessed=4_000_000, transcendentals=0),

time: 96.1 us -> 95.8 us (level)
  transfers between devices with their start and end apart: 14 -> 14, of which waited for: 4 -> 4; matrix products, arithmetic and copies ran while one was open for 1% -> 1% of each run, Pallas kernels for 32% -> 31%
where the time goes in v8:
time: 95.8 us; the launch traced here: 95.4 us
  Pallas kernels  58.1 us (61%)
  starting transfers between devices  23.6 us (25%)
  waiting for transfers between devices  12.3 us (13%)
    pallas_call x2, Pallas kernels, backward(): pl.pallas_call(functools.partial(backward_kernel, NB=math.gcd(cells, 256)...  21 us
    pallas_call x1, Pallas kernels, forward(): pl.pallas_call(functools.partial(forward_kernel, blocks=blocks, NB=math.g...  21 us
    ppermute x12, starting transfers between devices, shifted(): lax.ppermute(x, axes, [(partner(i, step, size), i) for i in range(size)])  13.7 us
    all_to_all x1, starting transfers between devices, on_device(): lax.all_to_all(partial.reshape(genes * blocks, own_q, part), every, 0, 0,...  6.18 us
    all_to_all x1, waiting for transfers between devices, on_device(): lax.all_to_all(send.reshape(genes * blocks, own_q, part), every, 0, 0, ti...  5.94 us
    pallas_call x1, Pallas kernels, middle(): pl.pallas_call(functools.partial(middle_kernel, scale=scale, cuts=cuts, s...  4.22 us
    pallas_call x1, Pallas kernels, observe(): pl.pallas_call(observe_kernel, out_shape=pltpu.HBM((count, cells, width),...  3.92 us
    all_to_all x1, waiting for transfers between devices, on_device(): lax.all_to_all(partial.reshape(genes * blocks, own_q, part), every, 0, 0,...  3.84 us
  transfers between devices with their start and end apart: 14, of which 4 were waited for; matrix products, arithmetic and copies ran while one was open for 1% of the time, Pallas kernels for 31%

profile of v8, /device:TPU:0, one launch (start us, length us, event | category | flops | bytes accessed | tf_op | source)
XLA Modules:
  0.0 95.4 jit_solution(8917294761684230285)
XLA Ops:
  0.6 1.6 %locate.1.rest_0_ = f32[2,256]{1,0:T(2,128)} custom-call(s32[1,256]{1,0:T(1,128)} %bitcast.26, f32[2,512]{1,0:T(2,128)} %table_ref.1), custom_call_target="tpu_custom_call" | custom-call | tf_op jit(solution)/shard_map/locate/pallas_call | solution.py:94
  2.3 2.4 %collective-permute-start.2 = (f32[2,256]{1,0:T(2,128)}, f32[2,256]{1,0:T(2,128)S(1)}, u32[]{:S(2)}, u32[]{:S(2)}) collective-permute-start(f32[2,256]{1,0:T(2,128)} %locate.1.rest_0_), channel_id=1, source_target_pairs={{3,0},{2,1},{1,2},{0,3},{7,4},{6,5},{5,6},{4,7},{11,8},{10,9},{9,1... | collective-permute-start | bytes 6152 | tf_op jit(solution)/shard_map/ppermute | solution.py:385
  4.6 0.6 collective-permute-start.1
  5.2 0.1 collective-permute-start
  5.3 0.1 pad_add_fusion.1.rows_ref.order_ref
  5.4 3.4 %build.1.rhs_ref = bf16[4,32,4096]{2,1,0:T(8,128)(2,1)} custom-call(s32[1]{0:T(128)} %bitcast.first_ref, f32[32]{0:T(128)} %length_ref.3, f32[2,32,4096]{2,1,0:T(8,128)} %points_ref.1), custom_call_target="tpu_custom_call" | custom-call | flops 4000000000 | bytes 4000000 | tf_op jit(solution)/shard_map/build/pallas_call | solution.py:122
  8.8 0.1 pad_add_fusion.order_ref
  8.9 21.0 %forward.1 = (f32[4,4,8,256]{3,2,1,0:T(8,128)}, bf16[4,2,1024,80]{3,2,1,0:T(8,128)(2,1)}) custom-call(s32[1]{0:T(128)} %bitcast.first_ref, s32[4]{0:T(128)S(1)} %pad_add_fusion.order_ref, f32[32]{0:T(128)S(1)} %copy-done.4, f32[32]{0:T(128)S(1)} %copy-done.5, f32[32,4096]{1,0:T(8,128)S(1)} %copy-done.1, bf16[4,32,4096]{2,1,0:T(8,128)(2,1)} %build.1.rhs_ref, ...), custom_call_target="tpu_custom_call" | custom-call | flops 24999999488 | bytes 4000000 | tf_op jit(solution)/shard_map/forward/pallas_call | solution.py:178
  29.9 6.2 %all-to-all-start = ((f32[16,8,256]{2,1,0:T(8,128)}), f32[16,8,256]{2,1,0:T(8,128)S(1)}, u32[]{:S(2)}, u32[]{:S(2)}) async-start(f32[16,8,256]{2,1,0:T(8,128)} %bitcast.8), calls=%async_computation | async-start | bytes 262144 | tf_op jit(solution)/shard_map/all_to_all | solution.py:411
  36.1 0.1 copy.11.index_ref
  36.3 3.9 %observe.1.observed_ref = bf16[4,256,1024]{2,1,0:T(8,128)(2,1)} custom-call(s32[256,1]{1,0:T(8,128)S(1)} %copy.11.index_ref, bf16[512,4096]{1,0:T(8,128)(2,1)} %expr_hbm.1), custom_call_target="tpu_custom_call" | custom-call | flops 3000000000 | bytes 6000000 | tf_op jit(solution)/shard_map/observe/pallas_call | solution.py:303
  40.2 3.8 %all-to-all-done = f32[16,8,256]{2,1,0:T(8,128)S(1)} async-done(((f32[16,8,256]{2,1,0:T(8,128)}), f32[16,8,256]{2,1,0:T(8,128)S(1)}, u32[]{:S(2)}, u32[]{:S(2)}) %all-to-all-start) | async-done | bytes 131104 | tf_op jit(solution)/shard_map/all_to_all | solution.py:411
  44.0 4.2 %middle.1 = (f32[32,4096]{1,0:T(8,128)S(1)}, f32[32,4096]{1,0:T(8,128)S(1)}, f32[4,4,8,256]{3,2,1,0:T(8,128)}) custom-call(s32[2]{0:T(128)S(1)} %pad_add_fusion.1.rows_ref.order_ref, f32[4,4,8,256]{3,2,1,0:T(8,128)S(1)} %bitcast.22, bf16[64,4096]{1,0:T(8,128)(2,1)S(1)} %copy-done.2, f32[1,4096]{1,0:T(1,128)S(1)} %bitcast.23, ...), custom_call_target="tpu_custom_call" | custom-call | flops 3000000000 | bytes 4000000 | tf_op jit(solution)/shard_map/middle/pallas_call | solution.py:362
  48.3 3.7 %all-to-all-start.1 = ((f32[16,8,256]{2,1,0:T(8,128)}), f32[16,8,256]{2,1,0:T(8,128)S(1)}, u32[]{:S(2)}, u32[]{:S(2)}) async-start(f32[16,8,256]{2,1,0:T(8,128)} %bitcast.12), calls=%async_computation.1 | async-start | bytes 262144 | tf_op jit(solution)/shard_map/all_to_all | solution.py:420
  52.0 0.1 add.20
  52.1 1.7 %collective-permute-start.4 = (f32[32,4096]{1,0:T(8,128)S(1)}, f32[32,4096]{1,0:T(8,128)S(1)}, u32[]{:S(2)}, u32[]{:S(2)}) collective-permute-start(f32[32,4096]{1,0:T(8,128)S(1)} %add.20), channel_id=1, source_target_pairs={{2,0},{0,2},{3,1},{1,3},{6,4},{4,6},{7,5},{5,7},{10,8},{8,10},{11,... | collective-permute-start | bytes 1572872 | tf_op jit(solution)/shard_map/ppermute | solution.py:385
  53.7 5.9 %all-to-all-done.1 = f32[16,8,256]{2,1,0:T(8,128)S(1)} async-done(((f32[16,8,256]{2,1,0:T(8,128)}), f32[16,8,256]{2,1,0:T(8,128)S(1)}, u32[]{:S(2)}, u32[]{:S(2)}) %all-to-all-start.1) | async-done | bytes 131104 | tf_op jit(solution)/shard_map/all_to_all | solution.py:420
  59.7 10.5 %backward.2.refs_0_ = f32[4,4096]{1,0:T(4,128)S(1)} custom-call(s32[1]{0:T(128)} %bitcast.first_ref, s32[4]{0:T(128)S(1)} %pad_add_fusion.order_ref, f32[32]{0:T(128)S(1)} %copy-done.5, f32[4,4,8,256]{3,2,1,0:T(8,128)S(1)} %bitcast.20, bf16[4,32,4096]{2,1,0:T(8,128)(2,1)} %build.1.rhs_ref, bf16[4,2,1024,80]{3,2,1,0:T(8,128)(2,1)} %get-tuple-element.28.lhs_ref), custom_call_target="tpu_custom_call" | custom-call | flops 24999999488 | bytes 4000000 | tf_op jit(solution)/shard_map/backward/pallas_call | solution.py:234
  70.2 0.7 collective-permute-start.7
  70.9 0.2 collective-permute-start.6
  71.1 3.5 %collective-permute-start.5 = (f32[4,4096]{1,0:T(4,128)S(1)}, f32[4,4096]{1,0:T(4,128)S(1)}, u32[]{:S(2)}, u32[]{:S(2)}) collective-permute-start(f32[4,4096]{1,0:T(4,128)S(1)} %backward.2.refs_0_), channel_id=1, source_target_pairs={{4,0},{0,4},{12,8},{8,12},{5,1},{1,5},{13,9},{9,13},{6,2},{2,6},{1... | collective-permute-start | bytes 196616 | tf_op jit(solution)/shard_map/ppermute | solution.py:385
  74.7 0.1 add.21.refs_0_
  74.7 0.1 collective-permute-start.11
  74.8 10.5 %backward.3.refs_1_ = f32[4,4096]{1,0:T(4,128)S(1)} custom-call(s32[1]{0:T(128)} %bitcast.first_ref, s32[4]{0:T(128)S(1)} %pad_add_fusion.order_ref, f32[32]{0:T(128)S(1)} %copy-done.5, f32[4,4,8,256]{3,2,1,0:T(8,128)S(1)} %bitcast.21, bf16[4,32,4096]{2,1,0:T(8,128)(2,1)} %build.1.rhs_ref, bf16[4,2,1024,80]{3,2,1,0:T(8,128)(2,1)} %get-tuple-element.28.lhs_ref), custom_call_target="tpu_custom_call" | custom-call | flops 24999999488 | bytes 4000000 | tf_op jit(solution)/shard_map/backward/pallas_call | solution.py:234
  85.3 0.7 collective-permute-start.10
  86.1 0.8 collective-permute-start.9
  86.9 2.9 %collective-permute-start.8 = (f32[4,4096]{1,0:T(4,128)S(1)}, f32[4,4096]{1,0:T(4,128)S(1)}, u32[]{:S(2)}, u32[]{:S(2)}) collective-permute-start(f32[4,4096]{1,0:T(4,128)S(1)} %backward.3.refs_1_), channel_id=1, source_target_pairs={{4,0},{0,4},{12,8},{8,12},{5,1},{1,5},{13,9},{9,13},{6,2},{2,6},{1... | collective-permute-start | bytes 196616 | tf_op jit(solution)/shard_map/ppermute | solution.py:385
  89.8 0.1 pad_add_fusion.2.order_ref
  89.9 1.6 %gather.2 = f32[2,32,4096]{2,1,0:T(8,128)} custom-call(s32[2]{0:T(128)S(1)} %pad_add_fusion.1.rows_ref.order_ref, f32[32,4096]{1,0:T(8,128)S(1)} %add.21.refs_0_, f32[32,4096]{1,0:T(8,128)S(1)} %collective-permute-done.11.refs_1_), custom_call_target="tpu_custom_call" | custom-call | bytes 2000000 | tf_op jit(solution)/shard_map/gather/pallas_call | solution.py:264
  91.5 0.7 collective-permute-done.10.refs_7_
  92.2 1.8 %collective-permute-done.9.refs_5_ = f32[4,4096]{1,0:T(4,128)S(1)} collective-permute-done((f32[4,4096]{1,0:T(4,128)S(1)}, f32[4,4096]{1,0:T(4,128)S(1)}, u32[]{:S(2)}, u32[]{:S(2)}) %collective-permute-start.9) | collective-permute-done | bytes 65568 | tf_op jit(solution)/shard_map/ppermute | solution.py:385
  94.0 1.4 %gather.3 = f32[4,8,4096]{2,1,0:T(8,128)} custom-call(s32[4]{0:T(128)S(1)} %pad_add_fusion.2.order_ref, f32[4,4096]{1,0:T(4,128)S(1)} %backward.2.refs_0_, f32[4,4096]{1,0:T(4,128)S(1)} %backward.3.refs_1_, f32[4,4096]{1,0:T(4,128)S(1)} %collective-permute-done.5.refs_2_, f32[4,4096]{1,0:T(4,128)S(1)} %collective-permute-done.8.refs_3_, ...), custom_call_target="tpu_custom_call" | custom-call | bytes 2000000 | tf_op jit(solution)/shard_map/gather/pallas_call | solution.py:264
  (25 shorter events, 0.1 us)
Async XLA Ops:
  2.3 6.6 %collective-permute-start.2 = (f32[2,256]{1,0:T(2,128)}, f32[2,256]{1,0:T(2,128)S(1)}, u32[]{:S(2)}, u32[]{:S(2)}) collective-permute-start(f32[2,256]{1,0:T(2,128)} %locate.1.rest_0_), channel_id=1, source_target_pairs={{3,0},{2,1},{1,2},{0,3},{7,4},{6,5},{5,6},{4,7},{11,8},{10,9},{9,1... | collective-permute-start | bytes 6152 | tf_op jit(solution)/shard_map/ppermute | solution.py:385
  4.6 4.2 %collective-permute-start.1 = (f32[2,256]{1,0:T(2,128)}, f32[2,256]{1,0:T(2,128)S(1)}, u32[]{:S(2)}, u32[]{:S(2)}) collective-permute-start(f32[2,256]{1,0:T(2,128)} %locate.1.rest_0_), channel_id=1, source_target_pairs={{2,0},{3,1},{0,2},{1,3},{6,4},{7,5},{4,6},{5,7},{10,8},{11,9},{8,1... | collective-permute-start | bytes 6152 | tf_op jit(solution)/shard_map/ppermute | solution.py:385
  5.2 3.6 %collective-permute-start = (f32[2,256]{1,0:T(2,128)}, f32[2,256]{1,0:T(2,128)S(1)}, u32[]{:S(2)}, u32[]{:S(2)}) collective-permute-start(f32[2,256]{1,0:T(2,128)} %locate.1.rest_0_), channel_id=1, source_target_pairs={{1,0},{0,1},{3,2},{2,3},{5,4},{4,5},{7,6},{6,7},{9,8},{8,9},{11,10... | collective-permute-start | bytes 6152 | tf_op jit(solution)/shard_map/ppermute | solution.py:385
  5.4 3.5 %copy-start = (f32[2,256]{1,0:T(2,128)S(1)}, f32[2,256]{1,0:T(2,128)}, u32[]{:S(2)}) copy-start(f32[2,256]{1,0:T(2,128)} %locate.1.rest_0_) | copy-start | bytes 6148
  5.4 3.5 %copy-start.1 = (f32[32,4096]{1,0:T(8,128)S(1)}, f32[32,4096]{1,0:T(8,128)}, u32[]{:S(2)}) copy-start(f32[32,4096]{1,0:T(8,128)} %weight_ref.1) | copy-start | bytes 1572868
  5.4 3.5 %copy-start.4 = (f32[32]{0:T(128)S(1)}, f32[32]{0:T(128)}, u32[]{:S(2)}) copy-start(f32[32]{0:T(128)} %length_ref.3) | copy-start | bytes 388
  5.4 3.5 %copy-start.5 = (f32[32]{0:T(128)S(1)}, f32[32]{0:T(128)}, u32[]{:S(2)}) copy-start(f32[32]{0:T(128)} %var_ref.5) | copy-start | bytes 388
  8.9 27.2 %copy-start.6 = (s32[256]{0:T(256)S(1)}, s32[256]{0:T(256)}, u32[]{:S(2)}) copy-start(s32[256]{0:T(256)} %param.9) | copy-start | bytes 3076
  29.9 14.1 %all-to-all-start = ((f32[16,8,256]{2,1,0:T(8,128)}), f32[16,8,256]{2,1,0:T(8,128)S(1)}, u32[]{:S(2)}, u32[]{:S(2)}) async-start(f32[16,8,256]{2,1,0:T(8,128)} %bitcast.8), calls=%async_computation | async-start | bytes 262144 | tf_op jit(solution)/shard_map/all_to_all | solution.py:411
  36.2 7.8 %copy-start.2 = (bf16[64,4096]{1,0:T(8,128)(2,1)S(1)}, bf16[64,4096]{1,0:T(8,128)(2,1)}, u32[]{:S(2)}) copy-start(bf16[64,4096]{1,0:T(8,128)(2,1)} %mixing_ref.1) | copy-start | bytes 1572868
  36.3 7.8 %copy-start.3 = (f32[4096]{0:T(1024)S(1)}, f32[4096]{0:T(1024)}, u32[]{:S(2)}) copy-start(f32[4096]{0:T(1024)} %param.17) | copy-start | bytes 49156
  48.3 3.7 %collective-permute-start.3 = (f32[32,4096]{1,0:T(8,128)S(1)}, f32[32,4096]{1,0:T(8,128)S(1)}, u32[]{:S(2)}, u32[]{:S(2)}) collective-permute-start(f32[32,4096]{1,0:T(8,128)S(1)} %get-tuple-element.30), channel_id=1, source_target_pairs={{1,0},{0,1},{3,2},{2,3},{5,4},{4,5},{7,6},{6,7},{9,8},{8,9},{11,10... | collective-permute-start | bytes 1572872 | tf_op jit(solution)/shard_map/ppermute | solution.py:385
  48.3 11.4 %all-to-all-start.1 = ((f32[16,8,256]{2,1,0:T(8,128)}), f32[16,8,256]{2,1,0:T(8,128)S(1)}, u32[]{:S(2)}, u32[]{:S(2)}) async-start(f32[16,8,256]{2,1,0:T(8,128)} %bitcast.12), calls=%async_computation.1 | async-start | bytes 262144 | tf_op jit(solution)/shard_map/all_to_all | solution.py:420
  52.1 18.1 %collective-permute-start.4 = (f32[32,4096]{1,0:T(8,128)S(1)}, f32[32,4096]{1,0:T(8,128)S(1)}, u32[]{:S(2)}, u32[]{:S(2)}) collective-permute-start(f32[32,4096]{1,0:T(8,128)S(1)} %add.20), channel_id=1, source_target_pairs={{2,0},{0,2},{3,1},{1,3},{6,4},{4,6},{7,5},{5,7},{10,8},{8,10},{11,... | collective-permute-start | bytes 1572872 | tf_op jit(solution)/shard_map/ppermute | solution.py:385
  70.2 15.1 %collective-permute-start.7 = (f32[4,4096]{1,0:T(4,128)S(1)}, f32[4,4096]{1,0:T(4,128)S(1)}, u32[]{:S(2)}, u32[]{:S(2)}) collective-permute-start(f32[4,4096]{1,0:T(4,128)S(1)} %backward.2.refs_0_), channel_id=1, source_target_pairs={{12,0},{8,4},{4,8},{0,12},{13,1},{9,5},{5,9},{1,13},{14,2},{10,6},... | collective-permute-start | bytes 196616 | tf_op jit(solution)/shard_map/ppermute | solution.py:385
  70.9 14.4 %collective-permute-start.6 = (f32[4,4096]{1,0:T(4,128)S(1)}, f32[4,4096]{1,0:T(4,128)S(1)}, u32[]{:S(2)}, u32[]{:S(2)}) collective-permute-start(f32[4,4096]{1,0:T(4,128)S(1)} %backward.2.refs_0_), channel_id=1, source_target_pairs={{8,0},{12,4},{0,8},{4,12},{9,1},{13,5},{1,9},{5,13},{10,2},{14,6},... | collective-permute-start | bytes 196616 | tf_op jit(solution)/shard_map/ppermute | solution.py:385
  71.1 14.2 %collective-permute-start.5 = (f32[4,4096]{1,0:T(4,128)S(1)}, f32[4,4096]{1,0:T(4,128)S(1)}, u32[]{:S(2)}, u32[]{:S(2)}) collective-permute-start(f32[4,4096]{1,0:T(4,128)S(1)} %backward.2.refs_0_), channel_id=1, source_target_pairs={{4,0},{0,4},{12,8},{8,12},{5,1},{1,5},{13,9},{9,13},{6,2},{2,6},{1... | collective-permute-start | bytes 196616 | tf_op jit(solution)/shard_map/ppermute | solution.py:385
  74.7 15.2 %collective-permute-start.11 = (f32[32,4096]{1,0:T(8,128)S(1)}, f32[32,4096]{1,0:T(8,128)S(1)}, u32[]{:S(2)}, u32[]{:S(2)}) collective-permute-start(f32[32,4096]{1,0:T(8,128)S(1)} %add.21.refs_0_), channel_id=1, source_target_pairs={{1,0},{0,1},{3,2},{2,3},{5,4},{4,5},{7,6},{6,7},{9,8},{8,9},{11,10... | collective-permute-start | bytes 1572872 | tf_op jit(solution)/shard_map/ppermute | solution.py:385
  85.3 6.9 %collective-permute-start.10 = (f32[4,4096]{1,0:T(4,128)S(1)}, f32[4,4096]{1,0:T(4,128)S(1)}, u32[]{:S(2)}, u32[]{:S(2)}) collective-permute-start(f32[4,4096]{1,0:T(4,128)S(1)} %backward.3.refs_1_), channel_id=1, source_target_pairs={{12,0},{8,4},{4,8},{0,12},{13,1},{9,5},{5,9},{1,13},{14,2},{10,6},... | collective-permute-start | bytes 196616 | tf_op jit(solution)/shard_map/ppermute | solution.py:385
  86.1 7.9 %collective-permute-start.9 = (f32[4,4096]{1,0:T(4,128)S(1)}, f32[4,4096]{1,0:T(4,128)S(1)}, u32[]{:S(2)}, u32[]{:S(2)}) collective-permute-start(f32[4,4096]{1,0:T(4,128)S(1)} %backward.3.refs_1_), channel_id=1, source_target_pairs={{8,0},{12,4},{0,8},{4,12},{9,1},{13,5},{1,9},{5,13},{10,2},{14,6},... | collective-permute-start | bytes 196616 | tf_op jit(solution)/shard_map/ppermute | solution.py:385
  86.9 7.1 %collective-permute-start.8 = (f32[4,4096]{1,0:T(4,128)S(1)}, f32[4,4096]{1,0:T(4,128)S(1)}, u32[]{:S(2)}, u32[]{:S(2)}) collective-permute-start(f32[4,4096]{1,0:T(4,128)S(1)} %backward.3.refs_1_), channel_id=1, source_target_pairs={{4,0},{0,4},{12,8},{8,12},{5,1},{1,5},{13,9},{9,13},{6,2},{2,6},{1... | collective-permute-start | bytes 196616 | tf_op jit(solution)/shard_map/ppermute | solution.py:385
